TPU v7x, 256 devices: a whole 4x4x8 slice. The times are simulated.
256 devices in a mesh: dp: 32 (over y, x, core), mp: 8 (over z).
Axes of the slice: x: 4, y: 4, z: 8, core: 2. Of those that a mesh axis runs over, the one named last changes fastest.
Arguments:
- query_heads: bfloat16 [32, 1024, 3072], P('dp', None, 'mp'), may hold values from -9 to 9
- key_heads: bfloat16 [32, 1024, 3072], P('dp', None, 'mp'), may hold values from -4.5 to 4.5
- value_heads: bfloat16 [32, 1024, 3072], P('dp', None, 'mp'), may hold values from -4.5 to 4.5
- out_proj: bfloat16 [3072, 6144], P('mp'), may hold values from -0.109375 to 0.109375
- norm_gain: bfloat16 [6144], replicated, may hold values from 0.5 to 1.5
- keep_order: int32 [32, 1024], P('dp'), may hold values from 0 to 1023, each once within a row
- keep_count: int32 [32], replicated, may hold values from 1 to 512, 8192 in all
- cotangent: bfloat16 [32, 1024, 6144], P('dp', None, 'mp'), may hold values from -0.59765625 to 0.59765625
Outputs:
- normed: bfloat16 [32, 1024, 6144], P('dp', None, 'mp')
- grad_query: bfloat16 [32, 1024, 3072], P('dp', None, 'mp')
- grad_key: bfloat16 [32, 1024, 3072], P('dp', None, 'mp')
- grad_value: bfloat16 [32, 1024, 3072], P('dp', None, 'mp')
- grad_out_proj: float32 [3072, 6144], P('mp', 'dp')
Inputs may be any that keep to these rules, and one draw needn't show every extreme that they name: `keep_order`: each row holds every token position once. `keep_count`: the counts sum to 8192; the largest is 512.
All inputs are finite; a program needn't handle non-finite values.
Results may differ from a plain program's by a relative error of at most 0.02.
Values may be sent and summed in bfloat16 or wider, within the bound.
No kernel may reach another device: no remote copies, remote signals or barrier semaphores. Data moves between devices by JAX's collectives and lax.ppermute only.
A program may use at most 128 MiB of HBM per device.

v0:
```python
import functools

import jax
import jax.numpy as jnp
from jax import lax
from jax.experimental import pallas as pl
from jax.experimental.pallas import tpu as pltpu
from jax.sharding import PartitionSpec as P

HEAD_DIM = 128
P_SIZE = 1024
KEEP_MAX = 512
VMEM_LIMIT = 56 * 1024 * 1024
BF = jnp.bfloat16
F32 = jnp.float32
STEPS = (0, -1, 1, 2)


def params():
    return pltpu.CompilerParams(vmem_limit_bytes=VMEM_LIMIT)


def call(kernel, grid, prefetched, in_specs, out_specs, out_shape, scratch, *operands):
    return pl.pallas_call(
        kernel,
        grid_spec=pltpu.PrefetchScalarGridSpec(
            num_scalar_prefetch=len(prefetched),
            grid=grid,
            in_specs=in_specs,
            out_specs=out_specs,
            scratch_shapes=scratch,
        ),
        out_shape=out_shape,
        compiler_params=params(),
    )(*prefetched, *operands)


def to_column(row):
    wide = jnp.broadcast_to(row, (128, row.shape[1]))
    return jnp.transpose(wide)[:, :1]


def rows_by_token(order_ref, live):
    token = to_column(order_ref[:, :KEEP_MAX].astype(F32)).astype(jnp.int32)
    row_at = lax.broadcasted_iota(jnp.int32, (KEEP_MAX, P_SIZE), 0)
    token_at = lax.broadcasted_iota(jnp.int32, (KEEP_MAX, P_SIZE), 1)
    return jnp.where((token == token_at) & (row_at < live), 1.0, 0.0).astype(BF)


def tokens_by_row(order_ref, live):
    token_at = lax.broadcasted_iota(jnp.int32, (P_SIZE, KEEP_MAX), 0)
    row_at = lax.broadcasted_iota(jnp.int32, (P_SIZE, KEEP_MAX), 1)
    hit = (order_ref[:, :KEEP_MAX] == token_at) & (row_at < live)
    return jnp.where(hit, 1.0, 0.0).astype(BF)


def dot(a, b, contract):
    return lax.dot_general(a, b, (((contract[0],), (contract[1],)), ((), ())), preferred_element_type=F32)


def attend_kernel(info, counts, order, query, key, value, mixed, query_c, key_c, value_c, weight, pick):
    live = counts[info[0]]

    @pl.when(pl.program_id(0) == 0)
    def _():
        pick[...] = rows_by_token(order, live)

    tokens = jnp.concatenate([query[0], key[0], value[0]], axis=1)
    rows = dot(pick[...], tokens, (1, 0)).astype(BF)
    q, k, v = rows[:, :128], rows[:, 128:256], rows[:, 256:]
    query_c[...], key_c[...], value_c[...] = q, k, v
    scores = dot(q, k, (1, 1)) * HEAD_DIM ** (-0.5)
    column = lax.broadcasted_iota(jnp.int32, (KEEP_MAX, KEEP_MAX), 1)
    scores = jnp.where(column < live, scores, -1000000000.0)
    exponent = jnp.exp(scores - jnp.max(scores, axis=-1, keepdims=True))
    w = exponent / jnp.sum(exponent, axis=-1, keepdims=True)
    weight[0] = w
    mixed[...] = dot(w.astype(BF), v, (1, 0)).astype(BF)


def attend(info, counts, order, query, key, value):
    heads = query.shape[2] // HEAD_DIM
    token_spec = pl.BlockSpec((1, P_SIZE, HEAD_DIM), lambda h, *_: (0, 0, h))
    row_spec = pl.BlockSpec((KEEP_MAX, HEAD_DIM), lambda h, *_: (0, h))
    row_shape = jax.ShapeDtypeStruct((KEEP_MAX, heads * HEAD_DIM), BF)
    return call(
        attend_kernel, (heads,), (info, counts),
        [pl.BlockSpec((1, P_SIZE), lambda h, *_: (0, 0)), token_spec, token_spec, token_spec],
        [row_spec] * 4 + [pl.BlockSpec((1, KEEP_MAX, KEEP_MAX), lambda h, *_: (h, 0, 0))],
        [row_shape] * 4 + [jax.ShapeDtypeStruct((heads, KEEP_MAX, KEEP_MAX), F32)],
        [pltpu.VMEM((KEEP_MAX, P_SIZE), BF)],
        order, query, key, value,
    )


def attend_back_kernel(info, counts, order, grad, query, key, value, weight, grad_q, grad_k, grad_v, place):
    live = counts[info[0]]

    @pl.when(pl.program_id(0) == 0)
    def _():
        place[...] = tokens_by_row(order, live)

    g, q, k, v = grad[...], query[...], key[...], value[...]
    w = weight[0]
    d_weight = dot(g, v, (1, 1)).astype(BF).astype(F32)
    inner = jnp.sum(d_weight * w, axis=-1, keepdims=True)
    d_scores = (w * (d_weight - inner) * HEAD_DIM ** (-0.5)).astype(BF)
    dq = dot(d_scores, k, (1, 0)).astype(BF)
    dk = dot(d_scores, q, (0, 0)).astype(BF)
    dv = dot(w.astype(BF), g, (0, 0)).astype(BF)
    out = dot(place[...], jnp.concatenate([dq, dk, dv], axis=1), (1, 0)).astype(BF)
    grad_q[0], grad_k[0], grad_v[0] = out[:, :128], out[:, 128:256], out[:, 256:]


def attend_back(info, counts, order, grad, query, key, value, weight):
    heads = query.shape[1] // HEAD_DIM
    token_spec = pl.BlockSpec((1, P_SIZE, HEAD_DIM), lambda h, *_: (0, 0, h))
    row_spec = pl.BlockSpec((KEEP_MAX, HEAD_DIM), lambda h, *_: (0, h))
    token_shape = jax.ShapeDtypeStruct((1, P_SIZE, heads * HEAD_DIM), BF)
    return call(
        attend_back_kernel, (heads,), (info, counts),
        [pl.BlockSpec((1, P_SIZE), lambda h, *_: (0, 0))] + [row_spec] * 4
        + [pl.BlockSpec((1, KEEP_MAX, KEEP_MAX), lambda h, *_: (h, 0, 0))],
        [token_spec] * 3, [token_shape] * 3,
        [pltpu.VMEM((P_SIZE, KEEP_MAX), BF)],
        order, grad, query, key, value, weight,
    )


def pick_kernel(info, counts, order, tokens, rows, pick):
    @pl.when(pl.program_id(0) == 0)
    def _():
        pick[...] = rows_by_token(order, counts[info[0]])

    rows[...] = dot(pick[...], tokens[0], (1, 0)).astype(BF)


def pick_rows(info, counts, order, tokens):
    width = tokens.shape[2]
    return call(
        pick_kernel, (width // 256,), (info, counts),
        [pl.BlockSpec((1, P_SIZE), lambda j, *_: (0, 0)), pl.BlockSpec((1, P_SIZE, 256), lambda j, *_: (0, 0, j))],
        pl.BlockSpec((KEEP_MAX, 256), lambda j, *_: (0, j)),
        jax.ShapeDtypeStruct((KEEP_MAX, width), BF),
        [pltpu.VMEM((KEEP_MAX, P_SIZE), BF)],
        order, tokens,
    )


def place_kernel(info, counts, order, rows, tokens, place):
    @pl.when(pl.program_id(0) == 0)
    def _():
        place[...] = tokens_by_row(order, counts[info[0]])

    tokens[0] = dot(place[...], rows[...], (1, 0)).astype(BF)


def place_rows(info, counts, order, rows):
    width = rows.shape[1]
    return call(
        place_kernel, (width // 256,), (info, counts),
        [pl.BlockSpec((1, P_SIZE), lambda j, *_: (0, 0)), pl.BlockSpec((KEEP_MAX, 256), lambda j, *_: (0, j))],
        pl.BlockSpec((1, P_SIZE, 256), lambda j, *_: (0, 0, j)),
        jax.ShapeDtypeStruct((1, P_SIZE, width), BF),
        [pltpu.VMEM((P_SIZE, KEEP_MAX), BF)],
        order, rows,
    )


def cut_kernel(info, left, right, out):
    half = left.shape[1]
    out[0, :, :half] = left[...]
    out[0, :, half:] = right[...]


def assemble_kernel(info, *refs):
    out = refs[-1]
    half = out.shape[2] // 2
    rows = out.shape[1]
    part = rows // 8
    for stream in range(2):
        place = info[2 + stream]
        for at, step in enumerate(STEPS):
            quarter = lax.rem(place + 4 + step, 4)
            for core in range(2):
                piece = refs[(stream * 4 + at) * 2 + core]
                side = jnp.where(core == 0, info[4], 1 - info[4])
                start = pl.multiple_of((side * 4 + quarter) * part, 16)
                out[0, pl.ds(start, part), pl.ds(stream * half, half)] = piece[0]


def gather_columns(info, out_proj, permute_tables):
    rows, full = out_proj.shape
    ranks = lax.axis_size("mp")
    width = full // ranks
    half, part = width // 2, rows // 8
    cut = call(
        cut_kernel, (ranks,), (info,),
        [
            pl.BlockSpec((part, half), lambda m, i: (i[4] * 4 + i[2], 2 * m)),
            pl.BlockSpec((part, half), lambda m, i: (i[4] * 4 + i[3], 2 * m + 1)),
        ],
        pl.BlockSpec((1, part, width), lambda m, i: (m, 0, 0)),
        jax.ShapeDtypeStruct((ranks, part, width), BF), [],
        out_proj, out_proj,
    )
    got = lax.all_to_all(cut, "mp", split_axis=0, concat_axis=0, tiled=True)
    pieces = []
    for stream in range(2):
        own = got[:, :, stream * half:(stream + 1) * half]
        for step in STEPS:
            piece = own if step == 0 else lax.ppermute(own, "dp", permute_tables[stream][step])
            pieces += [piece, lax.ppermute(piece, "dp", permute_tables[2])]
    piece_spec = pl.BlockSpec((1, part, half), lambda m, i: (m, 0, 0))
    whole = call(
        assemble_kernel, (ranks,), (info,),
        [piece_spec] * 16,
        pl.BlockSpec((1, rows, width), lambda m, i: (m, 0, 0)),
        jax.ShapeDtypeStruct((ranks, rows, width), BF), [],
        *pieces,
    )
    return whole.reshape(ranks * rows, width)


def project_kernel(info, mixed, weight, grad, gain, projected, sums):
    step = pl.program_id(0)
    part = dot(mixed[...], weight[...], (1, 0))

    @pl.when(step == 0)
    def _():
        projected[...] = part

    @pl.when(step > 0)
    def _():
        projected[...] += part

    @pl.when(step == pl.num_programs(0) - 1)
    def _():
        values = projected[...]
        scaled = grad[...].astype(F32) * gain[...].astype(F32)
        lane = lax.broadcasted_iota(jnp.int32, (KEEP_MAX, 128), 1)
        table = jnp.zeros((KEEP_MAX, 128), F32)
        for at, term in enumerate((values, values * values, scaled, scaled * values)):
            table = jnp.where(lane == at, jnp.sum(term, axis=-1, keepdims=True), table)
        sums[...] = jnp.transpose(table)[:8]


def project(info, mixed, weight, grad, gain):
    depth, width = weight.shape
    block = 768
    return call(
        project_kernel, (depth // block,), (info,),
        [
            pl.BlockSpec((KEEP_MAX, block), lambda k, i: (0, k)),
            pl.BlockSpec((block, width), lambda k, i: (k, 0)),
            pl.BlockSpec((KEEP_MAX, width), lambda k, i: (0, 0)),
            pl.BlockSpec((1, width), lambda k, i: (0, i[1])),
        ],
        [pl.BlockSpec((KEEP_MAX, width), lambda k, i: (0, 0)), pl.BlockSpec((8, KEEP_MAX), lambda k, i: (0, 0))],
        [jax.ShapeDtypeStruct((KEEP_MAX, width), F32), jax.ShapeDtypeStruct((8, KEEP_MAX), F32)],
        [], mixed, weight, grad, gain,
    )


def grad_kernel(full_width, info, counts, projected, grad, gain, weight, *refs):
    *sums, out, grad_proj, normed = refs

    @pl.when(pl.program_id(0) == 0)
    def _():
        total = sums[0][...]
        for other in sums[1:]:
            total = total + other[...]
        total = jnp.concatenate([total, jnp.zeros((120, KEEP_MAX), F32)], axis=0)
        table = jnp.transpose(total) / full_width
        row_mean, row_square, first, cross = (table[:, at:at + 1] for at in range(4))
        inv_std = lax.rsqrt(row_square - row_mean * row_mean + 1e-06)
        second = (cross - row_mean * first) * inv_std
        live = lax.broadcasted_iota(jnp.int32, (KEEP_MAX, 1), 0) < counts[info[0]]
        gain_wide = gain[...].astype(F32)
        centred = (projected[...] - row_mean) * inv_std
        scaled = grad[...].astype(F32) * gain_wide
        normed[...] = jnp.where(live, centred * gain_wide, 0.0).astype(BF)
        grad_proj[...] = jnp.where(live, inv_std * (scaled - first - centred * second), 0.0).astype(BF)

    product = dot(grad_proj[...], weight[...], (1, 1)).astype(BF)
    half = out.shape[2]
    out[0] = product[:, :half]
    out[1] = product[:, half:]


def grad_rows(info, counts, projected, grad, gain, weight, sums, full_width):
    depth, width = weight.shape
    block = 768
    whole = pl.BlockSpec((KEEP_MAX, width), lambda k, *i: (0, 0))
    rows_shape = jax.ShapeDtypeStruct((KEEP_MAX, width), BF)
    return call(
        functools.partial(grad_kernel, full_width), (depth // block,), (info, counts),
        [
            whole, whole,
            pl.BlockSpec((1, width), lambda k, i, c: (0, i[1])),
            pl.BlockSpec((block, width), lambda k, *i: (k, 0)),
        ] + [pl.BlockSpec((8, KEEP_MAX), lambda k, *i: (0, 0))] * len(sums),
        [pl.BlockSpec((2, KEEP_MAX, block // 2), lambda k, *i: (k, 0, 0)), whole, whole],
        [jax.ShapeDtypeStruct((depth * 2 // block, KEEP_MAX, block // 2), BF), rows_shape, rows_shape],
        [], projected, grad, gain, weight, *sums,
    )


def outer_kernel(info, grad_proj, mixed, out, turned):
    @pl.when(pl.program_id(0) == 0)
    def _():
        turned[...] = jnp.transpose(grad_proj[...])

    out[0] = dot(turned[...], mixed[...], (1, 0)).astype(BF)


def outer(info, grad_proj, mixed, keep):
    width = grad_proj.shape[1]
    block = mixed.shape[1] // 8

    def at(j, i):
        side = i[4] if keep else 1 - i[4]
        return 0, side * 4 + j

    return call(
        outer_kernel, (4,), (info,),
        [pl.BlockSpec((KEEP_MAX, width), lambda j, i: (0, 0)), pl.BlockSpec((KEEP_MAX, block), at)],
        pl.BlockSpec((1, width, block), lambda j, i: (j, 0, 0)),
        jax.ShapeDtypeStruct((4, width, block), BF),
        [pltpu.VMEM((width, KEEP_MAX), BF)],
        grad_proj, mixed,
    )


def dp_index(y, x, core):
    return (y % 4) * 8 + (x % 4) * 2 + core


def on_device(
    query_heads, key_heads, value_heads, out_proj, norm_gain, keep_order, keep_count, cotangent
):
    ranks = lax.axis_size("mp")
    image = lax.axis_index("dp")
    rank = lax.axis_index("mp")
    info = jnp.stack([image, rank, image // 8, (image // 2) % 4, image % 2]).astype(jnp.int32)
    chips = [(y, x, core) for y in range(4) for x in range(4) for core in range(2)]
    tables = (
        {s: [(dp_index(y, x, c), dp_index(y - s, x, c)) for y, x, c in chips] for s in STEPS[1:]},
        {s: [(dp_index(y, x, c), dp_index(y, x - s, c)) for y, x, c in chips] for s in STEPS[1:]},
        [(dp_index(y, x, c), dp_index(y, x, 1 - c)) for y, x, c in chips],
    )
    gain = norm_gain.reshape(1, -1)

    columns = gather_columns(info, out_proj, tables)
    mixed, query_c, key_c, value_c, weights = attend(
        info, keep_count, keep_order, query_heads, key_heads, value_heads
    )
    mixed_all = lax.all_gather(mixed, "mp", axis=1, tiled=True)
    grad_c = pick_rows(info, keep_count, keep_order, cotangent)
    projected, sums = project(info, mixed_all, columns, grad_c, gain)
    all_sums = [sums] + [
        lax.ppermute(sums, "mp", [(m, (m + s) % ranks) for m in range(ranks)]) for s in range(1, ranks)
    ]
    mixed_grad, grad_proj, normed_c = grad_rows(
        info, keep_count, projected, grad_c, gain, columns, all_sums, norm_gain.shape[0]
    )
    grad_mixed = lax.psum_scatter(mixed_grad, "mp", scatter_dimension=0, tiled=True)[0]

    sent = outer(info, grad_proj, mixed_all, False)
    other = lax.ppermute(sent, "dp", tables[2])
    kept = outer(info, grad_proj, mixed_all, True)
    width, depth = kept.shape[1], kept.shape[2]
    pair = (kept.astype(F32) + other.astype(F32)).astype(BF).reshape(16, width // 4, depth)
    groups = [[2 * j + c for j in range(16)] for c in range(2)]
    spread = lax.all_to_all(
        pair, "dp", split_axis=0, concat_axis=0, tiled=True, axis_index_groups=groups
    )
    total = jnp.sum(spread.astype(F32), axis=0).astype(BF)
    home = [
        (dp_index(y, x, c) * ranks + m, (4 * m + x) * ranks + 4 * c + y)
        for y, x, c in chips for m in range(ranks)
    ]
    weight_grad = lax.ppermute(total, ("dp", "mp"), home).astype(F32).T

    normed = place_rows(info, keep_count, keep_order, normed_c)
    grads = attend_back(info, keep_count, keep_order, grad_mixed, query_c, key_c, value_c, weights)
    return (normed, *grads, weight_grad)


def solution(mesh):
    in_specs = (
        P("dp", None, "mp"),
        P("dp", None, "mp"),
        P("dp", None, "mp"),
        P("mp", None),
        P(),
        P("dp", None),
        P(),
        P("dp", None, "mp"),
    )
    out_specs = (
        P("dp", None, "mp"),
        P("dp", None, "mp"),
        P("dp", None, "mp"),
        P("dp", None, "mp"),
        P("mp", "dp"),
    )
    return jax.shard_map(
        on_device, mesh=mesh, in_specs=in_specs, out_specs=out_specs, check_vma=False
    )
```

profile of v0, /device:TPU:2, one launch (start us, length us, event | category | flops | bytes accessed | tf_op | source)
XLA Modules:
  0.0 215.5 jit_solution(3570502722594117421)
XLA Ops:
  7.3 0.7 stack.23.info
  7.9 7.6 %shard_map.119 = (bf16[512,384]{1,0:T(8,128)(2,1)}, bf16[512,384]{1,0:T(8,128)(2,1)}, bf16[512,384]{1,0:T(8,128)(2,1)}, bf16[512,384]{1,0:T(8,128)(2,1)}, f32[3,512,512]{2,1,0:T(8,128)}) custom-call(s32[5]{0:T(128)} %stack.23.info, s32[32]{0:T(128)} %counts.9, s32[1,1024]{1,0:T(1,128)} %order.7, bf16[1,1024,384]{2,1,0:T(8,128)(2,1)} %query.1, ...), custom_call_target="tpu_custom_call" | custom-call | tf_op jit(solution)/shard_map/pallas_call | solution.py:24
  15.6 5.3 %shard_map.120 = bf16[8,48,768]{2,1,0:T(8,128)(2,1)} custom-call(s32[5]{0:T(128)} %stack.23.info, bf16[384,6144]{1,0:T(8,128)(2,1)} %right.1, bf16[384,6144]{1,0:T(8,128)(2,1)} %right.1), custom_call_target="tpu_custom_call" | custom-call | tf_op jit(solution)/shard_map/pallas_call | solution.py:24
  20.8 34.0 %all_to_all.10 = bf16[8,48,768]{2,1,0:T(8,128)(2,1)S(1)} all-to-all(bf16[8,48,768]{2,1,0:T(8,128)(2,1)} %shard_map.120), channel_id=1, replica_groups=mesh['dp'=32,'mp'=8] {'mp'}, dimensions={0} | all-to-all | bytes 1179648 | tf_op jit(solution)/shard_map/all_to_all | solution.py:207
  54.9 2.2 %collective-permute-start.12 = (bf16[8,48,384]{2,1,0:T(8,128)(2,1)S(1)}, bf16[8,48,384]{2,1,0:T(8,128)(2,1)S(1)}, u32[]{:S(2)}, u32[]{:S(2)}) collective-permute-start(bf16[8,48,384]{2,1,0:T(8,128)(2,1)S(1)} %get-tuple-element.31.refs_8_), channel_id=1, source_target_pairs={{0,32},{8,40},{16,48},{24,56},{32,0},{40,8},{48,16},{56,24},{64,96... | collective-permute-start | bytes 884744 | tf_op jit(solution)/shard_map/ppermute | solution.py:212
  57.1 1.4 collective-permute-start.10
  58.6 0.6 collective-permute-start.8
  59.2 3.3 %collective-permute-start.5 = (bf16[8,48,384]{2,1,0:T(8,128)(2,1)S(1)}, bf16[8,48,384]{2,1,0:T(8,128)(2,1)S(1)}, u32[]{:S(2)}, u32[]{:S(2)}) collective-permute-start(bf16[8,48,384]{2,1,0:T(8,128)(2,1)S(1)} %get-tuple-element.32.refs_0_), channel_id=1, source_target_pairs={{0,128},{8,136},{16,144},{24,152},{32,160},{40,168},{48,176},{56,1... | collective-permute-start | bytes 884744 | tf_op jit(solution)/shard_map/ppermute | solution.py:212
  62.5 4.0 %collective-permute-done.12.refs_14_ = bf16[8,48,384]{2,1,0:T(8,128)(2,1)S(1)} collective-permute-done((bf16[8,48,384]{2,1,0:T(8,128)(2,1)S(1)}, bf16[8,48,384]{2,1,0:T(8,128)(2,1)S(1)}, u32[]{:S(2)}, u32[]{:S(2)}) %collective-permute-start.12) | collective-permute-done | bytes 294944 | tf_op jit(solution)/shard_map/ppermute | solution.py:212
  66.5 3.2 %collective-permute-start.3 = (bf16[8,48,384]{2,1,0:T(8,128)(2,1)S(1)}, bf16[8,48,384]{2,1,0:T(8,128)(2,1)S(1)}, u32[]{:S(2)}, u32[]{:S(2)}) collective-permute-start(bf16[8,48,384]{2,1,0:T(8,128)(2,1)S(1)} %get-tuple-element.32.refs_0_), channel_id=1, source_target_pairs={{0,192},{8,200},{16,208},{24,216},{32,224},{40,232},{48,240},{56,2... | collective-permute-start | bytes 884744 | tf_op jit(solution)/shard_map/ppermute | solution.py:212
  69.7 1.2 collective-permute-done.10.refs_12_
  70.9 1.7 collective-permute-start.1
  72.6 0.5 collective-permute-start.13
  73.2 3.7 %collective-permute-done.3.refs_4_ = bf16[8,48,384]{2,1,0:T(8,128)(2,1)S(1)} collective-permute-done((bf16[8,48,384]{2,1,0:T(8,128)(2,1)S(1)}, bf16[8,48,384]{2,1,0:T(8,128)(2,1)S(1)}, u32[]{:S(2)}, u32[]{:S(2)}) %collective-permute-start.3) | collective-permute-done | bytes 294944 | tf_op jit(solution)/shard_map/ppermute | solution.py:212
  76.9 4.4 %collective-permute-done.1.refs_2_ = bf16[8,48,384]{2,1,0:T(8,128)(2,1)S(1)} collective-permute-done((bf16[8,48,384]{2,1,0:T(8,128)(2,1)S(1)}, bf16[8,48,384]{2,1,0:T(8,128)(2,1)S(1)}, u32[]{:S(2)}, u32[]{:S(2)}) %collective-permute-start.1) | collective-permute-done | bytes 294944 | tf_op jit(solution)/shard_map/ppermute | solution.py:212
  81.4 0.5 collective-permute-start.4
  81.9 0.3 collective-permute-start.2
  82.2 0.6 reshape.20.gain
  82.8 4.8 %shard_map.122.grad = bf16[512,768]{1,0:T(8,128)(2,1)} custom-call(s32[5]{0:T(128)} %stack.23.info, s32[32]{0:T(128)} %counts.9, s32[1,1024]{1,0:T(1,128)} %order.7, bf16[1,1024,768]{2,1,0:T(8,128)(2,1)} %tokens.1), custom_call_target="tpu_custom_call" | custom-call | tf_op jit(solution)/shard_map/pallas_call | solution.py:24
  87.8 0.5 copy-done.11
  88.3 0.1 copy-done.12
  88.5 0.1 copy-done.14
  88.6 0.7 copy-done.15
  89.3 7.4 %shard_map.121 = bf16[8,384,768]{2,1,0:T(8,128)(2,1)} custom-call(s32[5]{0:T(128)} %stack.23.info, bf16[8,48,384]{2,1,0:T(8,128)(2,1)} %copy-done.1, bf16[8,48,384]{2,1,0:T(8,128)(2,1)} %copy-done.9, bf16[8,48,384]{2,1,0:T(8,128)(2,1)} %copy-done.8, bf16[8,48,384]{2,1,0:T(8,128)(2,1)} %copy-done.15, bf16[8,48,384]{2,1,0:T(8,128)(2,1)} %copy-done.7, ...), custom_call_target="tpu_custom_call" | custom-call | tf_op jit(solution)/shard_map/pallas_call | solution.py:24
  96.8 8.5 %shard_map.123 = (f32[512,768]{1,0:T(8,128)}, f32[8,512]{1,0:T(8,128)}) custom-call(s32[5]{0:T(128)} %stack.23.info, bf16[512,3072]{1,0:T(8,128)(2,1)} %all-gather.2.cloned.1.call-done.mixed, bf16[3072,768]{1,0:T(8,128)(2,1)} %bitcast.10, bf16[512,768]{1,0:T(8,128)(2,1)} %shard_map.122.grad, bf16[1,6144]{1,0:T(2,128)(2,1)} %reshape.20.gain), custom_call_target="tpu_custom_call" | custom-call | tf_op jit(solution)/shard_map/pallas_call | solution.py:24
  105.2 1.1 collective-permute-start.19
  106.3 2.9 %collective-permute-start.18 = (f32[8,512]{1,0:T(8,128)}, f32[8,512]{1,0:T(8,128)S(1)}, u32[]{:S(2)}, u32[]{:S(2)}) collective-permute-start(f32[8,512]{1,0:T(8,128)} %get-tuple-element.20.refs_0_), channel_id=1, source_target_pairs={{0,5},{1,6},{2,7},{3,0},{4,1},{5,2},{6,3},{7,4},{8,13},{9,14},{10,... | collective-permute-start | bytes 49160 | tf_op jit(solution)/shard_map/ppermute | solution.py:362
  109.2 3.0 %collective-permute-start.17 = (f32[8,512]{1,0:T(8,128)}, f32[8,512]{1,0:T(8,128)S(1)}, u32[]{:S(2)}, u32[]{:S(2)}) collective-permute-start(f32[8,512]{1,0:T(8,128)} %get-tuple-element.20.refs_0_), channel_id=1, source_target_pairs={{0,4},{1,5},{2,6},{3,7},{4,0},{5,1},{6,2},{7,3},{8,12},{9,13},{10,... | collective-permute-start | bytes 49160 | tf_op jit(solution)/shard_map/ppermute | solution.py:362
  112.2 2.4 %collective-permute-start.16 = (f32[8,512]{1,0:T(8,128)}, f32[8,512]{1,0:T(8,128)S(1)}, u32[]{:S(2)}, u32[]{:S(2)}) collective-permute-start(f32[8,512]{1,0:T(8,128)} %get-tuple-element.20.refs_0_), channel_id=1, source_target_pairs={{0,3},{1,4},{2,5},{3,6},{4,7},{5,0},{6,1},{7,2},{8,11},{9,12},{10,... | collective-permute-start | bytes 49160 | tf_op jit(solution)/shard_map/ppermute | solution.py:362
  114.6 1.0 collective-permute-start.15
  115.6 0.2 collective-permute-start.14
  115.8 1.4 collective-permute-done.17.refs_4_
  117.3 1.9 collective-permute-done.16.refs_3_
  119.2 1.5 collective-permute-done.15.refs_2_
  120.7 0.2 collective-permute-done.14.refs_1_
  120.9 0.4 copy-done.21
  121.3 0.2 copy-done.22
  121.4 9.1 %shard_map.124 = (bf16[8,512,384]{2,1,0:T(8,128)(2,1)}, bf16[512,768]{1,0:T(8,128)(2,1)}, bf16[512,768]{1,0:T(8,128)(2,1)}) custom-call(s32[5]{0:T(128)} %stack.23.info, s32[32]{0:T(128)} %counts.9, f32[512,768]{1,0:T(8,128)} %get-tuple-element.19.projected, bf16[512,768]{1,0:T(8,128)(2,1)} %shard_map.122.grad, bf16[1,6144]{1,0:T(2,128)(2,1)} %reshape.20.gain, ...), custom_call_target="tpu_custom_call" | custom-call | tf_op jit(solution)/shard_map/pallas_call | solution.py:24
  130.6 6.0 %shard_map.128 = bf16[4,768,384]{2,1,0:T(8,128)(2,1)} custom-call(s32[5]{0:T(128)} %stack.23.info, bf16[512,768]{1,0:T(8,128)(2,1)} %get-tuple-element.30.grad_proj, bf16[512,3072]{1,0:T(8,128)(2,1)} %all-gather.2.cloned.1.call-done.mixed), custom_call_target="tpu_custom_call" | custom-call | tf_op jit(solution)/shard_map/pallas_call | solution.py:24
  136.6 6.0 %shard_map.127 = bf16[4,768,384]{2,1,0:T(8,128)(2,1)} custom-call(s32[5]{0:T(128)} %stack.23.info, bf16[512,768]{1,0:T(8,128)(2,1)} %get-tuple-element.30.grad_proj, bf16[512,3072]{1,0:T(8,128)(2,1)} %all-gather.2.cloned.1.call-done.mixed), custom_call_target="tpu_custom_call" | custom-call | tf_op jit(solution)/shard_map/pallas_call | solution.py:24
  142.7 2.2 %add_convert_fusion = bf16[4,768,384]{2,1,0:T(8,128)(2,1)S(1)} fusion(bf16[4,768,384]{2,1,0:T(8,128)(2,1)S(1)} %collective-permute-done.21, bf16[4,768,384]{2,1,0:T(8,128)(2,1)} %shard_map.127), kind=kLoop, calls=%fused_computation | loop fusion | flops 4718592 | bytes 7077888 | tf_op jit(solution)/shard_map/convert_element_type | solution.py:373
  144.9 36.4 %all_to_all.11 = bf16[16,192,384]{2,1,0:T(8,128)(2,1)S(1)} all-to-all(bf16[16,192,384]{2,1,0:T(8,128)(2,1)S(1)} %bitcast.12), channel_id=1, replica_groups={{0,16,32,48,64,80,96,112,128,144,160,176,192,208,224,240},{8,24,40,56,7..., dimensions={0} | all-to-all | bytes 4718592 | tf_op jit(solution)/shard_map/all_to_all | solution.py:375
  181.3 0.3 reduce_sum.12
  181.6 2.0 collective-permute-start.22
  183.6 4.6 %shard_map.125 = bf16[1,1024,768]{2,1,0:T(8,128)(2,1)} custom-call(s32[5]{0:T(128)} %stack.23.info, s32[32]{0:T(128)} %counts.9, s32[1,1024]{1,0:T(1,128)} %order.7, bf16[512,768]{1,0:T(8,128)(2,1)} %get-tuple-element.21.rows), custom_call_target="tpu_custom_call" | custom-call | tf_op jit(solution)/shard_map/pallas_call | solution.py:24
  188.3 11.4 %collective-permute-done.22 = bf16[192,384]{1,0:T(8,128)(2,1)S(1)} collective-permute-done((bf16[192,384]{1,0:T(8,128)(2,1)S(1)}, bf16[192,384]{1,0:T(8,128)(2,1)S(1)}, u32[]{:S(2)}, u32[]{:S(2)}) %collective-permute-start.22) | collective-permute-done | bytes 147488 | tf_op jit(solution)/shard_map/ppermute | solution.py:383
  199.7 0.7 convert_bitcast_fusion
  200.4 8.2 %shard_map.126 = (bf16[1,1024,384]{2,1,0:T(8,128)(2,1)}, bf16[1,1024,384]{2,1,0:T(8,128)(2,1)}, bf16[1,1024,384]{2,1,0:T(8,128)(2,1)}) custom-call(s32[5]{0:T(128)} %stack.23.info, s32[32]{0:T(128)} %counts.9, s32[1,1024]{1,0:T(1,128)} %order.7, bf16[512,384]{1,0:T(8,128)(2,1)} %bitcast.13, bf16[512,384]{1,0:T(8,128)(2,1)} %get-tuple-element.23.query, ...), custom_call_target="tpu_custom_call" | custom-call | tf_op jit(solution)/shard_map/pallas_call | solution.py:24
  (70 shorter events, 0.5 us)
Async XLA Ops:
  7.2 89.6 %all-gather.2.cloned.1.call-start = ((), (), s32[]{:S(2)}) async-start(), calls=%async_computation.3 | async-start | bytes 3538944 | tf_op jit(solution)/shard_map/all_gather | solution.py:358
  15.5 184.9 %reduce-scatter.2.cloned.1.call-start = ((), (), s32[]{:S(2)}) async-start(), calls=%async_computation.4 | async-start | bytes 3538944 | tf_op jit(solution)/shard_map/reduce_scatter | solution.py:367
  20.8 61.3 %copy-start.23 = (bf16[6144]{0:T(1024)(128)(2,1)S(1)}, bf16[6144]{0:T(1024)(128)(2,1)}, u32[]{:S(2)}) copy-start(bf16[6144]{0:T(1024)(128)(2,1)} %param.12) | copy-start | bytes 36868
  54.9 32.8 %copy-start = (bf16[8,48,384]{2,1,0:T(8,128)(2,1)}, bf16[8,48,384]{2,1,0:T(8,128)(2,1)S(1)}, u32[]{:S(2)}) copy-start(bf16[8,48,384]{2,1,0:T(8,128)(2,1)S(1)} %get-tuple-element.31.refs_8_) | copy-start | bytes 884740
  54.9 32.8 %copy-start.1 = (bf16[8,48,384]{2,1,0:T(8,128)(2,1)}, bf16[8,48,384]{2,1,0:T(8,128)(2,1)S(1)}, u32[]{:S(2)}) copy-start(bf16[8,48,384]{2,1,0:T(8,128)(2,1)S(1)} %get-tuple-element.32.refs_0_) | copy-start | bytes 884740
  54.9 11.6 %collective-permute-start.12 = (bf16[8,48,384]{2,1,0:T(8,128)(2,1)S(1)}, bf16[8,48,384]{2,1,0:T(8,128)(2,1)S(1)}, u32[]{:S(2)}, u32[]{:S(2)}) collective-permute-start(bf16[8,48,384]{2,1,0:T(8,128)(2,1)S(1)} %get-tuple-element.31.refs_8_), channel_id=1, source_target_pairs={{0,32},{8,40},{16,48},{24,56},{32,0},{40,8},{48,16},{56,24},{64,96... | collective-permute-start | bytes 884744 | tf_op jit(solution)/shard_map/ppermute | solution.py:212
  57.1 13.7 %collective-permute-start.10 = (bf16[8,48,384]{2,1,0:T(8,128)(2,1)S(1)}, bf16[8,48,384]{2,1,0:T(8,128)(2,1)S(1)}, u32[]{:S(2)}, u32[]{:S(2)}) collective-permute-start(bf16[8,48,384]{2,1,0:T(8,128)(2,1)S(1)} %get-tuple-element.31.refs_8_), channel_id=1, source_target_pairs={{0,48},{8,56},{16,0},{24,8},{32,16},{40,24},{48,32},{56,40},{64,11... | collective-permute-start | bytes 884744 | tf_op jit(solution)/shard_map/ppermute | solution.py:212
  58.6 14.0 %collective-permute-start.8 = (bf16[8,48,384]{2,1,0:T(8,128)(2,1)S(1)}, bf16[8,48,384]{2,1,0:T(8,128)(2,1)S(1)}, u32[]{:S(2)}, u32[]{:S(2)}) collective-permute-start(bf16[8,48,384]{2,1,0:T(8,128)(2,1)S(1)} %get-tuple-element.31.refs_8_), channel_id=1, source_target_pairs={{0,16},{8,24},{16,32},{24,40},{32,48},{40,56},{48,0},{56,8},{64,80... | collective-permute-start | bytes 884744 | tf_op jit(solution)/shard_map/ppermute | solution.py:212
  59.2 13.4 %collective-permute-start.7 = (bf16[8,48,384]{2,1,0:T(8,128)(2,1)S(1)}, bf16[8,48,384]{2,1,0:T(8,128)(2,1)S(1)}, u32[]{:S(2)}, u32[]{:S(2)}) collective-permute-start(bf16[8,48,384]{2,1,0:T(8,128)(2,1)S(1)} %get-tuple-element.31.refs_8_), channel_id=1, source_target_pairs={{0,8},{8,0},{16,24},{24,16},{32,40},{40,32},{48,56},{56,48},{64,72... | collective-permute-start | bytes 884744 | tf_op jit(solution)/shard_map/ppermute | solution.py:213
  59.2 13.9 %collective-permute-start.5 = (bf16[8,48,384]{2,1,0:T(8,128)(2,1)S(1)}, bf16[8,48,384]{2,1,0:T(8,128)(2,1)S(1)}, u32[]{:S(2)}, u32[]{:S(2)}) collective-permute-start(bf16[8,48,384]{2,1,0:T(8,128)(2,1)S(1)} %get-tuple-element.32.refs_0_), channel_id=1, source_target_pairs={{0,128},{8,136},{16,144},{24,152},{32,160},{40,168},{48,176},{56,1... | collective-permute-start | bytes 884744 | tf_op jit(solution)/shard_map/ppermute | solution.py:212
  66.5 21.2 %copy-start.2 = (bf16[8,48,384]{2,1,0:T(8,128)(2,1)}, bf16[8,48,384]{2,1,0:T(8,128)(2,1)S(1)}, u32[]{:S(2)}) copy-start(bf16[8,48,384]{2,1,0:T(8,128)(2,1)S(1)} %collective-permute-done.12.refs_14_) | copy-start | bytes 884740
  66.5 10.5 %collective-permute-start.3 = (bf16[8,48,384]{2,1,0:T(8,128)(2,1)S(1)}, bf16[8,48,384]{2,1,0:T(8,128)(2,1)S(1)}, u32[]{:S(2)}, u32[]{:S(2)}) collective-permute-start(bf16[8,48,384]{2,1,0:T(8,128)(2,1)S(1)} %get-tuple-element.32.refs_0_), channel_id=1, source_target_pairs={{0,192},{8,200},{16,208},{24,216},{32,224},{40,232},{48,240},{56,2... | collective-permute-start | bytes 884744 | tf_op jit(solution)/shard_map/ppermute | solution.py:212
  70.9 16.8 %copy-start.3 = (bf16[8,48,384]{2,1,0:T(8,128)(2,1)}, bf16[8,48,384]{2,1,0:T(8,128)(2,1)S(1)}, u32[]{:S(2)}) copy-start(bf16[8,48,384]{2,1,0:T(8,128)(2,1)S(1)} %collective-permute-done.10.refs_12_) | copy-start | bytes 884740
  70.9 10.5 %collective-permute-start.1 = (bf16[8,48,384]{2,1,0:T(8,128)(2,1)S(1)}, bf16[8,48,384]{2,1,0:T(8,128)(2,1)S(1)}, u32[]{:S(2)}, u32[]{:S(2)}) collective-permute-start(bf16[8,48,384]{2,1,0:T(8,128)(2,1)S(1)} %get-tuple-element.32.refs_0_), channel_id=1, source_target_pairs={{0,64},{8,72},{16,80},{24,88},{32,96},{40,104},{48,112},{56,120},{... | collective-permute-start | bytes 884744 | tf_op jit(solution)/shard_map/ppermute | solution.py:212
  72.6 15.1 %copy-start.4 = (bf16[8,48,384]{2,1,0:T(8,128)(2,1)}, bf16[8,48,384]{2,1,0:T(8,128)(2,1)S(1)}, u32[]{:S(2)}) copy-start(bf16[8,48,384]{2,1,0:T(8,128)(2,1)S(1)} %collective-permute-done.8.refs_10_) | copy-start | bytes 884740
  72.6 8.8 %collective-permute-start = (bf16[8,48,384]{2,1,0:T(8,128)(2,1)S(1)}, bf16[8,48,384]{2,1,0:T(8,128)(2,1)S(1)}, u32[]{:S(2)}, u32[]{:S(2)}) collective-permute-start(bf16[8,48,384]{2,1,0:T(8,128)(2,1)S(1)} %get-tuple-element.32.refs_0_), channel_id=1, source_target_pairs={{0,8},{8,0},{16,24},{24,16},{32,40},{40,32},{48,56},{56,48},{64,72... | collective-permute-start | bytes 884744 | tf_op jit(solution)/shard_map/ppermute | solution.py:213
  72.6 15.1 %copy-start.5 = (bf16[8,48,384]{2,1,0:T(8,128)(2,1)}, bf16[8,48,384]{2,1,0:T(8,128)(2,1)S(1)}, u32[]{:S(2)}) copy-start(bf16[8,48,384]{2,1,0:T(8,128)(2,1)S(1)} %collective-permute-done.7.refs_9_) | copy-start | bytes 884740
  72.6 9.3 %collective-permute-start.13 = (bf16[8,48,384]{2,1,0:T(8,128)(2,1)S(1)}, bf16[8,48,384]{2,1,0:T(8,128)(2,1)S(1)}, u32[]{:S(2)}, u32[]{:S(2)}) collective-permute-start(bf16[8,48,384]{2,1,0:T(8,128)(2,1)S(1)} %collective-permute-done.12.refs_14_), channel_id=1, source_target_pairs={{0,8},{8,0},{16,24},{24,16},{32,40},{40,32},{48,56},{56,48},{64,72... | collective-permute-start | bytes 884744 | tf_op jit(solution)/shard_map/ppermute | solution.py:213
  73.1 14.6 %copy-start.6 = (bf16[8,48,384]{2,1,0:T(8,128)(2,1)}, bf16[8,48,384]{2,1,0:T(8,128)(2,1)S(1)}, u32[]{:S(2)}) copy-start(bf16[8,48,384]{2,1,0:T(8,128)(2,1)S(1)} %collective-permute-done.5.refs_6_) | copy-start | bytes 884740
  73.1 14.5 %collective-permute-start.11 = (bf16[8,48,384]{2,1,0:T(8,128)(2,1)S(1)}, bf16[8,48,384]{2,1,0:T(8,128)(2,1)S(1)}, u32[]{:S(2)}, u32[]{:S(2)}) collective-permute-start(bf16[8,48,384]{2,1,0:T(8,128)(2,1)S(1)} %collective-permute-done.10.refs_12_), channel_id=1, source_target_pairs={{0,8},{8,0},{16,24},{24,16},{32,40},{40,32},{48,56},{56,48},{64,72... | collective-permute-start | bytes 884744 | tf_op jit(solution)/shard_map/ppermute | solution.py:213
  76.9 10.8 %copy-start.7 = (bf16[8,48,384]{2,1,0:T(8,128)(2,1)}, bf16[8,48,384]{2,1,0:T(8,128)(2,1)S(1)}, u32[]{:S(2)}) copy-start(bf16[8,48,384]{2,1,0:T(8,128)(2,1)S(1)} %collective-permute-done.3.refs_4_) | copy-start | bytes 884740
  76.9 10.7 %collective-permute-start.9 = (bf16[8,48,384]{2,1,0:T(8,128)(2,1)S(1)}, bf16[8,48,384]{2,1,0:T(8,128)(2,1)S(1)}, u32[]{:S(2)}, u32[]{:S(2)}) collective-permute-start(bf16[8,48,384]{2,1,0:T(8,128)(2,1)S(1)} %collective-permute-done.8.refs_10_), channel_id=1, source_target_pairs={{0,8},{8,0},{16,24},{24,16},{32,40},{40,32},{48,56},{56,48},{64,72... | collective-permute-start | bytes 884744 | tf_op jit(solution)/shard_map/ppermute | solution.py:213
  81.3 6.4 %copy-start.8 = (bf16[8,48,384]{2,1,0:T(8,128)(2,1)}, bf16[8,48,384]{2,1,0:T(8,128)(2,1)S(1)}, u32[]{:S(2)}) copy-start(bf16[8,48,384]{2,1,0:T(8,128)(2,1)S(1)} %collective-permute-done.1.refs_2_) | copy-start | bytes 884740
  81.3 6.3 %collective-permute-start.6 = (bf16[8,48,384]{2,1,0:T(8,128)(2,1)S(1)}, bf16[8,48,384]{2,1,0:T(8,128)(2,1)S(1)}, u32[]{:S(2)}, u32[]{:S(2)}) collective-permute-start(bf16[8,48,384]{2,1,0:T(8,128)(2,1)S(1)} %collective-permute-done.5.refs_6_), channel_id=1, source_target_pairs={{0,8},{8,0},{16,24},{24,16},{32,40},{40,32},{48,56},{56,48},{64,72... | collective-permute-start | bytes 884744 | tf_op jit(solution)/shard_map/ppermute | solution.py:213
  81.4 6.4 %copy-start.9 = (bf16[8,48,384]{2,1,0:T(8,128)(2,1)}, bf16[8,48,384]{2,1,0:T(8,128)(2,1)S(1)}, u32[]{:S(2)}) copy-start(bf16[8,48,384]{2,1,0:T(8,128)(2,1)S(1)} %collective-permute-done.refs_1_) | copy-start | bytes 884740
  81.4 6.2 %collective-permute-start.4 = (bf16[8,48,384]{2,1,0:T(8,128)(2,1)S(1)}, bf16[8,48,384]{2,1,0:T(8,128)(2,1)S(1)}, u32[]{:S(2)}, u32[]{:S(2)}) collective-permute-start(bf16[8,48,384]{2,1,0:T(8,128)(2,1)S(1)} %collective-permute-done.3.refs_4_), channel_id=1, source_target_pairs={{0,8},{8,0},{16,24},{24,16},{32,40},{40,32},{48,56},{56,48},{64,72... | collective-permute-start | bytes 884744 | tf_op jit(solution)/shard_map/ppermute | solution.py:213
  81.9 5.9 %copy-start.10 = (bf16[8,48,384]{2,1,0:T(8,128)(2,1)}, bf16[8,48,384]{2,1,0:T(8,128)(2,1)S(1)}, u32[]{:S(2)}) copy-start(bf16[8,48,384]{2,1,0:T(8,128)(2,1)S(1)} %collective-permute-done.13.refs_15_) | copy-start | bytes 884740
  81.9 5.8 %collective-permute-start.2 = (bf16[8,48,384]{2,1,0:T(8,128)(2,1)S(1)}, bf16[8,48,384]{2,1,0:T(8,128)(2,1)S(1)}, u32[]{:S(2)}, u32[]{:S(2)}) collective-permute-start(bf16[8,48,384]{2,1,0:T(8,128)(2,1)S(1)} %collective-permute-done.1.refs_2_), channel_id=1, source_target_pairs={{0,8},{8,0},{16,24},{24,16},{32,40},{40,32},{48,56},{56,48},{64,72... | collective-permute-start | bytes 884744 | tf_op jit(solution)/shard_map/ppermute | solution.py:213
  87.6 0.7 copy-start.11
  87.6 0.8 copy-start.12
  87.6 0.9 copy-start.13
  87.6 1.0 copy-start.14
  88.6 0.7 copy-start.15
  105.2 9.3 %collective-permute-start.20 = (f32[8,512]{1,0:T(8,128)}, f32[8,512]{1,0:T(8,128)S(1)}, u32[]{:S(2)}, u32[]{:S(2)}) collective-permute-start(f32[8,512]{1,0:T(8,128)} %get-tuple-element.20.refs_0_), channel_id=1, source_target_pairs={{0,7},{1,0},{2,1},{3,2},{4,3},{5,4},{6,5},{7,6},{8,15},{9,8},{10,9... | collective-permute-start | bytes 49160 | tf_op jit(solution)/shard_map/ppermute | solution.py:362
  105.2 10.4 %collective-permute-start.19 = (f32[8,512]{1,0:T(8,128)}, f32[8,512]{1,0:T(8,128)S(1)}, u32[]{:S(2)}, u32[]{:S(2)}) collective-permute-start(f32[8,512]{1,0:T(8,128)} %get-tuple-element.20.refs_0_), channel_id=1, source_target_pairs={{0,6},{1,7},{2,0},{3,1},{4,2},{5,3},{6,4},{7,5},{8,14},{9,15},{10,... | collective-permute-start | bytes 49160 | tf_op jit(solution)/shard_map/ppermute | solution.py:362
  106.3 9.5 %collective-permute-start.18 = (f32[8,512]{1,0:T(8,128)}, f32[8,512]{1,0:T(8,128)S(1)}, u32[]{:S(2)}, u32[]{:S(2)}) collective-permute-start(f32[8,512]{1,0:T(8,128)} %get-tuple-element.20.refs_0_), channel_id=1, source_target_pairs={{0,5},{1,6},{2,7},{3,0},{4,1},{5,2},{6,3},{7,4},{8,13},{9,14},{10,... | collective-permute-start | bytes 49160 | tf_op jit(solution)/shard_map/ppermute | solution.py:362
  109.2 8.0 %collective-permute-start.17 = (f32[8,512]{1,0:T(8,128)}, f32[8,512]{1,0:T(8,128)S(1)}, u32[]{:S(2)}, u32[]{:S(2)}) collective-permute-start(f32[8,512]{1,0:T(8,128)} %get-tuple-element.20.refs_0_), channel_id=1, source_target_pairs={{0,4},{1,5},{2,6},{3,7},{4,0},{5,1},{6,2},{7,3},{8,12},{9,13},{10,... | collective-permute-start | bytes 49160 | tf_op jit(solution)/shard_map/ppermute | solution.py:362
  112.2 7.0 %collective-permute-start.16 = (f32[8,512]{1,0:T(8,128)}, f32[8,512]{1,0:T(8,128)S(1)}, u32[]{:S(2)}, u32[]{:S(2)}) collective-permute-start(f32[8,512]{1,0:T(8,128)} %get-tuple-element.20.refs_0_), channel_id=1, source_target_pairs={{0,3},{1,4},{2,5},{3,6},{4,7},{5,0},{6,1},{7,2},{8,11},{9,12},{10,... | collective-permute-start | bytes 49160 | tf_op jit(solution)/shard_map/ppermute | solution.py:362
  114.6 6.2 %copy-start.16 = (f32[8,512]{1,0:T(8,128)}, f32[8,512]{1,0:T(8,128)S(1)}, u32[]{:S(2)}) copy-start(f32[8,512]{1,0:T(8,128)S(1)} %collective-permute-done.20.refs_7_) | copy-start | bytes 49156
  114.6 6.1 %collective-permute-start.15 = (f32[8,512]{1,0:T(8,128)}, f32[8,512]{1,0:T(8,128)S(1)}, u32[]{:S(2)}, u32[]{:S(2)}) collective-permute-start(f32[8,512]{1,0:T(8,128)} %get-tuple-element.20.refs_0_), channel_id=1, source_target_pairs={{0,2},{1,3},{2,4},{3,5},{4,6},{5,7},{6,0},{7,1},{8,10},{9,11},{10,... | collective-permute-start | bytes 49160 | tf_op jit(solution)/shard_map/ppermute | solution.py:362
  115.6 5.2 %copy-start.17 = (f32[8,512]{1,0:T(8,128)}, f32[8,512]{1,0:T(8,128)S(1)}, u32[]{:S(2)}) copy-start(f32[8,512]{1,0:T(8,128)S(1)} %collective-permute-done.19.refs_6_) | copy-start | bytes 49156
  115.6 5.2 %collective-permute-start.14 = (f32[8,512]{1,0:T(8,128)}, f32[8,512]{1,0:T(8,128)S(1)}, u32[]{:S(2)}, u32[]{:S(2)}) collective-permute-start(f32[8,512]{1,0:T(8,128)} %get-tuple-element.20.refs_0_), channel_id=1, source_target_pairs={{0,1},{1,2},{2,3},{3,4},{4,5},{5,6},{6,7},{7,0},{8,9},{9,10},{10,1... | collective-permute-start | bytes 49160 | tf_op jit(solution)/shard_map/ppermute | solution.py:362
  115.8 5.0 %copy-start.18 = (f32[8,512]{1,0:T(8,128)}, f32[8,512]{1,0:T(8,128)S(1)}, u32[]{:S(2)}) copy-start(f32[8,512]{1,0:T(8,128)S(1)} %collective-permute-done.18.refs_5_) | copy-start | bytes 49156
  117.3 3.6 %copy-start.19 = (f32[8,512]{1,0:T(8,128)}, f32[8,512]{1,0:T(8,128)S(1)}, u32[]{:S(2)}) copy-start(f32[8,512]{1,0:T(8,128)S(1)} %collective-permute-done.17.refs_4_) | copy-start | bytes 49156
  119.2 1.7 copy-start.20
  120.7 0.6 copy-start.21
  136.6 6.0 %collective-permute-start.21 = (bf16[4,768,384]{2,1,0:T(8,128)(2,1)}, bf16[4,768,384]{2,1,0:T(8,128)(2,1)S(1)}, u32[]{:S(2)}, u32[]{:S(2)}) collective-permute-start(bf16[4,768,384]{2,1,0:T(8,128)(2,1)} %shard_map.128), channel_id=1, source_target_pairs={{0,8},{8,0},{16,24},{24,16},{32,40},{40,32},{48,56},{56,48},{64,72... | collective-permute-start | bytes 7077896 | tf_op jit(solution)/shard_map/ppermute | solution.py:370
  181.6 18.1 %collective-permute-start.22 = (bf16[192,384]{1,0:T(8,128)(2,1)S(1)}, bf16[192,384]{1,0:T(8,128)(2,1)S(1)}, u32[]{:S(2)}, u32[]{:S(2)}) collective-permute-start(bf16[192,384]{1,0:T(8,128)(2,1)S(1)} %reduce_sum.12), channel_id=1, source_target_pairs={{0,0},{1,32},{2,64},{3,96},{4,128},{5,160},{6,192},{7,224},{8,4},{... | collective-permute-start | bytes 442376 | tf_op jit(solution)/shard_map/ppermute | solution.py:383
  (1 other events, 0.6 us)
Sparse Core Ops, SparseCore 0:
  15.6 60.3 all-gather.1
  130.7 44.6 reduce-scatter.1
where the time goes:
time: 217 us; the launch traced here: 215 us
  blocking collectives  70.4 us (32%)
  Pallas kernels  67.5 us (31%)
  waiting for transfers between devices  29.8 us (14%)
  starting transfers between devices  26.6 us (12%)
  between operations  14.3 us (7%)
  local copies, waits for them, and re-layouts  3.58 us (2%)
  other arithmetic  3.3 us (2%)
    pallas_call x10, Pallas kernels, call(): pl.pallas_call(kernel, grid_spec=pltpu.PrefetchScalarGridSpec(num_scalar_...  67.5 us
    all_to_all x1, blocking collectives, on_device(): lax.all_to_all(pair, 'dp', split_axis=0, concat_axis=0, tiled=True, axis_...  36.4 us
    all_to_all x1, blocking collectives, gather_columns(): got = lax.all_to_all(cut, 'mp', split_axis=0, concat_axis=0, tiled=True)  34 us
    ppermute x6, waiting for transfers between devices, gather_columns(): lax.ppermute(own, 'dp', permute_tables[stream][step])  13.3 us
    ppermute x6, starting transfers between devices, gather_columns(): lax.ppermute(own, 'dp', permute_tables[stream][step])  12.5 us
    ppermute x1, waiting for transfers between devices, on_device(): weight_grad = lax.ppermute(total, ('dp', 'mp'), home).astype(F32).T  11.4 us
    ppermute x7, starting transfers between devices, on_device(): lax.ppermute(sums, 'mp', [(m, (m + s) % ranks) for m in range(ranks)])  10.6 us
    ppermute x7, waiting for transfers between devices, on_device(): lax.ppermute(sums, 'mp', [(m, (m + s) % ranks) for m in range(ranks)])  4.99 us
  transfers between devices with their start and end apart: 25, of which 9 were waited for; matrix products, arithmetic and copies ran while one was open for 2% of the time, Pallas kernels for 16%

commit v1 on v0

--- a/solution.py
+++ b/solution.py
@@ -20,7 +20,8 @@
     return pltpu.CompilerParams(vmem_limit_bytes=VMEM_LIMIT)
 
 
-def call(kernel, grid, prefetched, in_specs, out_specs, out_shape, scratch, *operands):
+def call(kernel, grid, prefetched, in_specs, out_specs, out_shape, scratch, *operands, flops=0):
+    moved = sum(a.size * a.dtype.itemsize for a in jax.tree.leaves((operands, out_shape)))
     return pl.pallas_call(
         kernel,
         grid_spec=pltpu.PrefetchScalarGridSpec(
@@ -32,6 +33,7 @@
         ),
         out_shape=out_shape,
         compiler_params=params(),
+        cost_estimate=pl.CostEstimate(flops=flops, bytes_accessed=moved, transcendentals=0),
     )(*prefetched, *operands)
 
 
@@ -168,58 +170,63 @@
 
 
 def cut_kernel(info, left, right, out):
-    half = left.shape[1]
-    out[0, :, :half] = left[...]
-    out[0, :, half:] = right[...]
+    ranks, _, width = out.shape
+    half = width // 2
+    for m in range(ranks):
+        out[m, :, :half] = left[:, m * width:m * width + half]
+        out[m, :, half:] = right[:, m * width + half:(m + 1) * width]
 
 
 def assemble_kernel(info, *refs):
-    out = refs[-1]
-    half = out.shape[2] // 2
-    rows = out.shape[1]
-    part = rows // 8
+    *pieces, out = refs
+    _, rows, width = out.shape
+    half, part = width // 2, rows // 8
     for stream in range(2):
-        place = info[2 + stream]
         for at, step in enumerate(STEPS):
-            quarter = lax.rem(place + 4 + step, 4)
+            quarter = lax.rem(info[2 + stream] + 4 + step, 4)
             for core in range(2):
-                piece = refs[(stream * 4 + at) * 2 + core]
-                side = jnp.where(core == 0, info[4], 1 - info[4])
+                side = info[4] if core == 0 else 1 - info[4]
                 start = pl.multiple_of((side * 4 + quarter) * part, 16)
-                out[0, pl.ds(start, part), pl.ds(stream * half, half)] = piece[0]
-
-
-def gather_columns(info, out_proj, permute_tables):
+                piece = pieces[(stream * 4 + at) * 2 + core]
+                out[:, pl.ds(start, part), stream * half:(stream + 1) * half] = piece[...]
+
+
+def gather_columns(info, out_proj, chips):
     rows, full = out_proj.shape
     ranks = lax.axis_size("mp")
     width = full // ranks
     half, part = width // 2, rows // 8
     cut = call(
-        cut_kernel, (ranks,), (info,),
+        cut_kernel, (1,), (info,),
         [
-            pl.BlockSpec((part, half), lambda m, i: (i[4] * 4 + i[2], 2 * m)),
-            pl.BlockSpec((part, half), lambda m, i: (i[4] * 4 + i[3], 2 * m + 1)),
+            pl.BlockSpec((part, full), lambda _, i: (i[4] * 4 + i[2], 0)),
+            pl.BlockSpec((part, full), lambda _, i: (i[4] * 4 + i[3], 0)),
         ],
-        pl.BlockSpec((1, part, width), lambda m, i: (m, 0, 0)),
+        pl.BlockSpec((ranks, part, width), lambda _, i: (0, 0, 0)),
         jax.ShapeDtypeStruct((ranks, part, width), BF), [],
         out_proj, out_proj,
     )
     got = lax.all_to_all(cut, "mp", split_axis=0, concat_axis=0, tiled=True)
+    swap = [(dp_index(y, x, c), dp_index(y, x, 1 - c)) for y, x, c in chips]
     pieces = []
     for stream in range(2):
         own = got[:, :, stream * half:(stream + 1) * half]
-        for step in STEPS:
-            piece = own if step == 0 else lax.ppermute(own, "dp", permute_tables[stream][step])
-            pieces += [piece, lax.ppermute(piece, "dp", permute_tables[2])]
-    piece_spec = pl.BlockSpec((1, part, half), lambda m, i: (m, 0, 0))
+        for s in STEPS:
+            if stream == 0:
+                table = [(dp_index(y, x, c), dp_index(y - s, x, c)) for y, x, c in chips]
+            else:
+                table = [(dp_index(y, x, c), dp_index(y, x - s, c)) for y, x, c in chips]
+            piece = own if s == 0 else lax.ppermute(own, "dp", table)
+            pieces += [piece, lax.ppermute(piece, "dp", swap)]
+    steps = 2
     whole = call(
-        assemble_kernel, (ranks,), (info,),
-        [piece_spec] * 16,
-        pl.BlockSpec((1, rows, width), lambda m, i: (m, 0, 0)),
+        assemble_kernel, (steps,), (info,),
+        [pl.BlockSpec((ranks // steps, part, half), lambda m, i: (m, 0, 0))] * 16,
+        pl.BlockSpec((ranks // steps, rows, width), lambda m, i: (m, 0, 0)),
         jax.ShapeDtypeStruct((ranks, rows, width), BF), [],
         *pieces,
     )
-    return whole.reshape(ranks * rows, width)
+    return cut, whole.reshape(ranks * rows, width)
 
 
 def project_kernel(info, mixed, weight, grad, gain, projected, sums):
@@ -306,29 +313,31 @@
     )
 
 
-def outer_kernel(info, grad_proj, mixed, out, turned):
-    @pl.when(pl.program_id(0) == 0)
-    def _():
-        turned[...] = jnp.transpose(grad_proj[...])
-
-    out[0] = dot(turned[...], mixed[...], (1, 0)).astype(BF)
-
-
-def outer(info, grad_proj, mixed, keep):
-    width = grad_proj.shape[1]
+def outer_kernel(info, own_grad, other_grad, own_mixed, other_mixed, out, turned):
+    @pl.when(pl.program_id(0) == 0)
+    def _():
+        turned[:, :KEEP_MAX] = jnp.transpose(own_grad[...])
+        turned[:, KEEP_MAX:] = jnp.transpose(other_grad[...])
+
+    rows = jnp.concatenate([own_mixed[...], other_mixed[...]], axis=0)
+    out[0] = dot(turned[...], rows, (1, 0)).astype(BF)
+
+
+def outer(info, own_grad, other_grad, mixed, other_mixed):
+    width = own_grad.shape[1]
     block = mixed.shape[1] // 8
-
-    def at(j, i):
-        side = i[4] if keep else 1 - i[4]
-        return 0, side * 4 + j
-
+    grad_spec = pl.BlockSpec((KEEP_MAX, width), lambda j, i: (0, 0))
     return call(
         outer_kernel, (4,), (info,),
-        [pl.BlockSpec((KEEP_MAX, width), lambda j, i: (0, 0)), pl.BlockSpec((KEEP_MAX, block), at)],
+        [
+            grad_spec, grad_spec,
+            pl.BlockSpec((KEEP_MAX, block), lambda j, i: (0, i[4] * 4 + j)),
+            pl.BlockSpec((KEEP_MAX, block), lambda j, i: (0, j)),
+        ],
         pl.BlockSpec((1, width, block), lambda j, i: (j, 0, 0)),
         jax.ShapeDtypeStruct((4, width, block), BF),
-        [pltpu.VMEM((width, KEEP_MAX), BF)],
-        grad_proj, mixed,
+        [pltpu.VMEM((width, 2 * KEEP_MAX), BF)],
+        own_grad, other_grad, mixed, other_mixed,
     )
 
 
@@ -344,33 +353,37 @@
     rank = lax.axis_index("mp")
     info = jnp.stack([image, rank, image // 8, (image // 2) % 4, image % 2]).astype(jnp.int32)
     chips = [(y, x, core) for y in range(4) for x in range(4) for core in range(2)]
-    tables = (
-        {s: [(dp_index(y, x, c), dp_index(y - s, x, c)) for y, x, c in chips] for s in STEPS[1:]},
-        {s: [(dp_index(y, x, c), dp_index(y, x - s, c)) for y, x, c in chips] for s in STEPS[1:]},
-        [(dp_index(y, x, c), dp_index(y, x, 1 - c)) for y, x, c in chips],
-    )
+    swap = [(dp_index(y, x, c), dp_index(y, x, 1 - c)) for y, x, c in chips]
     gain = norm_gain.reshape(1, -1)
 
-    columns = gather_columns(info, out_proj, tables)
+    cut, columns = gather_columns(info, out_proj, chips)
+    early, _ = lax.optimization_barrier((info, cut))
     mixed, query_c, key_c, value_c, weights = attend(
-        info, keep_count, keep_order, query_heads, key_heads, value_heads
+        early, keep_count, keep_order, query_heads, key_heads, value_heads
     )
     mixed_all = lax.all_gather(mixed, "mp", axis=1, tiled=True)
-    grad_c = pick_rows(info, keep_count, keep_order, cotangent)
+    late, _ = lax.optimization_barrier((info, columns))
+    grad_c = pick_rows(late, keep_count, keep_order, cotangent)
     projected, sums = project(info, mixed_all, columns, grad_c, gain)
-    all_sums = [sums] + [
-        lax.ppermute(sums, "mp", [(m, (m + s) % ranks) for m in range(ranks)]) for s in range(1, ranks)
+    pair_sums = sums + lax.ppermute(sums, "mp", [(m, m ^ 1) for m in range(ranks)])
+    all_sums = [pair_sums] + [
+        lax.ppermute(pair_sums, "mp", [(m, m ^ s) for m in range(ranks)]) for s in range(2, ranks, 2)
     ]
+    half = mixed_all.shape[1] // 2
+    sent_mixed = lax.dynamic_slice_in_dim(mixed_all, (1 - image % 2) * half, half, 1)
+    other_mixed = lax.ppermute(sent_mixed, "dp", swap)
+    all_sums, other_mixed = lax.optimization_barrier((all_sums, other_mixed))
     mixed_grad, grad_proj, normed_c = grad_rows(
         info, keep_count, projected, grad_c, gain, columns, all_sums, norm_gain.shape[0]
     )
     grad_mixed = lax.psum_scatter(mixed_grad, "mp", scatter_dimension=0, tiled=True)[0]
 
-    sent = outer(info, grad_proj, mixed_all, False)
-    other = lax.ppermute(sent, "dp", tables[2])
-    kept = outer(info, grad_proj, mixed_all, True)
-    width, depth = kept.shape[1], kept.shape[2]
-    pair = (kept.astype(F32) + other.astype(F32)).astype(BF).reshape(16, width // 4, depth)
+    other_grad = lax.ppermute(grad_proj, "dp", swap)
+    normed = place_rows(info, keep_count, keep_order, normed_c)
+    other_grad, normed = lax.optimization_barrier((other_grad, normed))
+    pair = outer(info, grad_proj, other_grad, mixed_all, other_mixed)
+    width, depth = pair.shape[1], pair.shape[2]
+    pair = pair.reshape(16, width // 4, depth)
     groups = [[2 * j + c for j in range(16)] for c in range(2)]
     spread = lax.all_to_all(
         pair, "dp", split_axis=0, concat_axis=0, tiled=True, axis_index_groups=groups
@@ -380,11 +393,11 @@
         (dp_index(y, x, c) * ranks + m, (4 * m + x) * ranks + 4 * c + y)
         for y, x, c in chips for m in range(ranks)
     ]
-    weight_grad = lax.ppermute(total, ("dp", "mp"), home).astype(F32).T
-
-    normed = place_rows(info, keep_count, keep_order, normed_c)
+    total = lax.ppermute(total, ("dp", "mp"), home)
+
     grads = attend_back(info, keep_count, keep_order, grad_mixed, query_c, key_c, value_c, weights)
-    return (normed, *grads, weight_grad)
+    total, grads = lax.optimization_barrier((total, grads))
+    return (normed, *grads, total.astype(F32).T)
 
 
 def solution(mesh):

time: 217 us -> 230 us (1.060)
  waiting for transfers between devices: 29.8 us -> 81.6 us
  blocking collectives: 70.4 us -> 35.9 us
  Pallas kernels: 67.5 us -> 58.6 us
  starting transfers between devices: 26.6 us -> 30.2 us
  local copies, waits for them, and re-layouts: 3.58 us -> 6.33 us
    all_gather x1, waiting for transfers between devices: 0.02 us -> 46.3 us  [on_device(): mixed_all = lax.all_gather(mixed, 'mp', axis=1, tiled=True)]
    all_to_all x1 -> x0, blocking collectives: 34 us -> none  [gather_columns(): got = lax.all_to_all(cut, 'mp', split_axis=0, concat_axis=0, tiled=True)]
    pallas_call x10 -> x9, Pallas kernels: 67.5 us -> 58.6 us  [call(): pl.pallas_call(kernel, grid_spec=pltpu.PrefetchScalarGridSpec(num_scalar_...]
    all_to_all x0 -> x1, starting transfers between devices: none -> 8.47 us  [gather_columns(): got = lax.all_to_all(cut, 'mp', split_axis=0, concat_axis=0, tiled=True)]
    ppermute x23 -> x21, waiting for transfers between devices: 29.7 us -> 35.2 us  [the longest x6 19.6 us: gather_columns(): piece = own if s == 0 else lax.ppermute(own, 'dp', table)]
    ppermute x23 -> x21, starting transfers between devices: 26.5 us -> 21.6 us  [the longest x6 10.5 us: gather_columns(): piece = own if s == 0 else lax.ppermute(own, 'dp', table)]
  transfers between devices with their start and end apart: 25 -> 24, of which waited for: 9 -> 13; matrix products, arithmetic and copies ran while one was open for 2% -> 1% of each run, Pallas kernels for 16% -> 17%
where the time goes in v1:
time: 230 us; the launch traced here: 229 us
  waiting for transfers between devices  81.6 us (35%)
  Pallas kernels  58.6 us (25%)
  blocking collectives  35.9 us (16%)
  starting transfers between devices  30.2 us (13%)
  between operations  14.3 us (6%)
  local copies, waits for them, and re-layouts  6.33 us (3%)
    pallas_call x9, Pallas kernels, call(): pl.pallas_call(kernel, grid_spec=pltpu.PrefetchScalarGridSpec(num_scalar_...  58.6 us
    all_gather x1, waiting for transfers between devices, on_device(): mixed_all = lax.all_gather(mixed, 'mp', axis=1, tiled=True)  46.3 us
    all_to_all x1, blocking collectives, on_device(): lax.all_to_all(pair, 'dp', split_axis=0, concat_axis=0, tiled=True, axis_...  35.9 us
    ppermute x6, waiting for transfers between devices, gather_columns(): piece = own if s == 0 else lax.ppermute(own, 'dp', table)  19.6 us
    ppermute x6, starting transfers between devices, gather_columns(): piece = own if s == 0 else lax.ppermute(own, 'dp', table)  10.5 us
    all_to_all x1, starting transfers between devices, gather_columns(): got = lax.all_to_all(cut, 'mp', split_axis=0, concat_axis=0, tiled=True)  8.47 us
    ppermute x1, waiting for transfers between devices, on_device(): total = lax.ppermute(total, ('dp', 'mp'), home)  7.75 us
    ppermute x3, starting transfers between devices, on_device(): lax.ppermute(pair_sums, 'mp', [(m, m ^ s) for m in range(ranks)])  6.5 us
  transfers between devices with their start and end apart: 24, of which 13 were waited for; matrix products, arithmetic and copies ran while one was open for 1% of the time, Pallas kernels for 17%

profile of v1, /device:TPU:2, one launch (start us, length us, event | category | flops | bytes accessed | tf_op | source)
XLA Modules:
  0.0 228.7 jit_solution(14899179073502414879)
XLA Ops:
  7.3 0.6 stack.23.info
  7.9 2.8 %shard_map.119 = bf16[8,48,768]{2,1,0:T(8,128)(2,1)} custom-call(s32[5]{0:T(128)} %stack.23.info, bf16[384,6144]{1,0:T(8,128)(2,1)} %right.1, bf16[384,6144]{1,0:T(8,128)(2,1)} %right.1), custom_call_target="tpu_custom_call" | custom-call | bytes 10027008 | tf_op jit(solution)/shard_map/pallas_call | solution.py:25
  10.7 7.5 %shard_map.120 = (bf16[512,384]{1,0:T(8,128)(2,1)}, bf16[512,384]{1,0:T(8,128)(2,1)}, bf16[512,384]{1,0:T(8,128)(2,1)}, bf16[512,384]{1,0:T(8,128)(2,1)}, f32[3,512,512]{2,1,0:T(8,128)}) custom-call(s32[5]{0:T(128)} %stack.23.info, s32[32]{0:T(128)} %counts.9, s32[1,1024]{1,0:T(1,128)} %order.7, bf16[1,1024,384]{2,1,0:T(8,128)(2,1)} %query.1, ...), custom_call_target="tpu_custom_call" | custom-call | bytes 7081984 | tf_op jit(solution)/shard_map/pallas_call | solution.py:25
  18.2 8.5 %all-to-all-start = ((bf16[8,48,768]{2,1,0:T(8,128)(2,1)}), bf16[8,48,768]{2,1,0:T(8,128)(2,1)S(1)}, u32[]{:S(2)}, u32[]{:S(2)}) async-start(bf16[8,48,768]{2,1,0:T(8,128)(2,1)} %shard_map.119), calls=%async_computation | async-start | bytes 1179648 | tf_op jit(solution)/shard_map/all_to_all | solution.py:209
  26.7 46.3 %all-gather.2.cloned.1.call-done.mixed.own_mixed = bf16[512,3072]{1,0:T(8,128)(2,1)} async-done(((bf16[512,384]{1,0:T(8,128)(2,1)}), bf16[512,3072]{1,0:T(8,128)(2,1)}) %all-gather.2.cloned.1.call-update) | async-done | bytes 3145744 | tf_op jit(solution)/shard_map/all_gather | solution.py:364
  73.1 1.5 constant_dynamic-slice_fusion
  74.8 2.2 collective-permute-start.12
  77.0 1.4 collective-permute-start.10
  78.4 0.6 collective-permute-start.8
  79.0 7.2 %collective-permute-done.12.refs_14_ = bf16[8,48,384]{2,1,0:T(8,128)(2,1)S(1)} collective-permute-done((bf16[8,48,384]{2,1,0:T(8,128)(2,1)S(1)}, bf16[8,48,384]{2,1,0:T(8,128)(2,1)S(1)}, u32[]{:S(2)}, u32[]{:S(2)}) %collective-permute-start.12) | collective-permute-done | bytes 294944 | tf_op jit(solution)/shard_map/ppermute | solution.py:219
  86.2 3.2 %collective-permute-start.5 = (bf16[8,48,384]{2,1,0:T(8,128)(2,1)S(1)}, bf16[8,48,384]{2,1,0:T(8,128)(2,1)S(1)}, u32[]{:S(2)}, u32[]{:S(2)}) collective-permute-start(bf16[8,48,384]{2,1,0:T(8,128)(2,1)S(1)} %get-tuple-element.58.refs_0_), channel_id=1, source_target_pairs={{0,128},{8,136},{16,144},{24,152},{32,160},{40,168},{48,176},{56,1... | collective-permute-start | bytes 884744 | tf_op jit(solution)/shard_map/ppermute | solution.py:219
  89.4 2.7 %collective-permute-done.10.refs_12_ = bf16[8,48,384]{2,1,0:T(8,128)(2,1)S(1)} collective-permute-done((bf16[8,48,384]{2,1,0:T(8,128)(2,1)S(1)}, bf16[8,48,384]{2,1,0:T(8,128)(2,1)S(1)}, u32[]{:S(2)}, u32[]{:S(2)}) %collective-permute-start.10) | collective-permute-done | bytes 294944 | tf_op jit(solution)/shard_map/ppermute | solution.py:219
  92.1 3.0 %collective-permute-start.3 = (bf16[8,48,384]{2,1,0:T(8,128)(2,1)S(1)}, bf16[8,48,384]{2,1,0:T(8,128)(2,1)S(1)}, u32[]{:S(2)}, u32[]{:S(2)}) collective-permute-start(bf16[8,48,384]{2,1,0:T(8,128)(2,1)S(1)} %get-tuple-element.58.refs_0_), channel_id=1, source_target_pairs={{0,192},{8,200},{16,208},{24,216},{32,224},{40,232},{48,240},{56,2... | collective-permute-start | bytes 884744 | tf_op jit(solution)/shard_map/ppermute | solution.py:219
  95.2 0.7 collective-permute-done.5.refs_6_
  95.9 6.7 %collective-permute-done.3.refs_4_ = bf16[8,48,384]{2,1,0:T(8,128)(2,1)S(1)} collective-permute-done((bf16[8,48,384]{2,1,0:T(8,128)(2,1)S(1)}, bf16[8,48,384]{2,1,0:T(8,128)(2,1)S(1)}, u32[]{:S(2)}, u32[]{:S(2)}) %collective-permute-start.3) | collective-permute-done | bytes 294944 | tf_op jit(solution)/shard_map/ppermute | solution.py:219
  102.6 2.4 %collective-permute-done.1.refs_2_ = bf16[8,48,384]{2,1,0:T(8,128)(2,1)S(1)} collective-permute-done((bf16[8,48,384]{2,1,0:T(8,128)(2,1)S(1)}, bf16[8,48,384]{2,1,0:T(8,128)(2,1)S(1)}, u32[]{:S(2)}, u32[]{:S(2)}) %collective-permute-start.1) | collective-permute-done | bytes 294944 | tf_op jit(solution)/shard_map/ppermute | solution.py:219
  105.0 0.5 collective-permute-start.6
  105.5 0.1 collective-permute-start.4
  105.6 0.4 collective-permute-start.2
  106.0 0.6 reshape.20.gain
  106.7 0.3 collective-permute-done.6.refs_7_
  107.0 0.4 collective-permute-done.4.refs_5_
  107.4 0.4 collective-permute-done.2.refs_3_
  108.0 0.2 copy-done.16
  108.1 0.7 copy-done.17
  108.8 4.8 %shard_map.121 = bf16[8,384,768]{2,1,0:T(8,128)(2,1)} custom-call(s32[5]{0:T(128)} %stack.23.info, bf16[8,48,384]{2,1,0:T(8,128)(2,1)} %copy-done.1, bf16[8,48,384]{2,1,0:T(8,128)(2,1)} %copy-done.11, bf16[8,48,384]{2,1,0:T(8,128)(2,1)} %copy-done.10, bf16[8,48,384]{2,1,0:T(8,128)(2,1)} %copy-done.17, bf16[8,48,384]{2,1,0:T(8,128)(2,1)} %copy-done.9, ...), custom_call_target="tpu_custom_call" | custom-call | bytes 9437184 | tf_op jit(solution)/shard_map/pallas_call | solution.py:25
  113.7 4.8 %shard_map.122.grad = bf16[512,768]{1,0:T(8,128)(2,1)} custom-call(s32[5]{0:T(128)} %stack.23.info, s32[32]{0:T(128)} %counts.9, s32[1,1024]{1,0:T(1,128)} %order.7, bf16[1,1024,768]{2,1,0:T(8,128)(2,1)} %tokens.1), custom_call_target="tpu_custom_call" | custom-call | bytes 2363392 | tf_op jit(solution)/shard_map/pallas_call | solution.py:25
  118.5 8.5 %shard_map.123 = (f32[512,768]{1,0:T(8,128)}, f32[8,512]{1,0:T(8,128)}) custom-call(s32[5]{0:T(128)} %stack.23.info, bf16[512,3072]{1,0:T(8,128)(2,1)} %all-gather.2.cloned.1.call-done.mixed.own_mixed, bf16[3072,768]{1,0:T(8,128)(2,1)} %bitcast.10, bf16[512,768]{1,0:T(8,128)(2,1)} %shard_map.122.grad, bf16[1,6144]{1,0:T(2,128)(2,1)} %reshape.20.gain), custom_call_target="tpu_custom_call" | custom-call | bytes 10252288 | tf_op jit(solution)/shard_map/pallas_call | solution.py:25
  127.0 1.4 collective-permute-start.14
  128.3 2.6 %collective-permute-done.14 = f32[8,512]{1,0:T(8,128)S(1)} collective-permute-done((f32[8,512]{1,0:T(8,128)}, f32[8,512]{1,0:T(8,128)S(1)}, u32[]{:S(2)}, u32[]{:S(2)}) %collective-permute-start.14) | collective-permute-done | bytes 16416 | tf_op jit(solution)/shard_map/ppermute | solution.py:368
  130.9 0.7 add.20.refs_0_
  131.6 2.3 %collective-permute-start.17 = (f32[8,512]{1,0:T(8,128)S(1)}, f32[8,512]{1,0:T(8,128)S(1)}, u32[]{:S(2)}, u32[]{:S(2)}) collective-permute-start(f32[8,512]{1,0:T(8,128)S(1)} %add.20.refs_0_), channel_id=1, source_target_pairs={{0,6},{1,7},{2,4},{3,5},{4,2},{5,3},{6,0},{7,1},{8,14},{9,15},{10,... | collective-permute-start | bytes 49160 | tf_op jit(solution)/shard_map/ppermute | solution.py:370
  134.0 3.5 %collective-permute-start.16 = (f32[8,512]{1,0:T(8,128)S(1)}, f32[8,512]{1,0:T(8,128)S(1)}, u32[]{:S(2)}, u32[]{:S(2)}) collective-permute-start(f32[8,512]{1,0:T(8,128)S(1)} %add.20.refs_0_), channel_id=1, source_target_pairs={{0,4},{1,5},{2,6},{3,7},{4,0},{5,1},{6,2},{7,3},{8,12},{9,13},{10,... | collective-permute-start | bytes 49160 | tf_op jit(solution)/shard_map/ppermute | solution.py:370
  137.5 0.6 collective-permute-start.15
  138.1 3.5 %collective-permute-done.16.refs_2_ = f32[8,512]{1,0:T(8,128)S(1)} collective-permute-done((f32[8,512]{1,0:T(8,128)S(1)}, f32[8,512]{1,0:T(8,128)S(1)}, u32[]{:S(2)}, u32[]{:S(2)}) %collective-permute-start.16) | collective-permute-done | bytes 16416 | tf_op jit(solution)/shard_map/ppermute | solution.py:370
  141.6 0.6 collective-permute-done.15.refs_1_
  142.3 0.6 copy-done.21
  142.8 9.1 %shard_map.124 = (bf16[8,512,384]{2,1,0:T(8,128)(2,1)}, bf16[512,768]{1,0:T(8,128)(2,1)}, bf16[512,768]{1,0:T(8,128)(2,1)}) custom-call(s32[5]{0:T(128)} %stack.23.info, s32[32]{0:T(128)} %counts.9, f32[512,768]{1,0:T(8,128)} %get-tuple-element.34.projected, bf16[512,768]{1,0:T(8,128)(2,1)} %shard_map.122.grad, bf16[1,6144]{1,0:T(2,128)(2,1)} %reshape.20.gain, ...), custom_call_target="tpu_custom_call" | custom-call | bytes 11874304 | tf_op jit(solution)/shard_map/pallas_call | solution.py:25
  151.9 1.1 copy-done.2
  153.0 4.6 %shard_map.125 = bf16[1,1024,768]{2,1,0:T(8,128)(2,1)} custom-call(s32[5]{0:T(128)} %stack.23.info, s32[32]{0:T(128)} %counts.9, s32[1,1024]{1,0:T(1,128)} %order.7, bf16[512,768]{1,0:T(8,128)(2,1)} %get-tuple-element.41.rows), custom_call_target="tpu_custom_call" | custom-call | bytes 2363392 | tf_op jit(solution)/shard_map/pallas_call | solution.py:25
  157.7 0.9 copy-done.3
  158.6 8.2 %shard_map.126 = bf16[4,768,384]{2,1,0:T(8,128)(2,1)} custom-call(s32[5]{0:T(128)} %stack.23.info, bf16[512,768]{1,0:T(8,128)(2,1)} %get-tuple-element.40.own_grad, bf16[512,768]{1,0:T(8,128)(2,1)} %copy-done.3, bf16[512,3072]{1,0:T(8,128)(2,1)} %all-gather.2.cloned.1.call-done.mixed.own_mixed, bf16[512,1536]{1,0:T(8,128)(2,1)} %collective-permute-done.18.other_mixed), custom_call_target="tpu_custom_call" | custom-call | bytes 8650752 | tf_op jit(solution)/shard_map/pallas_call | solution.py:25
  166.8 35.9 %all_to_all.10 = bf16[16,192,384]{2,1,0:T(8,128)(2,1)S(1)} all-to-all(bf16[16,192,384]{2,1,0:T(8,128)(2,1)} %bitcast.12), channel_id=1, replica_groups={{0,16,32,48,64,80,96,112,128,144,160,176,192,208,224,240},{8,24,40,56,7..., dimensions={0} | all-to-all | bytes 4718592 | tf_op jit(solution)/shard_map/all_to_all | solution.py:388
  202.7 0.3 reduce_sum.12
  203.0 2.1 collective-permute-start.20
  205.2 8.2 %shard_map.127 = (bf16[1,1024,384]{2,1,0:T(8,128)(2,1)}, bf16[1,1024,384]{2,1,0:T(8,128)(2,1)}, bf16[1,1024,384]{2,1,0:T(8,128)(2,1)}) custom-call(s32[5]{0:T(128)} %stack.23.info, s32[32]{0:T(128)} %counts.9, s32[1,1024]{1,0:T(1,128)} %order.7, bf16[512,384]{1,0:T(8,128)(2,1)} %bitcast.13, bf16[512,384]{1,0:T(8,128)(2,1)} %get-tuple-element.46.query, ...), custom_call_target="tpu_custom_call" | custom-call | bytes 7081984 | tf_op jit(solution)/shard_map/pallas_call | solution.py:25
  213.4 7.8 %collective-permute-done.20 = bf16[192,384]{1,0:T(8,128)(2,1)S(1)} collective-permute-done((bf16[192,384]{1,0:T(8,128)(2,1)S(1)}, bf16[192,384]{1,0:T(8,128)(2,1)S(1)}, u32[]{:S(2)}, u32[]{:S(2)}) %collective-permute-start.20) | collective-permute-done | bytes 147488 | tf_op jit(solution)/shard_map/ppermute | solution.py:396
  221.1 0.7 convert_bitcast_fusion
  (65 shorter events, 0.5 us)
Async XLA Ops:
  7.2 65.9 %all-gather.2.cloned.1.call-start = ((), (), s32[]{:S(2)}) async-start(), calls=%async_computation.3 | async-start | bytes 3538944 | tf_op jit(solution)/shard_map/all_gather | solution.py:364
  18.2 56.5 %all-to-all-start = ((bf16[8,48,768]{2,1,0:T(8,128)(2,1)}), bf16[8,48,768]{2,1,0:T(8,128)(2,1)S(1)}, u32[]{:S(2)}, u32[]{:S(2)}) async-start(bf16[8,48,768]{2,1,0:T(8,128)(2,1)} %shard_map.119), calls=%async_computation | async-start | bytes 1179648 | tf_op jit(solution)/shard_map/all_to_all | solution.py:209
  26.7 79.4 %copy-start.22 = (bf16[6144]{0:T(1024)(128)(2,1)S(1)}, bf16[6144]{0:T(1024)(128)(2,1)}, u32[]{:S(2)}) copy-start(bf16[6144]{0:T(1024)(128)(2,1)} %param.12) | copy-start | bytes 36868
  26.7 178.5 %reduce-scatter.2.cloned.1.call-start = ((), (), s32[]{:S(2)}) async-start(), calls=%async_computation.4 | async-start | bytes 3538944 | tf_op jit(solution)/shard_map/reduce_scatter | solution.py:379
  74.6 67.7 %collective-permute-start.18 = (bf16[512,1536]{1,0:T(8,128)(2,1)S(1)}, bf16[512,1536]{1,0:T(8,128)(2,1)}, u32[]{:S(2)}, u32[]{:S(2)}) collective-permute-start(bf16[512,1536]{1,0:T(8,128)(2,1)S(1)} %constant_dynamic-slice_fusion), channel_id=1, source_target_pairs={{0,8},{8,0},{16,24},{24,16},{32,40},{40,32},{48,56},{56,48},{64,72... | collective-permute-start | bytes 4718600 | tf_op jit(solution)/shard_map/ppermute | solution.py:374
  74.7 33.1 %copy-start = (bf16[8,48,384]{2,1,0:T(8,128)(2,1)}, bf16[8,48,384]{2,1,0:T(8,128)(2,1)S(1)}, u32[]{:S(2)}) copy-start(bf16[8,48,384]{2,1,0:T(8,128)(2,1)S(1)} %get-tuple-element.57.refs_8_) | copy-start | bytes 884740
  74.8 33.1 %copy-start.1 = (bf16[8,48,384]{2,1,0:T(8,128)(2,1)}, bf16[8,48,384]{2,1,0:T(8,128)(2,1)S(1)}, u32[]{:S(2)}) copy-start(bf16[8,48,384]{2,1,0:T(8,128)(2,1)S(1)} %get-tuple-element.58.refs_0_) | copy-start | bytes 884740
  74.8 11.4 %collective-permute-start.12 = (bf16[8,48,384]{2,1,0:T(8,128)(2,1)S(1)}, bf16[8,48,384]{2,1,0:T(8,128)(2,1)S(1)}, u32[]{:S(2)}, u32[]{:S(2)}) collective-permute-start(bf16[8,48,384]{2,1,0:T(8,128)(2,1)S(1)} %get-tuple-element.57.refs_8_), channel_id=1, source_target_pairs={{0,32},{8,40},{16,48},{24,56},{32,0},{40,8},{48,16},{56,24},{64,96... | collective-permute-start | bytes 884744 | tf_op jit(solution)/shard_map/ppermute | solution.py:219
  77.0 15.1 %collective-permute-start.10 = (bf16[8,48,384]{2,1,0:T(8,128)(2,1)S(1)}, bf16[8,48,384]{2,1,0:T(8,128)(2,1)S(1)}, u32[]{:S(2)}, u32[]{:S(2)}) collective-permute-start(bf16[8,48,384]{2,1,0:T(8,128)(2,1)S(1)} %get-tuple-element.57.refs_8_), channel_id=1, source_target_pairs={{0,48},{8,56},{16,0},{24,8},{32,16},{40,24},{48,32},{56,40},{64,11... | collective-permute-start | bytes 884744 | tf_op jit(solution)/shard_map/ppermute | solution.py:219
  78.4 16.7 %collective-permute-start.8 = (bf16[8,48,384]{2,1,0:T(8,128)(2,1)S(1)}, bf16[8,48,384]{2,1,0:T(8,128)(2,1)S(1)}, u32[]{:S(2)}, u32[]{:S(2)}) collective-permute-start(bf16[8,48,384]{2,1,0:T(8,128)(2,1)S(1)} %get-tuple-element.57.refs_8_), channel_id=1, source_target_pairs={{0,16},{8,24},{16,32},{24,40},{32,48},{40,56},{48,0},{56,8},{64,80... | collective-permute-start | bytes 884744 | tf_op jit(solution)/shard_map/ppermute | solution.py:219
  79.0 16.1 %collective-permute-start.7 = (bf16[8,48,384]{2,1,0:T(8,128)(2,1)S(1)}, bf16[8,48,384]{2,1,0:T(8,128)(2,1)S(1)}, u32[]{:S(2)}, u32[]{:S(2)}) collective-permute-start(bf16[8,48,384]{2,1,0:T(8,128)(2,1)S(1)} %get-tuple-element.57.refs_8_), channel_id=1, source_target_pairs={{0,8},{8,0},{16,24},{24,16},{32,40},{40,32},{48,56},{56,48},{64,72... | collective-permute-start | bytes 884744 | tf_op jit(solution)/shard_map/ppermute | solution.py:220
  86.2 21.6 %copy-start.4 = (bf16[8,48,384]{2,1,0:T(8,128)(2,1)}, bf16[8,48,384]{2,1,0:T(8,128)(2,1)S(1)}, u32[]{:S(2)}) copy-start(bf16[8,48,384]{2,1,0:T(8,128)(2,1)S(1)} %collective-permute-done.12.refs_14_) | copy-start | bytes 884740
  86.2 9.7 %collective-permute-start.5 = (bf16[8,48,384]{2,1,0:T(8,128)(2,1)S(1)}, bf16[8,48,384]{2,1,0:T(8,128)(2,1)S(1)}, u32[]{:S(2)}, u32[]{:S(2)}) collective-permute-start(bf16[8,48,384]{2,1,0:T(8,128)(2,1)S(1)} %get-tuple-element.58.refs_0_), channel_id=1, source_target_pairs={{0,128},{8,136},{16,144},{24,152},{32,160},{40,168},{48,176},{56,1... | collective-permute-start | bytes 884744 | tf_op jit(solution)/shard_map/ppermute | solution.py:219
  92.1 15.8 %copy-start.5 = (bf16[8,48,384]{2,1,0:T(8,128)(2,1)}, bf16[8,48,384]{2,1,0:T(8,128)(2,1)S(1)}, u32[]{:S(2)}) copy-start(bf16[8,48,384]{2,1,0:T(8,128)(2,1)S(1)} %collective-permute-done.10.refs_12_) | copy-start | bytes 884740
  92.1 10.5 %collective-permute-start.3 = (bf16[8,48,384]{2,1,0:T(8,128)(2,1)S(1)}, bf16[8,48,384]{2,1,0:T(8,128)(2,1)S(1)}, u32[]{:S(2)}, u32[]{:S(2)}) collective-permute-start(bf16[8,48,384]{2,1,0:T(8,128)(2,1)S(1)} %get-tuple-element.58.refs_0_), channel_id=1, source_target_pairs={{0,192},{8,200},{16,208},{24,216},{32,224},{40,232},{48,240},{56,2... | collective-permute-start | bytes 884744 | tf_op jit(solution)/shard_map/ppermute | solution.py:219
  95.1 12.8 %copy-start.6 = (bf16[8,48,384]{2,1,0:T(8,128)(2,1)}, bf16[8,48,384]{2,1,0:T(8,128)(2,1)S(1)}, u32[]{:S(2)}) copy-start(bf16[8,48,384]{2,1,0:T(8,128)(2,1)S(1)} %collective-permute-done.8.refs_10_) | copy-start | bytes 884740
  95.1 9.9 %collective-permute-start.1 = (bf16[8,48,384]{2,1,0:T(8,128)(2,1)S(1)}, bf16[8,48,384]{2,1,0:T(8,128)(2,1)S(1)}, u32[]{:S(2)}, u32[]{:S(2)}) collective-permute-start(bf16[8,48,384]{2,1,0:T(8,128)(2,1)S(1)} %get-tuple-element.58.refs_0_), channel_id=1, source_target_pairs={{0,64},{8,72},{16,80},{24,88},{32,96},{40,104},{48,112},{56,120},{... | collective-permute-start | bytes 884744 | tf_op jit(solution)/shard_map/ppermute | solution.py:219
  95.1 12.8 %copy-start.7 = (bf16[8,48,384]{2,1,0:T(8,128)(2,1)}, bf16[8,48,384]{2,1,0:T(8,128)(2,1)S(1)}, u32[]{:S(2)}) copy-start(bf16[8,48,384]{2,1,0:T(8,128)(2,1)S(1)} %collective-permute-done.7.refs_9_) | copy-start | bytes 884740
  95.1 9.9 %collective-permute-start = (bf16[8,48,384]{2,1,0:T(8,128)(2,1)S(1)}, bf16[8,48,384]{2,1,0:T(8,128)(2,1)S(1)}, u32[]{:S(2)}, u32[]{:S(2)}) collective-permute-start(bf16[8,48,384]{2,1,0:T(8,128)(2,1)S(1)} %get-tuple-element.58.refs_0_), channel_id=1, source_target_pairs={{0,8},{8,0},{16,24},{24,16},{32,40},{40,32},{48,56},{56,48},{64,72... | collective-permute-start | bytes 884744 | tf_op jit(solution)/shard_map/ppermute | solution.py:220
  95.9 12.0 %copy-start.8 = (bf16[8,48,384]{2,1,0:T(8,128)(2,1)}, bf16[8,48,384]{2,1,0:T(8,128)(2,1)S(1)}, u32[]{:S(2)}) copy-start(bf16[8,48,384]{2,1,0:T(8,128)(2,1)S(1)} %collective-permute-done.5.refs_6_) | copy-start | bytes 884740
  95.9 9.6 %collective-permute-start.13 = (bf16[8,48,384]{2,1,0:T(8,128)(2,1)S(1)}, bf16[8,48,384]{2,1,0:T(8,128)(2,1)S(1)}, u32[]{:S(2)}, u32[]{:S(2)}) collective-permute-start(bf16[8,48,384]{2,1,0:T(8,128)(2,1)S(1)} %collective-permute-done.12.refs_14_), channel_id=1, source_target_pairs={{0,8},{8,0},{16,24},{24,16},{32,40},{40,32},{48,56},{56,48},{64,72... | collective-permute-start | bytes 884744 | tf_op jit(solution)/shard_map/ppermute | solution.py:220
  102.6 5.3 %copy-start.9 = (bf16[8,48,384]{2,1,0:T(8,128)(2,1)}, bf16[8,48,384]{2,1,0:T(8,128)(2,1)S(1)}, u32[]{:S(2)}) copy-start(bf16[8,48,384]{2,1,0:T(8,128)(2,1)S(1)} %collective-permute-done.3.refs_4_) | copy-start | bytes 884740
  102.6 3.0 %collective-permute-start.11 = (bf16[8,48,384]{2,1,0:T(8,128)(2,1)S(1)}, bf16[8,48,384]{2,1,0:T(8,128)(2,1)S(1)}, u32[]{:S(2)}, u32[]{:S(2)}) collective-permute-start(bf16[8,48,384]{2,1,0:T(8,128)(2,1)S(1)} %collective-permute-done.10.refs_12_), channel_id=1, source_target_pairs={{0,8},{8,0},{16,24},{24,16},{32,40},{40,32},{48,56},{56,48},{64,72... | collective-permute-start | bytes 884744 | tf_op jit(solution)/shard_map/ppermute | solution.py:220
  105.0 2.9 %copy-start.10 = (bf16[8,48,384]{2,1,0:T(8,128)(2,1)}, bf16[8,48,384]{2,1,0:T(8,128)(2,1)S(1)}, u32[]{:S(2)}) copy-start(bf16[8,48,384]{2,1,0:T(8,128)(2,1)S(1)} %collective-permute-done.1.refs_2_) | copy-start | bytes 884740
  105.0 1.7 collective-permute-start.9
  105.0 2.9 %copy-start.11 = (bf16[8,48,384]{2,1,0:T(8,128)(2,1)}, bf16[8,48,384]{2,1,0:T(8,128)(2,1)S(1)}, u32[]{:S(2)}) copy-start(bf16[8,48,384]{2,1,0:T(8,128)(2,1)S(1)} %collective-permute-done.refs_1_) | copy-start | bytes 884740
  105.0 2.0 collective-permute-start.6
  105.5 2.4 %copy-start.12 = (bf16[8,48,384]{2,1,0:T(8,128)(2,1)}, bf16[8,48,384]{2,1,0:T(8,128)(2,1)S(1)}, u32[]{:S(2)}) copy-start(bf16[8,48,384]{2,1,0:T(8,128)(2,1)S(1)} %collective-permute-done.13.refs_15_) | copy-start | bytes 884740
  105.5 1.9 collective-permute-start.4
  105.6 2.3 %copy-start.13 = (bf16[8,48,384]{2,1,0:T(8,128)(2,1)}, bf16[8,48,384]{2,1,0:T(8,128)(2,1)S(1)}, u32[]{:S(2)}) copy-start(bf16[8,48,384]{2,1,0:T(8,128)(2,1)S(1)} %collective-permute-done.11.refs_13_) | copy-start | bytes 884740
  105.6 2.2 collective-permute-start.2
  106.7 1.3 copy-start.14
  107.0 1.0 copy-start.15
  107.4 0.7 copy-start.16
  108.1 0.7 copy-start.17
  127.0 3.9 %collective-permute-start.14 = (f32[8,512]{1,0:T(8,128)}, f32[8,512]{1,0:T(8,128)S(1)}, u32[]{:S(2)}, u32[]{:S(2)}) collective-permute-start(f32[8,512]{1,0:T(8,128)} %get-tuple-element.35), channel_id=1, source_target_pairs={{0,1},{1,0},{2,3},{3,2},{4,5},{5,4},{6,7},{7,6},{8,9},{9,8},{10,11... | collective-permute-start | bytes 49160 | tf_op jit(solution)/shard_map/ppermute | solution.py:368
  131.6 10.6 %copy-start.18 = (f32[8,512]{1,0:T(8,128)}, f32[8,512]{1,0:T(8,128)S(1)}, u32[]{:S(2)}) copy-start(f32[8,512]{1,0:T(8,128)S(1)} %add.20.refs_0_) | copy-start | bytes 49156
  131.6 6.5 %collective-permute-start.17 = (f32[8,512]{1,0:T(8,128)S(1)}, f32[8,512]{1,0:T(8,128)S(1)}, u32[]{:S(2)}, u32[]{:S(2)}) collective-permute-start(f32[8,512]{1,0:T(8,128)S(1)} %add.20.refs_0_), channel_id=1, source_target_pairs={{0,6},{1,7},{2,4},{3,5},{4,2},{5,3},{6,0},{7,1},{8,14},{9,15},{10,... | collective-permute-start | bytes 49160 | tf_op jit(solution)/shard_map/ppermute | solution.py:370
  134.0 7.6 %collective-permute-start.16 = (f32[8,512]{1,0:T(8,128)S(1)}, f32[8,512]{1,0:T(8,128)S(1)}, u32[]{:S(2)}, u32[]{:S(2)}) collective-permute-start(f32[8,512]{1,0:T(8,128)S(1)} %add.20.refs_0_), channel_id=1, source_target_pairs={{0,4},{1,5},{2,6},{3,7},{4,0},{5,1},{6,2},{7,3},{8,12},{9,13},{10,... | collective-permute-start | bytes 49160 | tf_op jit(solution)/shard_map/ppermute | solution.py:370
  137.5 4.7 %collective-permute-start.15 = (f32[8,512]{1,0:T(8,128)S(1)}, f32[8,512]{1,0:T(8,128)S(1)}, u32[]{:S(2)}, u32[]{:S(2)}) collective-permute-start(f32[8,512]{1,0:T(8,128)S(1)} %add.20.refs_0_), channel_id=1, source_target_pairs={{0,2},{1,3},{2,0},{3,1},{4,6},{5,7},{6,4},{7,5},{8,10},{9,11},{10,... | collective-permute-start | bytes 49160 | tf_op jit(solution)/shard_map/ppermute | solution.py:370
  138.1 4.1 %copy-start.19 = (f32[8,512]{1,0:T(8,128)}, f32[8,512]{1,0:T(8,128)S(1)}, u32[]{:S(2)}) copy-start(f32[8,512]{1,0:T(8,128)S(1)} %collective-permute-done.17.refs_3_) | copy-start | bytes 49156
  141.6 0.6 copy-start.20
  142.2 0.6 copy-start.21
  151.9 1.1 copy-start.2
  153.0 4.6 %collective-permute-start.19 = (bf16[512,768]{1,0:T(8,128)(2,1)S(1)}, bf16[512,768]{1,0:T(8,128)(2,1)S(1)}, u32[]{:S(2)}, u32[]{:S(2)}) collective-permute-start(bf16[512,768]{1,0:T(8,128)(2,1)S(1)} %copy-done.2), channel_id=1, source_target_pairs={{0,8},{8,0},{16,24},{24,16},{32,40},{40,32},{48,56},{56,48},{64,72... | collective-permute-start | bytes 2359304 | tf_op jit(solution)/shard_map/ppermute | solution.py:381
  157.7 0.9 copy-start.3
  203.0 18.1 %collective-permute-start.20 = (bf16[192,384]{1,0:T(8,128)(2,1)S(1)}, bf16[192,384]{1,0:T(8,128)(2,1)S(1)}, u32[]{:S(2)}, u32[]{:S(2)}) collective-permute-start(bf16[192,384]{1,0:T(8,128)(2,1)S(1)} %reduce_sum.12), channel_id=1, source_target_pairs={{0,0},{1,32},{2,64},{3,96},{4,128},{5,160},{6,192},{7,224},{8,4},{... | collective-permute-start | bytes 442376 | tf_op jit(solution)/shard_map/ppermute | solution.py:396
Sparse Core Ops, SparseCore 0:
  18.3 54.6 all-gather.1
  152.0 43.7 reduce-scatter.1

commit v2 on v1

--- a/solution.py
+++ b/solution.py
@@ -332,7 +332,7 @@
         [
             grad_spec, grad_spec,
             pl.BlockSpec((KEEP_MAX, block), lambda j, i: (0, i[4] * 4 + j)),
-            pl.BlockSpec((KEEP_MAX, block), lambda j, i: (0, j)),
+            pl.BlockSpec((KEEP_MAX, block), lambda j, i: (0, i[4] * 4 + j)),
         ],
         pl.BlockSpec((1, width, block), lambda j, i: (j, 0, 0)),
         jax.ShapeDtypeStruct((4, width, block), BF),
@@ -364,14 +364,13 @@
     mixed_all = lax.all_gather(mixed, "mp", axis=1, tiled=True)
     late, _ = lax.optimization_barrier((info, columns))
     grad_c = pick_rows(late, keep_count, keep_order, cotangent)
+    mixed_all, columns, grad_c = lax.optimization_barrier((mixed_all, columns, grad_c))
     projected, sums = project(info, mixed_all, columns, grad_c, gain)
     pair_sums = sums + lax.ppermute(sums, "mp", [(m, m ^ 1) for m in range(ranks)])
     all_sums = [pair_sums] + [
         lax.ppermute(pair_sums, "mp", [(m, m ^ s) for m in range(ranks)]) for s in range(2, ranks, 2)
     ]
-    half = mixed_all.shape[1] // 2
-    sent_mixed = lax.dynamic_slice_in_dim(mixed_all, (1 - image % 2) * half, half, 1)
-    other_mixed = lax.ppermute(sent_mixed, "dp", swap)
+    other_mixed = lax.ppermute(mixed_all, "dp", swap)
     all_sums, other_mixed = lax.optimization_barrier((all_sums, other_mixed))
     mixed_grad, grad_proj, normed_c = grad_rows(
         info, keep_count, projected, grad_c, gain, columns, all_sums, norm_gain.shape[0]
@@ -380,7 +379,6 @@
 
     other_grad = lax.ppermute(grad_proj, "dp", swap)
     normed = place_rows(info, keep_count, keep_order, normed_c)
-    other_grad, normed = lax.optimization_barrier((other_grad, normed))
     pair = outer(info, grad_proj, other_grad, mixed_all, other_mixed)
     width, depth = pair.shape[1], pair.shape[2]
     pair = pair.reshape(16, width // 4, depth)
@@ -396,7 +394,7 @@
     total = lax.ppermute(total, ("dp", "mp"), home)
 
     grads = attend_back(info, keep_count, keep_order, grad_mixed, query_c, key_c, value_c, weights)
-    total, grads = lax.optimization_barrier((total, grads))
+    total, grads, normed = lax.optimization_barrier((total, grads, normed))
     return (normed, *grads, total.astype(F32).T)
 
 

time: 230 us -> 197 us (0.86)
  waiting for transfers between devices: 81.6 us -> 25.6 us
  blocking collectives: 35.9 us -> 67.4 us
  starting transfers between devices: 30.2 us -> 22.1 us
    all_gather x1, waiting for transfers between devices: 46.3 us -> 0.01 us  [on_device(): mixed_all = lax.all_gather(mixed, 'mp', axis=1, tiled=True)]
    all_to_all x0 -> x1, blocking collectives: none -> 31.5 us  [gather_columns(): got = lax.all_to_all(cut, 'mp', split_axis=0, concat_axis=0, tiled=True)]
    ppermute x6, waiting for transfers between devices: 19.6 us -> 9.94 us  [gather_columns(): piece = own if s == 0 else lax.ppermute(own, 'dp', table)]
    all_to_all x1 -> x0, starting transfers between devices: 8.47 us -> none  [gather_columns(): got = lax.all_to_all(cut, 'mp', split_axis=0, concat_axis=0, tiled=True)]
    ppermute x1, waiting for transfers between devices: 7.75 us -> 3.2 us  [on_device(): total = lax.ppermute(total, ('dp', 'mp'), home)]
  transfers between devices with their start and end apart: 24 -> 23, of which waited for: 13 -> 11; matrix products, arithmetic and copies ran while one was open for 1% -> 1% of each run, Pallas kernels for 17% -> 20%
where the time goes in v2:
time: 197 us; the launch traced here: 195 us
  blocking collectives  67.4 us (34%)
  Pallas kernels  58.4 us (30%)
  waiting for transfers between devices  25.6 us (13%)
  starting transfers between devices  22.1 us (11%)
  between operations  14.3 us (7%)
  local copies, waits for them, and re-layouts  4.84 us (2%)
    pallas_call x9, Pallas kernels, call(): pl.pallas_call(kernel, grid_spec=pltpu.PrefetchScalarGridSpec(num_scalar_...  58.4 us
    all_to_all x1, blocking collectives, on_device(): lax.all_to_all(pair, 'dp', split_axis=0, concat_axis=0, tiled=True, axis_...  36 us
    all_to_all x1, blocking collectives, gather_columns(): got = lax.all_to_all(cut, 'mp', split_axis=0, concat_axis=0, tiled=True)  31.5 us
    ppermute x6, starting transfers between devices, gather_columns(): piece = own if s == 0 else lax.ppermute(own, 'dp', table)  12.2 us
    ppermute x6, waiting for transfers between devices, gather_columns(): piece = own if s == 0 else lax.ppermute(own, 'dp', table)  9.94 us
    ppermute x3, starting transfers between devices, on_device(): lax.ppermute(pair_sums, 'mp', [(m, m ^ s) for m in range(ranks)])  6.5 us
    ppermute x3, waiting for transfers between devices, on_device(): lax.ppermute(pair_sums, 'mp', [(m, m ^ s) for m in range(ranks)])  4.33 us
    ppermute x1, waiting for transfers between devices, on_device(): lax.ppermute(sums, 'mp', [(m, m ^ 1) for m in range(ranks)])  3.96 us
  transfers between devices with their start and end apart: 23, of which 11 were waited for; matrix products, arithmetic and copies ran while one was open for 1% of the time, Pallas kernels for 20%

profile of v2, /device:TPU:2, one launch (start us, length us, event | category | flops | bytes accessed | tf_op | source)
XLA Modules:
  0.0 194.5 jit_solution(8138418767989177906)
XLA Ops:
  7.3 0.7 stack.23.info
  7.9 2.8 %shard_map.119 = bf16[8,48,768]{2,1,0:T(8,128)(2,1)} custom-call(s32[5]{0:T(128)} %stack.23.info, bf16[384,6144]{1,0:T(8,128)(2,1)} %right.1, bf16[384,6144]{1,0:T(8,128)(2,1)} %right.1), custom_call_target="tpu_custom_call" | custom-call | bytes 10027008 | tf_op jit(solution)/shard_map/pallas_call | solution.py:25
  10.7 7.7 %shard_map.120 = (bf16[512,384]{1,0:T(8,128)(2,1)}, bf16[512,384]{1,0:T(8,128)(2,1)}, bf16[512,384]{1,0:T(8,128)(2,1)}, bf16[512,384]{1,0:T(8,128)(2,1)}, f32[3,512,512]{2,1,0:T(8,128)}) custom-call(s32[5]{0:T(128)} %stack.23.info, s32[32]{0:T(128)} %counts.9, s32[1,1024]{1,0:T(1,128)} %order.7, bf16[1,1024,384]{2,1,0:T(8,128)(2,1)} %query.1, ...), custom_call_target="tpu_custom_call" | custom-call | bytes 7081984 | tf_op jit(solution)/shard_map/pallas_call | solution.py:25
  18.5 31.5 %all_to_all.10 = bf16[8,48,768]{2,1,0:T(8,128)(2,1)S(1)} all-to-all(bf16[8,48,768]{2,1,0:T(8,128)(2,1)S(1)} %copy-done.1), channel_id=1, replica_groups=mesh['dp'=32,'mp'=8] {'mp'}, dimensions={0} | all-to-all | bytes 1179648 | tf_op jit(solution)/shard_map/all_to_all | solution.py:209
  49.9 0.1 fusion
  50.0 2.2 %collective-permute-start.12 = (bf16[8,48,384]{2,1,0:T(8,128)(2,1)S(1)}, bf16[8,48,384]{2,1,0:T(8,128)(2,1)S(1)}, u32[]{:S(2)}, u32[]{:S(2)}) collective-permute-start(bf16[8,48,384]{2,1,0:T(8,128)(2,1)S(1)} %get-tuple-element.61.refs_8_), channel_id=1, source_target_pairs={{0,32},{8,40},{16,48},{24,56},{32,0},{40,8},{48,16},{56,24},{64,96... | collective-permute-start | bytes 884744 | tf_op jit(solution)/shard_map/ppermute | solution.py:219
  52.2 1.4 collective-permute-start.10
  53.7 0.6 collective-permute-start.8
  54.3 3.3 %collective-permute-start.5 = (bf16[8,48,384]{2,1,0:T(8,128)(2,1)S(1)}, bf16[8,48,384]{2,1,0:T(8,128)(2,1)S(1)}, u32[]{:S(2)}, u32[]{:S(2)}) collective-permute-start(bf16[8,48,384]{2,1,0:T(8,128)(2,1)S(1)} %get-tuple-element.62.refs_0_), channel_id=1, source_target_pairs={{0,128},{8,136},{16,144},{24,152},{32,160},{40,168},{48,176},{56,1... | collective-permute-start | bytes 884744 | tf_op jit(solution)/shard_map/ppermute | solution.py:219
  57.5 3.1 %collective-permute-done.12.refs_14_ = bf16[8,48,384]{2,1,0:T(8,128)(2,1)S(1)} collective-permute-done((bf16[8,48,384]{2,1,0:T(8,128)(2,1)S(1)}, bf16[8,48,384]{2,1,0:T(8,128)(2,1)S(1)}, u32[]{:S(2)}, u32[]{:S(2)}) %collective-permute-start.12) | collective-permute-done | bytes 294944 | tf_op jit(solution)/shard_map/ppermute | solution.py:219
  60.6 3.2 %collective-permute-start.3 = (bf16[8,48,384]{2,1,0:T(8,128)(2,1)S(1)}, bf16[8,48,384]{2,1,0:T(8,128)(2,1)S(1)}, u32[]{:S(2)}, u32[]{:S(2)}) collective-permute-start(bf16[8,48,384]{2,1,0:T(8,128)(2,1)S(1)} %get-tuple-element.62.refs_0_), channel_id=1, source_target_pairs={{0,192},{8,200},{16,208},{24,216},{32,224},{40,232},{48,240},{56,2... | collective-permute-start | bytes 884744 | tf_op jit(solution)/shard_map/ppermute | solution.py:219
  63.8 1.5 collective-permute-start.1
  65.3 0.5 collective-permute-start.13
  65.8 0.1 collective-permute-start.11
  65.9 6.1 %collective-permute-done.3.refs_4_ = bf16[8,48,384]{2,1,0:T(8,128)(2,1)S(1)} collective-permute-done((bf16[8,48,384]{2,1,0:T(8,128)(2,1)S(1)}, bf16[8,48,384]{2,1,0:T(8,128)(2,1)S(1)}, u32[]{:S(2)}, u32[]{:S(2)}) %collective-permute-start.3) | collective-permute-done | bytes 294944 | tf_op jit(solution)/shard_map/ppermute | solution.py:219
  72.0 0.8 collective-permute-done.1.refs_2_
  72.8 0.5 collective-permute-start.4
  73.3 0.1 collective-permute-start.2
  73.4 0.2 collective-permute-done.9.refs_11_
  73.6 0.8 collective-permute-done.6.refs_7_
  74.4 0.4 collective-permute-done.4.refs_5_
  74.8 0.4 collective-permute-done.2.refs_3_
  75.4 0.2 copy-done.18
  75.5 0.7 copy-done.19
  76.2 4.8 %shard_map.121 = bf16[8,384,768]{2,1,0:T(8,128)(2,1)} custom-call(s32[5]{0:T(128)} %stack.23.info, bf16[8,48,384]{2,1,0:T(8,128)(2,1)} %copy-done.3, bf16[8,48,384]{2,1,0:T(8,128)(2,1)} %copy-done.13, bf16[8,48,384]{2,1,0:T(8,128)(2,1)} %copy-done.12, bf16[8,48,384]{2,1,0:T(8,128)(2,1)} %copy-done.19, bf16[8,48,384]{2,1,0:T(8,128)(2,1)} %copy-done.11, ...), custom_call_target="tpu_custom_call" | custom-call | bytes 9437184 | tf_op jit(solution)/shard_map/pallas_call | solution.py:25
  81.0 4.8 %shard_map.122.grad = bf16[512,768]{1,0:T(8,128)(2,1)} custom-call(s32[5]{0:T(128)} %stack.23.info, s32[32]{0:T(128)} %counts.9, s32[1,1024]{1,0:T(1,128)} %order.7, bf16[1,1024,768]{2,1,0:T(8,128)(2,1)} %tokens.1), custom_call_target="tpu_custom_call" | custom-call | bytes 2363392 | tf_op jit(solution)/shard_map/pallas_call | solution.py:25
  85.8 0.1 collective-permute-start.18
  85.9 0.6 reshape.20.gain
  86.5 8.5 %shard_map.123 = (f32[512,768]{1,0:T(8,128)}, f32[8,512]{1,0:T(8,128)}) custom-call(s32[5]{0:T(128)} %stack.23.info, bf16[512,3072]{1,0:T(8,128)(2,1)} %all-gather.2.cloned.1.call-done.mixed.own_mixed, bf16[3072,768]{1,0:T(8,128)(2,1)} %bitcast.10, bf16[512,768]{1,0:T(8,128)(2,1)} %shard_map.122.grad, bf16[1,6144]{1,0:T(2,128)(2,1)} %reshape.20.gain), custom_call_target="tpu_custom_call" | custom-call | bytes 10252288 | tf_op jit(solution)/shard_map/pallas_call | solution.py:25
  95.0 4.0 %collective-permute-done.14 = f32[8,512]{1,0:T(8,128)S(1)} collective-permute-done((f32[8,512]{1,0:T(8,128)}, f32[8,512]{1,0:T(8,128)S(1)}, u32[]{:S(2)}, u32[]{:S(2)}) %collective-permute-start.14) | collective-permute-done | bytes 16416 | tf_op jit(solution)/shard_map/ppermute | solution.py:369
  99.0 0.7 add.16.refs_0_
  99.7 3.2 %collective-permute-start.17 = (f32[8,512]{1,0:T(8,128)S(1)}, f32[8,512]{1,0:T(8,128)S(1)}, u32[]{:S(2)}, u32[]{:S(2)}) collective-permute-start(f32[8,512]{1,0:T(8,128)S(1)} %add.16.refs_0_), channel_id=1, source_target_pairs={{0,6},{1,7},{2,4},{3,5},{4,2},{5,3},{6,0},{7,1},{8,14},{9,15},{10,... | collective-permute-start | bytes 49160 | tf_op jit(solution)/shard_map/ppermute | solution.py:371
  102.9 0.5 collective-permute-start.16
  103.4 2.8 %collective-permute-start.15 = (f32[8,512]{1,0:T(8,128)S(1)}, f32[8,512]{1,0:T(8,128)S(1)}, u32[]{:S(2)}, u32[]{:S(2)}) collective-permute-start(f32[8,512]{1,0:T(8,128)S(1)} %add.16.refs_0_), channel_id=1, source_target_pairs={{0,2},{1,3},{2,0},{3,1},{4,6},{5,7},{6,4},{7,5},{8,10},{9,11},{10,... | collective-permute-start | bytes 49160 | tf_op jit(solution)/shard_map/ppermute | solution.py:371
  106.2 4.3 %collective-permute-done.16.refs_2_ = f32[8,512]{1,0:T(8,128)S(1)} collective-permute-done((f32[8,512]{1,0:T(8,128)S(1)}, f32[8,512]{1,0:T(8,128)S(1)}, u32[]{:S(2)}, u32[]{:S(2)}) %collective-permute-start.16) | collective-permute-done | bytes 16416 | tf_op jit(solution)/shard_map/ppermute | solution.py:371
  110.6 0.6 copy-done.22
  111.2 9.0 %shard_map.124 = (bf16[8,512,384]{2,1,0:T(8,128)(2,1)}, bf16[512,768]{1,0:T(8,128)(2,1)}, bf16[512,768]{1,0:T(8,128)(2,1)}) custom-call(s32[5]{0:T(128)} %stack.23.info, s32[32]{0:T(128)} %counts.9, f32[512,768]{1,0:T(8,128)} %get-tuple-element.39.projected, bf16[512,768]{1,0:T(8,128)(2,1)} %shard_map.122.grad, bf16[1,6144]{1,0:T(2,128)(2,1)} %reshape.20.gain, ...), custom_call_target="tpu_custom_call" | custom-call | bytes 11874304 | tf_op jit(solution)/shard_map/pallas_call | solution.py:25
  120.2 1.1 copy-done.4
  121.3 2.3 %collective-permute-done.19.other_grad = bf16[512,768]{1,0:T(8,128)(2,1)S(1)} collective-permute-done((bf16[512,768]{1,0:T(8,128)(2,1)S(1)}, bf16[512,768]{1,0:T(8,128)(2,1)S(1)}, u32[]{:S(2)}, u32[]{:S(2)}) %collective-permute-start.19) | collective-permute-done | bytes 786464 | tf_op jit(solution)/shard_map/ppermute | solution.py:380
  123.6 0.9 copy-done.5
  124.5 8.0 %shard_map.125 = bf16[4,768,384]{2,1,0:T(8,128)(2,1)} custom-call(s32[5]{0:T(128)} %stack.23.info, bf16[512,768]{1,0:T(8,128)(2,1)} %get-tuple-element.45.own_grad, bf16[512,768]{1,0:T(8,128)(2,1)} %copy-done.5, bf16[512,3072]{1,0:T(8,128)(2,1)} %all-gather.2.cloned.1.call-done.mixed.own_mixed, bf16[512,3072]{1,0:T(8,128)(2,1)} %copy-done), custom_call_target="tpu_custom_call" | custom-call | bytes 10223616 | tf_op jit(solution)/shard_map/pallas_call | solution.py:25
  132.5 36.0 %all_to_all.11 = bf16[16,192,384]{2,1,0:T(8,128)(2,1)S(1)} all-to-all(bf16[16,192,384]{2,1,0:T(8,128)(2,1)} %bitcast.12), channel_id=1, replica_groups={{0,16,32,48,64,80,96,112,128,144,160,176,192,208,224,240},{8,24,40,56,7..., dimensions={0} | all-to-all | bytes 4718592 | tf_op jit(solution)/shard_map/all_to_all | solution.py:386
  168.5 0.3 reduce_sum.12
  168.8 2.0 %collective-permute-start.20 = (bf16[192,384]{1,0:T(8,128)(2,1)S(1)}, bf16[192,384]{1,0:T(8,128)(2,1)S(1)}, u32[]{:S(2)}, u32[]{:S(2)}) collective-permute-start(bf16[192,384]{1,0:T(8,128)(2,1)S(1)} %reduce_sum.12), channel_id=1, source_target_pairs={{0,0},{1,32},{2,64},{3,96},{4,128},{5,160},{6,192},{7,224},{8,4},{... | collective-permute-start | bytes 442376 | tf_op jit(solution)/shard_map/ppermute | solution.py:394
  170.9 4.6 %shard_map.127 = bf16[1,1024,768]{2,1,0:T(8,128)(2,1)} custom-call(s32[5]{0:T(128)} %stack.23.info, s32[32]{0:T(128)} %counts.9, s32[1,1024]{1,0:T(1,128)} %order.7, bf16[512,768]{1,0:T(8,128)(2,1)} %get-tuple-element.55.rows), custom_call_target="tpu_custom_call" | custom-call | bytes 2363392 | tf_op jit(solution)/shard_map/pallas_call | solution.py:25
  175.5 8.2 %shard_map.126 = (bf16[1,1024,384]{2,1,0:T(8,128)(2,1)}, bf16[1,1024,384]{2,1,0:T(8,128)(2,1)}, bf16[1,1024,384]{2,1,0:T(8,128)(2,1)}) custom-call(s32[5]{0:T(128)} %stack.23.info, s32[32]{0:T(128)} %counts.9, s32[1,1024]{1,0:T(1,128)} %order.7, bf16[512,384]{1,0:T(8,128)(2,1)} %bitcast.13, bf16[512,384]{1,0:T(8,128)(2,1)} %get-tuple-element.48.query, ...), custom_call_target="tpu_custom_call" | custom-call | bytes 7081984 | tf_op jit(solution)/shard_map/pallas_call | solution.py:25
  183.7 3.2 %collective-permute-done.20 = bf16[192,384]{1,0:T(8,128)(2,1)S(1)} collective-permute-done((bf16[192,384]{1,0:T(8,128)(2,1)S(1)}, bf16[192,384]{1,0:T(8,128)(2,1)S(1)}, u32[]{:S(2)}, u32[]{:S(2)}) %collective-permute-start.20) | collective-permute-done | bytes 147488 | tf_op jit(solution)/shard_map/ppermute | solution.py:394
  186.9 0.7 convert_bitcast_fusion
  (67 shorter events, 0.3 us)
Async XLA Ops:
  7.2 78.6 %all-gather.2.cloned.1.call-start = ((), (), s32[]{:S(2)}) async-start(), calls=%async_computation.3 | async-start | bytes 3538944 | tf_op jit(solution)/shard_map/all_gather | solution.py:364
  10.7 7.8 %copy-start.1 = (bf16[8,48,768]{2,1,0:T(8,128)(2,1)S(1)}, bf16[8,48,768]{2,1,0:T(8,128)(2,1)}, u32[]{:S(2)}) copy-start(bf16[8,48,768]{2,1,0:T(8,128)(2,1)} %shard_map.119) | copy-start | bytes 1769476
  18.4 157.1 %reduce-scatter.2.cloned.1.call-start = ((), (), s32[]{:S(2)}) async-start(), calls=%async_computation.4 | async-start | bytes 3538944 | tf_op jit(solution)/shard_map/reduce_scatter | solution.py:378
  50.0 25.2 %copy-start.2 = (bf16[8,48,384]{2,1,0:T(8,128)(2,1)}, bf16[8,48,384]{2,1,0:T(8,128)(2,1)S(1)}, u32[]{:S(2)}) copy-start(bf16[8,48,384]{2,1,0:T(8,128)(2,1)S(1)} %get-tuple-element.61.refs_8_) | copy-start | bytes 884740
  50.0 25.2 %copy-start.3 = (bf16[8,48,384]{2,1,0:T(8,128)(2,1)}, bf16[8,48,384]{2,1,0:T(8,128)(2,1)S(1)}, u32[]{:S(2)}) copy-start(bf16[8,48,384]{2,1,0:T(8,128)(2,1)S(1)} %get-tuple-element.62.refs_0_) | copy-start | bytes 884740
  50.0 10.6 %collective-permute-start.12 = (bf16[8,48,384]{2,1,0:T(8,128)(2,1)S(1)}, bf16[8,48,384]{2,1,0:T(8,128)(2,1)S(1)}, u32[]{:S(2)}, u32[]{:S(2)}) collective-permute-start(bf16[8,48,384]{2,1,0:T(8,128)(2,1)S(1)} %get-tuple-element.61.refs_8_), channel_id=1, source_target_pairs={{0,32},{8,40},{16,48},{24,56},{32,0},{40,8},{48,16},{56,24},{64,96... | collective-permute-start | bytes 884744 | tf_op jit(solution)/shard_map/ppermute | solution.py:219
  52.2 11.5 %collective-permute-start.10 = (bf16[8,48,384]{2,1,0:T(8,128)(2,1)S(1)}, bf16[8,48,384]{2,1,0:T(8,128)(2,1)S(1)}, u32[]{:S(2)}, u32[]{:S(2)}) collective-permute-start(bf16[8,48,384]{2,1,0:T(8,128)(2,1)S(1)} %get-tuple-element.61.refs_8_), channel_id=1, source_target_pairs={{0,48},{8,56},{16,0},{24,8},{32,16},{40,24},{48,32},{56,40},{64,11... | collective-permute-start | bytes 884744 | tf_op jit(solution)/shard_map/ppermute | solution.py:219
  53.7 11.7 %collective-permute-start.8 = (bf16[8,48,384]{2,1,0:T(8,128)(2,1)S(1)}, bf16[8,48,384]{2,1,0:T(8,128)(2,1)S(1)}, u32[]{:S(2)}, u32[]{:S(2)}) collective-permute-start(bf16[8,48,384]{2,1,0:T(8,128)(2,1)S(1)} %get-tuple-element.61.refs_8_), channel_id=1, source_target_pairs={{0,16},{8,24},{16,32},{24,40},{32,48},{40,56},{48,0},{56,8},{64,80... | collective-permute-start | bytes 884744 | tf_op jit(solution)/shard_map/ppermute | solution.py:219
  54.3 11.1 %collective-permute-start.7 = (bf16[8,48,384]{2,1,0:T(8,128)(2,1)S(1)}, bf16[8,48,384]{2,1,0:T(8,128)(2,1)S(1)}, u32[]{:S(2)}, u32[]{:S(2)}) collective-permute-start(bf16[8,48,384]{2,1,0:T(8,128)(2,1)S(1)} %get-tuple-element.61.refs_8_), channel_id=1, source_target_pairs={{0,8},{8,0},{16,24},{24,16},{32,40},{40,32},{48,56},{56,48},{64,72... | collective-permute-start | bytes 884744 | tf_op jit(solution)/shard_map/ppermute | solution.py:220
  54.3 31.6 %copy-start.24 = (bf16[6144]{0:T(1024)(128)(2,1)S(1)}, bf16[6144]{0:T(1024)(128)(2,1)}, u32[]{:S(2)}) copy-start(bf16[6144]{0:T(1024)(128)(2,1)} %param.12) | copy-start | bytes 36868
  54.3 11.6 %collective-permute-start.5 = (bf16[8,48,384]{2,1,0:T(8,128)(2,1)S(1)}, bf16[8,48,384]{2,1,0:T(8,128)(2,1)S(1)}, u32[]{:S(2)}, u32[]{:S(2)}) collective-permute-start(bf16[8,48,384]{2,1,0:T(8,128)(2,1)S(1)} %get-tuple-element.62.refs_0_), channel_id=1, source_target_pairs={{0,128},{8,136},{16,144},{24,152},{32,160},{40,168},{48,176},{56,1... | collective-permute-start | bytes 884744 | tf_op jit(solution)/shard_map/ppermute | solution.py:219
  60.6 14.6 %copy-start.6 = (bf16[8,48,384]{2,1,0:T(8,128)(2,1)}, bf16[8,48,384]{2,1,0:T(8,128)(2,1)S(1)}, u32[]{:S(2)}) copy-start(bf16[8,48,384]{2,1,0:T(8,128)(2,1)S(1)} %collective-permute-done.12.refs_14_) | copy-start | bytes 884740
  60.6 11.4 %collective-permute-start.3 = (bf16[8,48,384]{2,1,0:T(8,128)(2,1)S(1)}, bf16[8,48,384]{2,1,0:T(8,128)(2,1)S(1)}, u32[]{:S(2)}, u32[]{:S(2)}) collective-permute-start(bf16[8,48,384]{2,1,0:T(8,128)(2,1)S(1)} %get-tuple-element.62.refs_0_), channel_id=1, source_target_pairs={{0,192},{8,200},{16,208},{24,216},{32,224},{40,232},{48,240},{56,2... | collective-permute-start | bytes 884744 | tf_op jit(solution)/shard_map/ppermute | solution.py:219
  63.8 11.5 %copy-start.7 = (bf16[8,48,384]{2,1,0:T(8,128)(2,1)}, bf16[8,48,384]{2,1,0:T(8,128)(2,1)S(1)}, u32[]{:S(2)}) copy-start(bf16[8,48,384]{2,1,0:T(8,128)(2,1)S(1)} %collective-permute-done.10.refs_12_) | copy-start | bytes 884740
  63.8 9.0 %collective-permute-start.1 = (bf16[8,48,384]{2,1,0:T(8,128)(2,1)S(1)}, bf16[8,48,384]{2,1,0:T(8,128)(2,1)S(1)}, u32[]{:S(2)}, u32[]{:S(2)}) collective-permute-start(bf16[8,48,384]{2,1,0:T(8,128)(2,1)S(1)} %get-tuple-element.62.refs_0_), channel_id=1, source_target_pairs={{0,64},{8,72},{16,80},{24,88},{32,96},{40,104},{48,112},{56,120},{... | collective-permute-start | bytes 884744 | tf_op jit(solution)/shard_map/ppermute | solution.py:219
  65.3 9.9 %copy-start.8 = (bf16[8,48,384]{2,1,0:T(8,128)(2,1)}, bf16[8,48,384]{2,1,0:T(8,128)(2,1)S(1)}, u32[]{:S(2)}) copy-start(bf16[8,48,384]{2,1,0:T(8,128)(2,1)S(1)} %collective-permute-done.8.refs_10_) | copy-start | bytes 884740
  65.3 7.5 %collective-permute-start = (bf16[8,48,384]{2,1,0:T(8,128)(2,1)S(1)}, bf16[8,48,384]{2,1,0:T(8,128)(2,1)S(1)}, u32[]{:S(2)}, u32[]{:S(2)}) collective-permute-start(bf16[8,48,384]{2,1,0:T(8,128)(2,1)S(1)} %get-tuple-element.62.refs_0_), channel_id=1, source_target_pairs={{0,8},{8,0},{16,24},{24,16},{32,40},{40,32},{48,56},{56,48},{64,72... | collective-permute-start | bytes 884744 | tf_op jit(solution)/shard_map/ppermute | solution.py:220
  65.3 9.9 %copy-start.9 = (bf16[8,48,384]{2,1,0:T(8,128)(2,1)}, bf16[8,48,384]{2,1,0:T(8,128)(2,1)S(1)}, u32[]{:S(2)}) copy-start(bf16[8,48,384]{2,1,0:T(8,128)(2,1)S(1)} %collective-permute-done.7.refs_9_) | copy-start | bytes 884740
  65.3 8.0 %collective-permute-start.13 = (bf16[8,48,384]{2,1,0:T(8,128)(2,1)S(1)}, bf16[8,48,384]{2,1,0:T(8,128)(2,1)S(1)}, u32[]{:S(2)}, u32[]{:S(2)}) collective-permute-start(bf16[8,48,384]{2,1,0:T(8,128)(2,1)S(1)} %collective-permute-done.12.refs_14_), channel_id=1, source_target_pairs={{0,8},{8,0},{16,24},{24,16},{32,40},{40,32},{48,56},{56,48},{64,72... | collective-permute-start | bytes 884744 | tf_op jit(solution)/shard_map/ppermute | solution.py:220
  65.8 9.4 %copy-start.10 = (bf16[8,48,384]{2,1,0:T(8,128)(2,1)}, bf16[8,48,384]{2,1,0:T(8,128)(2,1)S(1)}, u32[]{:S(2)}) copy-start(bf16[8,48,384]{2,1,0:T(8,128)(2,1)S(1)} %collective-permute-done.5.refs_6_) | copy-start | bytes 884740
  65.8 7.6 %collective-permute-start.11 = (bf16[8,48,384]{2,1,0:T(8,128)(2,1)S(1)}, bf16[8,48,384]{2,1,0:T(8,128)(2,1)S(1)}, u32[]{:S(2)}, u32[]{:S(2)}) collective-permute-start(bf16[8,48,384]{2,1,0:T(8,128)(2,1)S(1)} %collective-permute-done.10.refs_12_), channel_id=1, source_target_pairs={{0,8},{8,0},{16,24},{24,16},{32,40},{40,32},{48,56},{56,48},{64,72... | collective-permute-start | bytes 884744 | tf_op jit(solution)/shard_map/ppermute | solution.py:220
  72.0 3.3 %copy-start.11 = (bf16[8,48,384]{2,1,0:T(8,128)(2,1)}, bf16[8,48,384]{2,1,0:T(8,128)(2,1)S(1)}, u32[]{:S(2)}) copy-start(bf16[8,48,384]{2,1,0:T(8,128)(2,1)S(1)} %collective-permute-done.3.refs_4_) | copy-start | bytes 884740
  72.0 1.6 collective-permute-start.9
  72.8 2.5 %copy-start.12 = (bf16[8,48,384]{2,1,0:T(8,128)(2,1)}, bf16[8,48,384]{2,1,0:T(8,128)(2,1)S(1)}, u32[]{:S(2)}) copy-start(bf16[8,48,384]{2,1,0:T(8,128)(2,1)S(1)} %collective-permute-done.1.refs_2_) | copy-start | bytes 884740
  72.8 1.6 collective-permute-start.6
  72.8 2.5 %copy-start.13 = (bf16[8,48,384]{2,1,0:T(8,128)(2,1)}, bf16[8,48,384]{2,1,0:T(8,128)(2,1)S(1)}, u32[]{:S(2)}) copy-start(bf16[8,48,384]{2,1,0:T(8,128)(2,1)S(1)} %collective-permute-done.refs_1_) | copy-start | bytes 884740
  72.8 2.0 %collective-permute-start.4 = (bf16[8,48,384]{2,1,0:T(8,128)(2,1)S(1)}, bf16[8,48,384]{2,1,0:T(8,128)(2,1)S(1)}, u32[]{:S(2)}, u32[]{:S(2)}) collective-permute-start(bf16[8,48,384]{2,1,0:T(8,128)(2,1)S(1)} %collective-permute-done.3.refs_4_), channel_id=1, source_target_pairs={{0,8},{8,0},{16,24},{24,16},{32,40},{40,32},{48,56},{56,48},{64,72... | collective-permute-start | bytes 884744 | tf_op jit(solution)/shard_map/ppermute | solution.py:220
  73.3 2.0 %copy-start.14 = (bf16[8,48,384]{2,1,0:T(8,128)(2,1)}, bf16[8,48,384]{2,1,0:T(8,128)(2,1)S(1)}, u32[]{:S(2)}) copy-start(bf16[8,48,384]{2,1,0:T(8,128)(2,1)S(1)} %collective-permute-done.13.refs_15_) | copy-start | bytes 884740
  73.3 1.9 collective-permute-start.2
  73.4 1.9 copy-start.15
  73.6 1.7 copy-start.16
  74.4 1.0 copy-start.17
  74.8 0.7 copy-start.18
  75.5 0.7 copy-start.19
  85.8 24.8 %collective-permute-start.18 = (bf16[512,3072]{1,0:T(8,128)(2,1)}, bf16[512,3072]{1,0:T(8,128)(2,1)S(1)}, u32[]{:S(2)}, u32[]{:S(2)}) collective-permute-start(bf16[512,3072]{1,0:T(8,128)(2,1)} %all-gather.2.cloned.1.call-done.mixed.own_mixed), channel_id=1, source_target_pairs={{0,8},{8,0},{16,24},{24,16},{32,40},{40,32},{48,56},{56,48},{64,72... | collective-permute-start | bytes 9437192 | tf_op jit(solution)/shard_map/ppermute | solution.py:373
  95.0 4.0 %collective-permute-start.14 = (f32[8,512]{1,0:T(8,128)}, f32[8,512]{1,0:T(8,128)S(1)}, u32[]{:S(2)}, u32[]{:S(2)}) collective-permute-start(f32[8,512]{1,0:T(8,128)} %get-tuple-element.40), channel_id=1, source_target_pairs={{0,1},{1,0},{2,3},{3,2},{4,5},{5,4},{6,7},{7,6},{8,9},{9,8},{10,11... | collective-permute-start | bytes 49160 | tf_op jit(solution)/shard_map/ppermute | solution.py:369
  99.7 10.9 %copy-start.20 = (f32[8,512]{1,0:T(8,128)}, f32[8,512]{1,0:T(8,128)S(1)}, u32[]{:S(2)}) copy-start(f32[8,512]{1,0:T(8,128)S(1)} %add.16.refs_0_) | copy-start | bytes 49156
  99.7 6.5 %collective-permute-start.17 = (f32[8,512]{1,0:T(8,128)S(1)}, f32[8,512]{1,0:T(8,128)S(1)}, u32[]{:S(2)}, u32[]{:S(2)}) collective-permute-start(f32[8,512]{1,0:T(8,128)S(1)} %add.16.refs_0_), channel_id=1, source_target_pairs={{0,6},{1,7},{2,4},{3,5},{4,2},{5,3},{6,0},{7,1},{8,14},{9,15},{10,... | collective-permute-start | bytes 49160 | tf_op jit(solution)/shard_map/ppermute | solution.py:371
  102.9 7.6 %collective-permute-start.16 = (f32[8,512]{1,0:T(8,128)S(1)}, f32[8,512]{1,0:T(8,128)S(1)}, u32[]{:S(2)}, u32[]{:S(2)}) collective-permute-start(f32[8,512]{1,0:T(8,128)S(1)} %add.16.refs_0_), channel_id=1, source_target_pairs={{0,4},{1,5},{2,6},{3,7},{4,0},{5,1},{6,2},{7,3},{8,12},{9,13},{10,... | collective-permute-start | bytes 49160 | tf_op jit(solution)/shard_map/ppermute | solution.py:371
  103.4 7.2 %collective-permute-start.15 = (f32[8,512]{1,0:T(8,128)S(1)}, f32[8,512]{1,0:T(8,128)S(1)}, u32[]{:S(2)}, u32[]{:S(2)}) collective-permute-start(f32[8,512]{1,0:T(8,128)S(1)} %add.16.refs_0_), channel_id=1, source_target_pairs={{0,2},{1,3},{2,0},{3,1},{4,6},{5,7},{6,4},{7,5},{8,10},{9,11},{10,... | collective-permute-start | bytes 49160 | tf_op jit(solution)/shard_map/ppermute | solution.py:371
  106.2 4.4 %copy-start.21 = (f32[8,512]{1,0:T(8,128)}, f32[8,512]{1,0:T(8,128)S(1)}, u32[]{:S(2)}) copy-start(f32[8,512]{1,0:T(8,128)S(1)} %collective-permute-done.17.refs_3_) | copy-start | bytes 49156
  110.5 0.6 copy-start.22
  110.5 0.6 copy-start.23
  110.6 9.6 %copy-start = (bf16[512,3072]{1,0:T(8,128)(2,1)}, bf16[512,3072]{1,0:T(8,128)(2,1)S(1)}, u32[]{:S(2)}) copy-start(bf16[512,3072]{1,0:T(8,128)(2,1)S(1)} %collective-permute-done.18.other_mixed) | copy-start | bytes 9437188
  120.2 1.1 copy-start.4
  121.3 2.3 %collective-permute-start.19 = (bf16[512,768]{1,0:T(8,128)(2,1)S(1)}, bf16[512,768]{1,0:T(8,128)(2,1)S(1)}, u32[]{:S(2)}, u32[]{:S(2)}) collective-permute-start(bf16[512,768]{1,0:T(8,128)(2,1)S(1)} %copy-done.4), channel_id=1, source_target_pairs={{0,8},{8,0},{16,24},{24,16},{32,40},{40,32},{48,56},{56,48},{64,72... | collective-permute-start | bytes 2359304 | tf_op jit(solution)/shard_map/ppermute | solution.py:380
  123.6 0.9 copy-start.5
  168.8 18.1 %collective-permute-start.20 = (bf16[192,384]{1,0:T(8,128)(2,1)S(1)}, bf16[192,384]{1,0:T(8,128)(2,1)S(1)}, u32[]{:S(2)}, u32[]{:S(2)}) collective-permute-start(bf16[192,384]{1,0:T(8,128)(2,1)S(1)} %reduce_sum.12), channel_id=1, source_target_pairs={{0,0},{1,32},{2,64},{3,96},{4,128},{5,160},{6,192},{7,224},{8,4},{... | collective-permute-start | bytes 442376 | tf_op jit(solution)/shard_map/ppermute | solution.py:394
Sparse Core Ops, SparseCore 0:
  18.5 54.4 all-gather.1
  120.4 43.7 reduce-scatter.1

commit v3 on v2

--- a/solution.py
+++ b/solution.py
@@ -10,18 +10,14 @@
 HEAD_DIM = 128
 P_SIZE = 1024
 KEEP_MAX = 512
-VMEM_LIMIT = 56 * 1024 * 1024
+MIB = 1024 * 1024
 BF = jnp.bfloat16
 F32 = jnp.float32
 STEPS = (0, -1, 1, 2)
 
 
-def params():
-    return pltpu.CompilerParams(vmem_limit_bytes=VMEM_LIMIT)
-
-
-def call(kernel, grid, prefetched, in_specs, out_specs, out_shape, scratch, *operands, flops=0):
-    moved = sum(a.size * a.dtype.itemsize for a in jax.tree.leaves((operands, out_shape)))
+def call(kernel, grid, prefetched, in_specs, out_specs, out_shape, scratch, *operands, vmem):
+    moved = 2 * sum(a.size * a.dtype.itemsize for a in operands)
     return pl.pallas_call(
         kernel,
         grid_spec=pltpu.PrefetchScalarGridSpec(
@@ -32,9 +28,17 @@
             scratch_shapes=scratch,
         ),
         out_shape=out_shape,
-        compiler_params=params(),
-        cost_estimate=pl.CostEstimate(flops=flops, bytes_accessed=moved, transcendentals=0),
+        compiler_params=pltpu.CompilerParams(vmem_limit_bytes=vmem * MIB),
+        cost_estimate=pl.CostEstimate(flops=0, bytes_accessed=moved, transcendentals=0),
     )(*prefetched, *operands)
+
+
+def in_hbm(x):
+    return pltpu.with_memory_space_constraint(x, pltpu.HBM)
+
+
+def in_vmem(x):
+    return pltpu.with_memory_space_constraint(x, pltpu.VMEM)
 
 
 def to_column(row):
@@ -84,14 +88,14 @@
     heads = query.shape[2] // HEAD_DIM
     token_spec = pl.BlockSpec((1, P_SIZE, HEAD_DIM), lambda h, *_: (0, 0, h))
     row_spec = pl.BlockSpec((KEEP_MAX, HEAD_DIM), lambda h, *_: (0, h))
-    row_shape = jax.ShapeDtypeStruct((KEEP_MAX, heads * HEAD_DIM), BF)
+    row_shape = pltpu.HBM((KEEP_MAX, heads * HEAD_DIM), BF)
     return call(
         attend_kernel, (heads,), (info, counts),
         [pl.BlockSpec((1, P_SIZE), lambda h, *_: (0, 0)), token_spec, token_spec, token_spec],
         [row_spec] * 4 + [pl.BlockSpec((1, KEEP_MAX, KEEP_MAX), lambda h, *_: (h, 0, 0))],
-        [row_shape] * 4 + [jax.ShapeDtypeStruct((heads, KEEP_MAX, KEEP_MAX), F32)],
+        [row_shape] * 4 + [pltpu.HBM((heads, KEEP_MAX, KEEP_MAX), F32)],
         [pltpu.VMEM((KEEP_MAX, P_SIZE), BF)],
-        order, query, key, value,
+        in_hbm(order), in_hbm(query), in_hbm(key), in_hbm(value), vmem=20,
     )
 
 
@@ -125,7 +129,7 @@
         + [pl.BlockSpec((1, KEEP_MAX, KEEP_MAX), lambda h, *_: (h, 0, 0))],
         [token_spec] * 3, [token_shape] * 3,
         [pltpu.VMEM((P_SIZE, KEEP_MAX), BF)],
-        order, grad, query, key, value, weight,
+        in_hbm(order), in_hbm(grad), in_hbm(query), in_hbm(key), in_hbm(value), in_hbm(weight), vmem=20,
     )
 
 
@@ -145,7 +149,7 @@
         pl.BlockSpec((KEEP_MAX, 256), lambda j, *_: (0, j)),
         jax.ShapeDtypeStruct((KEEP_MAX, width), BF),
         [pltpu.VMEM((KEEP_MAX, P_SIZE), BF)],
-        order, tokens,
+        order, tokens, vmem=12,
     )
 
 
@@ -165,68 +169,92 @@
         pl.BlockSpec((1, P_SIZE, 256), lambda j, *_: (0, 0, j)),
         jax.ShapeDtypeStruct((1, P_SIZE, width), BF),
         [pltpu.VMEM((P_SIZE, KEEP_MAX), BF)],
-        order, rows,
-    )
-
-
-def cut_kernel(info, left, right, out):
-    ranks, _, width = out.shape
+        order, in_hbm(rows), vmem=12,
+    )
+
+
+def shift_of(y, core):
+    return y if core == 0 else (8 - y if y else 4)
+
+
+def cut_kernel(info, block, out):
+    half = out.shape[2]
+    out[0] = block[:, :half]
+    out[1] = block[:, half:]
+
+
+def fetch_columns(info, out_proj, chips):
+    rows, full = out_proj.shape
+    ranks = lax.axis_size("mp")
+    width, part = full // ranks, rows // 4
     half = width // 2
-    for m in range(ranks):
-        out[m, :, :half] = left[:, m * width:m * width + half]
-        out[m, :, half:] = right[:, m * width + half:(m + 1) * width]
+    parts = call(
+        cut_kernel, (1,), (info,),
+        [pl.BlockSpec((part, width), lambda _, i: (i[3], lax.rem(i[1] + ranks - i[5], ranks)))],
+        pl.BlockSpec((2, part, half), lambda _, i: (0, 0, 0)),
+        jax.ShapeDtypeStruct((2, part, half), BF), [],
+        in_hbm(out_proj), vmem=4,
+    )
+    table = [
+        (dp_index(y, x, c) * ranks + m, dp_index(y, x, c) * ranks + (m - shift_of(y, c)) % ranks)
+        for y, x, c in chips for m in range(ranks)
+    ]
+    got = lax.ppermute(parts, ("dp", "mp"), table)
+    return got[0], got[1]
+
+
+def spread_columns(parts, chips, after, beside):
+    swap = [(dp_index(y, x, c), dp_index(y, x, 1 - c)) for y, x, c in chips]
+    along = {
+        "y": {s: [(dp_index(y, x, c), dp_index(y - s, x, c)) for y, x, c in chips] for s in STEPS[1:]},
+        "x": {s: [(dp_index(y, x, c), dp_index(y, x - s, c)) for y, x, c in chips] for s in STEPS[1:]},
+    }
+    ways = (("y", "x"), ("x", "y"))
+    first = [
+        [part] + [lax.ppermute(part, "dp", along[way][s]) for s in STEPS[1:]]
+        for part, (way, _) in zip(parts, ways)
+    ]
+    fours = [jnp.stack(pieces) for pieces in first]
+    after, fours = lax.optimization_barrier((after, fours))
+    done = beside(after)
+    pieces = []
+    for four, (_, way) in zip(fours, ways):
+        for s in STEPS:
+            piece = four if s == 0 else lax.ppermute(four, "dp", along[way][s])
+            if way == "y" and s == STEPS[-1]:
+                piece, *done = lax.optimization_barrier((piece, *done))
+            pieces += [piece, lax.ppermute(piece, "dp", swap)]
+    return pieces, done
 
 
 def assemble_kernel(info, *refs):
     *pieces, out = refs
-    _, rows, width = out.shape
-    half, part = width // 2, rows // 8
+    ranks, rows, width = out.shape
+    half, part = width // 2, rows // 4
     for stream in range(2):
-        for at, step in enumerate(STEPS):
-            quarter = lax.rem(info[2 + stream] + 4 + step, 4)
+        for at, second in enumerate(STEPS):
             for core in range(2):
+                piece = pieces[(stream * 4 + at) * 2 + core]
                 side = info[4] if core == 0 else 1 - info[4]
-                start = pl.multiple_of((side * 4 + quarter) * part, 16)
-                piece = pieces[(stream * 4 + at) * 2 + core]
-                out[:, pl.ds(start, part), stream * half:(stream + 1) * half] = piece[...]
-
-
-def gather_columns(info, out_proj, chips):
-    rows, full = out_proj.shape
-    ranks = lax.axis_size("mp")
-    width = full // ranks
-    half, part = width // 2, rows // 8
-    cut = call(
-        cut_kernel, (1,), (info,),
-        [
-            pl.BlockSpec((part, full), lambda _, i: (i[4] * 4 + i[2], 0)),
-            pl.BlockSpec((part, full), lambda _, i: (i[4] * 4 + i[3], 0)),
-        ],
-        pl.BlockSpec((ranks, part, width), lambda _, i: (0, 0, 0)),
-        jax.ShapeDtypeStruct((ranks, part, width), BF), [],
-        out_proj, out_proj,
-    )
-    got = lax.all_to_all(cut, "mp", split_axis=0, concat_axis=0, tiled=True)
-    swap = [(dp_index(y, x, c), dp_index(y, x, 1 - c)) for y, x, c in chips]
-    pieces = []
-    for stream in range(2):
-        own = got[:, :, stream * half:(stream + 1) * half]
-        for s in STEPS:
-            if stream == 0:
-                table = [(dp_index(y, x, c), dp_index(y - s, x, c)) for y, x, c in chips]
-            else:
-                table = [(dp_index(y, x, c), dp_index(y, x - s, c)) for y, x, c in chips]
-            piece = own if s == 0 else lax.ppermute(own, "dp", table)
-            pieces += [piece, lax.ppermute(piece, "dp", swap)]
-    steps = 2
+                for j, first in enumerate(STEPS):
+                    dy, dx = (first, second) if stream == 0 else (second, first)
+                    y, x = lax.rem(info[2] + 4 + dy, 4), lax.rem(info[3] + 4 + dx, 4)
+                    shift = jnp.where(side == 0, y, jnp.where(y == 0, 4, 8 - y))
+                    start = pl.multiple_of(x * part, 16)
+                    out[lax.rem(info[1] + shift, ranks), pl.ds(start, part), stream * half:(stream + 1) * half] = piece[j]
+
+
+def assemble(info, pieces, ranks):
+    four, part, half = pieces[0].shape
+    rows, width = four * part, 2 * half
     whole = call(
-        assemble_kernel, (steps,), (info,),
-        [pl.BlockSpec((ranks // steps, part, half), lambda m, i: (m, 0, 0))] * 16,
-        pl.BlockSpec((ranks // steps, rows, width), lambda m, i: (m, 0, 0)),
-        jax.ShapeDtypeStruct((ranks, rows, width), BF), [],
-        *pieces,
-    )
-    return cut, whole.reshape(ranks * rows, width)
+        assemble_kernel, (1,), (info,),
+        [pl.BlockSpec((four, part, half), lambda _, i: (0, 0, 0))] * 16,
+        pl.BlockSpec((ranks, rows, width), lambda _, i: (0, 0, 0)),
+        pltpu.HBM((ranks, rows, width), BF), [],
+        *pieces, vmem=24,
+    )
+    return whole.reshape(ranks * rows, width)
 
 
 def project_kernel(info, mixed, weight, grad, gain, projected, sums):
@@ -265,51 +293,57 @@
         ],
         [pl.BlockSpec((KEEP_MAX, width), lambda k, i: (0, 0)), pl.BlockSpec((8, KEEP_MAX), lambda k, i: (0, 0))],
         [jax.ShapeDtypeStruct((KEEP_MAX, width), F32), jax.ShapeDtypeStruct((8, KEEP_MAX), F32)],
-        [], mixed, weight, grad, gain,
-    )
-
-
-def grad_kernel(full_width, info, counts, projected, grad, gain, weight, *refs):
-    *sums, out, grad_proj, normed = refs
-
-    @pl.when(pl.program_id(0) == 0)
-    def _():
-        total = sums[0][...]
-        for other in sums[1:]:
-            total = total + other[...]
-        total = jnp.concatenate([total, jnp.zeros((120, KEEP_MAX), F32)], axis=0)
-        table = jnp.transpose(total) / full_width
-        row_mean, row_square, first, cross = (table[:, at:at + 1] for at in range(4))
-        inv_std = lax.rsqrt(row_square - row_mean * row_mean + 1e-06)
-        second = (cross - row_mean * first) * inv_std
-        live = lax.broadcasted_iota(jnp.int32, (KEEP_MAX, 1), 0) < counts[info[0]]
-        gain_wide = gain[...].astype(F32)
-        centred = (projected[...] - row_mean) * inv_std
-        scaled = grad[...].astype(F32) * gain_wide
-        normed[...] = jnp.where(live, centred * gain_wide, 0.0).astype(BF)
-        grad_proj[...] = jnp.where(live, inv_std * (scaled - first - centred * second), 0.0).astype(BF)
-
+        [], in_hbm(mixed), in_hbm(weight), grad, gain, vmem=18,
+    )
+
+
+def grad_kernel(full_width, info, counts, projected, grad, gain, *refs):
+    *sums, grad_proj, normed = refs
+    total = sums[0][...]
+    for other in sums[1:]:
+        total = total + other[...]
+    total = jnp.concatenate([total, jnp.zeros((120, KEEP_MAX), F32)], axis=0)
+    table = jnp.transpose(total) / full_width
+    row_mean, row_square, first, cross = (table[:, at:at + 1] for at in range(4))
+    inv_std = lax.rsqrt(row_square - row_mean * row_mean + 1e-06)
+    second = (cross - row_mean * first) * inv_std
+    live = lax.broadcasted_iota(jnp.int32, (KEEP_MAX, 1), 0) < counts[info[0]]
+    gain_wide = gain[...].astype(F32)
+    centred = (projected[...] - row_mean) * inv_std
+    scaled = grad[...].astype(F32) * gain_wide
+    normed[...] = jnp.where(live, centred * gain_wide, 0.0).astype(BF)
+    grad_proj[...] = jnp.where(live, inv_std * (scaled - first - centred * second), 0.0).astype(BF)
+
+
+def grad_rows(info, counts, projected, grad, gain, sums, full_width):
+    width = projected.shape[1]
+    whole = pl.BlockSpec((KEEP_MAX, width), lambda k, *i: (0, 0))
+    shape = (KEEP_MAX, width)
+    return call(
+        functools.partial(grad_kernel, full_width), (1,), (info, counts),
+        [whole, whole, pl.BlockSpec((1, width), lambda k, i, c: (0, i[1]))]
+        + [pl.BlockSpec((8, KEEP_MAX), lambda k, *i: (0, 0))] * len(sums),
+        [whole, whole], [pltpu.VMEM(shape, BF), pltpu.HBM(shape, BF)],
+        [], projected, grad, gain, *sums, vmem=20,
+    )
+
+
+def back_kernel(grad_proj, weight, out):
     product = dot(grad_proj[...], weight[...], (1, 1)).astype(BF)
     half = out.shape[2]
     out[0] = product[:, :half]
     out[1] = product[:, half:]
 
 
-def grad_rows(info, counts, projected, grad, gain, weight, sums, full_width):
+def project_back(grad_proj, weight):
     depth, width = weight.shape
     block = 768
-    whole = pl.BlockSpec((KEEP_MAX, width), lambda k, *i: (0, 0))
-    rows_shape = jax.ShapeDtypeStruct((KEEP_MAX, width), BF)
-    return call(
-        functools.partial(grad_kernel, full_width), (depth // block,), (info, counts),
-        [
-            whole, whole,
-            pl.BlockSpec((1, width), lambda k, i, c: (0, i[1])),
-            pl.BlockSpec((block, width), lambda k, *i: (k, 0)),
-        ] + [pl.BlockSpec((8, KEEP_MAX), lambda k, *i: (0, 0))] * len(sums),
-        [pl.BlockSpec((2, KEEP_MAX, block // 2), lambda k, *i: (k, 0, 0)), whole, whole],
-        [jax.ShapeDtypeStruct((depth * 2 // block, KEEP_MAX, block // 2), BF), rows_shape, rows_shape],
-        [], projected, grad, gain, weight, *sums,
+    return call(
+        back_kernel, (depth // block,), (),
+        [pl.BlockSpec((KEEP_MAX, width), lambda k: (0, 0)), pl.BlockSpec((block, width), lambda k: (k, 0))],
+        pl.BlockSpec((2, KEEP_MAX, block // 2), lambda k: (k, 0, 0)),
+        pltpu.HBM((depth * 2 // block, KEEP_MAX, block // 2), BF),
+        [], grad_proj, in_vmem(weight), vmem=12,
     )
 
 
@@ -337,7 +371,7 @@
         pl.BlockSpec((1, width, block), lambda j, i: (j, 0, 0)),
         jax.ShapeDtypeStruct((4, width, block), BF),
         [pltpu.VMEM((width, 2 * KEEP_MAX), BF)],
-        own_grad, other_grad, mixed, other_mixed,
+        own_grad, other_grad, in_hbm(mixed), in_hbm(other_mixed), vmem=16,
     )
 
 
@@ -351,20 +385,24 @@
     ranks = lax.axis_size("mp")
     image = lax.axis_index("dp")
     rank = lax.axis_index("mp")
-    info = jnp.stack([image, rank, image // 8, (image // 2) % 4, image % 2]).astype(jnp.int32)
+    y_at, core = image // 8, image % 2
+    shift = jnp.where(core == 0, y_at, jnp.where(y_at == 0, 4, 8 - y_at))
+    info = jnp.stack([image, rank, y_at, (image // 2) % 4, core, shift]).astype(jnp.int32)
     chips = [(y, x, core) for y in range(4) for x in range(4) for core in range(2)]
     swap = [(dp_index(y, x, c), dp_index(y, x, 1 - c)) for y, x, c in chips]
-    gain = norm_gain.reshape(1, -1)
-
-    cut, columns = gather_columns(info, out_proj, chips)
-    early, _ = lax.optimization_barrier((info, cut))
+
     mixed, query_c, key_c, value_c, weights = attend(
-        early, keep_count, keep_order, query_heads, key_heads, value_heads
-    )
+        info, keep_count, keep_order, query_heads, key_heads, value_heads
+    )
+    later, mixed = lax.optimization_barrier((info, mixed))
+    parts = fetch_columns(later, out_proj, chips)
     mixed_all = lax.all_gather(mixed, "mp", axis=1, tiled=True)
-    late, _ = lax.optimization_barrier((info, columns))
-    grad_c = pick_rows(late, keep_count, keep_order, cotangent)
-    mixed_all, columns, grad_c = lax.optimization_barrier((mixed_all, columns, grad_c))
+    pieces, (grad_c, gain) = spread_columns(
+        parts, chips, info,
+        lambda after: (pick_rows(after, keep_count, keep_order, cotangent), norm_gain.reshape(1, -1)),
+    )
+    columns = assemble(info, pieces, ranks)
+    mixed_all, grad_c, columns = lax.optimization_barrier((mixed_all, grad_c, columns))
     projected, sums = project(info, mixed_all, columns, grad_c, gain)
     pair_sums = sums + lax.ppermute(sums, "mp", [(m, m ^ 1) for m in range(ranks)])
     all_sums = [pair_sums] + [
@@ -372,12 +410,14 @@
     ]
     other_mixed = lax.ppermute(mixed_all, "dp", swap)
     all_sums, other_mixed = lax.optimization_barrier((all_sums, other_mixed))
-    mixed_grad, grad_proj, normed_c = grad_rows(
-        info, keep_count, projected, grad_c, gain, columns, all_sums, norm_gain.shape[0]
-    )
+    grad_proj, normed_c = grad_rows(
+        info, keep_count, projected, grad_c, gain, all_sums, norm_gain.shape[0]
+    )
+    mixed_grad = project_back(grad_proj, columns)
+    other_grad = lax.ppermute(grad_proj, "dp", swap)
+    mixed_grad, other_grad = lax.optimization_barrier((mixed_grad, other_grad))
     grad_mixed = lax.psum_scatter(mixed_grad, "mp", scatter_dimension=0, tiled=True)[0]
 
-    other_grad = lax.ppermute(grad_proj, "dp", swap)
     normed = place_rows(info, keep_count, keep_order, normed_c)
     pair = outer(info, grad_proj, other_grad, mixed_all, other_mixed)
     width, depth = pair.shape[1], pair.shape[2]

time: 197 us -> 174 us (0.88)
  blocking collectives: 67.4 us -> 36.3 us
  starting transfers between devices: 22.1 us -> 43.5 us
  Pallas kernels: 58.4 us -> 47.9 us
  local copies, waits for them, and re-layouts: 4.84 us -> 0.82 us
  waiting for transfers between devices: 25.6 us -> 28 us
    all_to_all x1 -> x0, blocking collectives: 31.5 us -> none  [gather_columns(): got = lax.all_to_all(cut, 'mp', split_axis=0, concat_axis=0, tiled=True)]
    ppermute x14 -> x21, starting transfers between devices: 13.4 us -> 34.3 us  [the longest x6 23.8 us: spread_columns(): lax.ppermute(part, 'dp', along[way][s])]
    pallas_call x9 -> x10, Pallas kernels: 58.4 us -> 47.9 us  [call(): pl.pallas_call(kernel, grid_spec=pltpu.PrefetchScalarGridSpec(num_scalar_...]
    ppermute x14 -> x21, waiting for transfers between devices: 11.7 us -> 17.7 us  [the longest x6 12.1 us: spread_columns(): piece = four if s == 0 else lax.ppermute(four, 'dp', along[way][s])]
    unnamed x50 -> x16, local copies, waits for them, and re-layouts: 3.49 us -> 0.69 us
    ppermute x1, waiting for transfers between devices: 2.28 us -> 0.01 us  [on_device(): other_grad = lax.ppermute(grad_proj, 'dp', swap)]
  transfers between devices with their start and end apart: 23 -> 30, of which waited for: 11 -> 14; matrix products, arithmetic and copies ran while one was open for 1% -> 0% of each run, Pallas kernels for 20% -> 22%
where the time goes in v3:
time: 174 us; the launch traced here: 172 us
  Pallas kernels  47.9 us (28%)
  starting transfers between devices  43.5 us (25%)
  blocking collectives  36.3 us (21%)
  waiting for transfers between devices  28 us (16%)
  between operations  14.3 us (8%)
    pallas_call x10, Pallas kernels, call(): pl.pallas_call(kernel, grid_spec=pltpu.PrefetchScalarGridSpec(num_scalar_...  47.9 us
    all_to_all x1, blocking collectives, on_device(): lax.all_to_all(pair, 'dp', split_axis=0, concat_axis=0, tiled=True, axis_...  36.3 us
    ppermute x6, starting transfers between devices, spread_columns(): lax.ppermute(part, 'dp', along[way][s])  23.8 us
    ppermute x6, waiting for transfers between devices, spread_columns(): piece = four if s == 0 else lax.ppermute(four, 'dp', along[way][s])  12.1 us
    ppermute x6, starting transfers between devices, spread_columns(): piece = four if s == 0 else lax.ppermute(four, 'dp', along[way][s])  8.34 us
    ppermute x3, starting transfers between devices, on_device(): lax.ppermute(pair_sums, 'mp', [(m, m ^ s) for m in range(ranks)])  6.5 us
    ppermute x1, waiting for transfers between devices, on_device(): lax.ppermute(sums, 'mp', [(m, m ^ 1) for m in range(ranks)])  3.74 us
    ppermute x6, waiting for transfers between devices, spread_columns(): lax.ppermute(part, 'dp', along[way][s])  3.71 us
  transfers between devices with their start and end apart: 30, of which 14 were waited for; matrix products, arithmetic and copies ran while one was open for 0% of the time, Pallas kernels for 22%

profile of v3, /device:TPU:2, one launch (start us, length us, event | category | flops | bytes accessed | tf_op | source)
XLA Modules:
  0.0 172.0 jit_solution(14139357603071662851)
XLA Ops:
  7.3 0.7 copy-done.2
  8.0 7.4 %shard_map.119 = (bf16[512,384]{1,0:T(8,128)(2,1)}, bf16[512,384]{1,0:T(8,128)(2,1)}, bf16[512,384]{1,0:T(8,128)(2,1)}, bf16[512,384]{1,0:T(8,128)(2,1)}, f32[3,512,512]{2,1,0:T(8,128)}) custom-call(s32[6]{0:T(128)S(1)} %stack.51.info, s32[32]{0:T(128)S(1)} %copy-done.2, s32[1,1024]{1,0:T(1,128)} %order.7, bf16[1,1024,384]{2,1,0:T(8,128)(2,1)} %query.1, ...), custom_call_target="tpu_custom_call" | custom-call | bytes 4726784 | tf_op jit(solution)/shard_map/pallas_call | solution.py:21
  15.5 1.5 shard_map.120
  17.0 0.7 collective-permute-start
  17.7 15.1 %collective-permute-start.3 = (bf16[96,384]{1,0:T(8,128)(2,1)S(1)}, bf16[96,384]{1,0:T(8,128)(2,1)S(1)}, u32[]{:S(2)}, u32[]{:S(2)}) collective-permute-start(bf16[96,384]{1,0:T(8,128)(2,1)S(1)} %get-tuple-element.76), channel_id=1, source_target_pairs={{0,128},{8,136},{16,144},{24,152},{32,160},{40,168},{48,176},{56,1... | collective-permute-start | bytes 221192 | tf_op jit(solution)/shard_map/ppermute | solution.py:214
  32.8 3.8 %collective-permute-start.2 = (bf16[96,384]{1,0:T(8,128)(2,1)S(1)}, bf16[96,384]{1,0:T(8,128)(2,1)S(1)}, u32[]{:S(2)}, u32[]{:S(2)}) collective-permute-start(bf16[96,384]{1,0:T(8,128)(2,1)S(1)} %get-tuple-element.76), channel_id=1, source_target_pairs={{0,192},{8,200},{16,208},{24,216},{32,224},{40,232},{48,240},{56,2... | collective-permute-start | bytes 221192 | tf_op jit(solution)/shard_map/ppermute | solution.py:214
  36.6 0.8 collective-permute-start.1
  37.4 2.1 %collective-permute-start.6 = (bf16[96,384]{1,0:T(8,128)(2,1)S(1)}, bf16[96,384]{1,0:T(8,128)(2,1)S(1)}, u32[]{:S(2)}, u32[]{:S(2)}) collective-permute-start(bf16[96,384]{1,0:T(8,128)(2,1)S(1)} %get-tuple-element.77), channel_id=1, source_target_pairs={{0,32},{8,40},{16,48},{24,56},{32,0},{40,8},{48,16},{56,24},{64,96... | collective-permute-start | bytes 221192 | tf_op jit(solution)/shard_map/ppermute | solution.py:214
  39.5 1.4 collective-permute-start.5
  40.9 0.6 collective-permute-start.4
  41.5 0.7 collective-permute-done.1
  42.2 1.0 collective-permute-done.6
  43.3 0.8 collective-permute-done.5
  44.0 1.2 collective-permute-done.4
  45.3 2.5 %collective-permute-start.18 = (bf16[4,96,384]{2,1,0:T(8,128)(2,1)S(1)}, bf16[4,96,384]{2,1,0:T(8,128)(2,1)S(1)}, u32[]{:S(2)}, u32[]{:S(2)}) collective-permute-start(bf16[4,96,384]{2,1,0:T(8,128)(2,1)S(1)} %pad_maximum_fusion.1.refs_8_), channel_id=1, source_target_pairs={{0,192},{8,200},{16,208},{24,216},{32,224},{40,232},{48,240},{56,2... | collective-permute-start | bytes 884744 | tf_op jit(solution)/shard_map/ppermute | solution.py:223
  47.9 1.6 collective-permute-start.7
  49.5 1.2 collective-permute-start.13
  50.7 1.5 collective-permute-done.18.refs_12_
  52.2 2.4 %collective-permute-start.11 = (bf16[4,96,384]{2,1,0:T(8,128)(2,1)S(1)}, bf16[4,96,384]{2,1,0:T(8,128)(2,1)S(1)}, u32[]{:S(2)}, u32[]{:S(2)}) collective-permute-start(bf16[4,96,384]{2,1,0:T(8,128)(2,1)S(1)} %pad_maximum_fusion.refs_0_), channel_id=1, source_target_pairs={{0,48},{8,56},{16,0},{24,8},{32,16},{40,24},{48,32},{56,40},{64,11... | collective-permute-start | bytes 884744 | tf_op jit(solution)/shard_map/ppermute | solution.py:223
  54.6 7.5 %collective-permute-done.16.refs_10_ = bf16[4,96,384]{2,1,0:T(8,128)(2,1)S(1)} collective-permute-done((bf16[4,96,384]{2,1,0:T(8,128)(2,1)S(1)}, bf16[4,96,384]{2,1,0:T(8,128)(2,1)S(1)}, u32[]{:S(2)}, u32[]{:S(2)}) %collective-permute-start.16) | collective-permute-done | bytes 294944 | tf_op jit(solution)/shard_map/ppermute | solution.py:223
  62.1 0.6 collective-permute-start.9
  62.7 0.5 collective-permute-start.19
  63.2 2.4 %shard_map.121.grad = bf16[512,768]{1,0:T(8,128)(2,1)S(1)} custom-call(s32[6]{0:T(128)S(1)} %stack.51.info, s32[32]{0:T(128)S(1)} %copy-done.3, s32[1,1024]{1,0:T(1,128)S(1)} %copy-done.1, bf16[1,1024,768]{2,1,0:T(8,128)(2,1)S(1)} %copy-done), custom_call_target="tpu_custom_call" | custom-call | bytes 3153920 | tf_op jit(solution)/shard_map/pallas_call | solution.py:21
  65.6 0.4 collective-permute-start.17
  66.0 0.5 collective-permute-done.11.refs_4_
  66.5 2.7 %collective-permute-done.9.refs_2_ = bf16[4,96,384]{2,1,0:T(8,128)(2,1)S(1)} collective-permute-done((bf16[4,96,384]{2,1,0:T(8,128)(2,1)S(1)}, bf16[4,96,384]{2,1,0:T(8,128)(2,1)S(1)}, u32[]{:S(2)}, u32[]{:S(2)}) %collective-permute-start.9) | collective-permute-done | bytes 294944 | tf_op jit(solution)/shard_map/ppermute | solution.py:223
  69.2 0.5 collective-permute-start.10
  69.8 1.0 collective-permute-done.12.refs_5_
  70.7 0.4 collective-permute-done.10.refs_3_
  71.2 0.4 collective-permute-done.20.refs_15_
  71.6 3.2 %shard_map.122 = bf16[8,384,768]{2,1,0:T(8,128)(2,1)} custom-call(s32[6]{0:T(128)S(1)} %stack.51.info, bf16[4,96,384]{2,1,0:T(8,128)(2,1)S(1)} %pad_maximum_fusion.refs_0_, bf16[4,96,384]{2,1,0:T(8,128)(2,1)S(1)} %collective-permute-done.8.refs_1_, bf16[4,96,384]{2,1,0:T(8,128)(2,1)S(1)} %collective-permute-done.9.refs_2_, ...), custom_call_target="tpu_custom_call" | custom-call | bytes 9437184 | tf_op jit(solution)/shard_map/pallas_call | solution.py:21
  74.8 0.1 collective-permute-start.25
  74.9 7.6 %shard_map.123 = (f32[512,768]{1,0:T(8,128)S(1)}, f32[8,512]{1,0:T(8,128)S(1)}) custom-call(s32[6]{0:T(128)S(1)} %stack.51.info, bf16[512,3072]{1,0:T(8,128)(2,1)} %all-gather.2.cloned.1.call-done.mixed.own_mixed, bf16[3072,768]{1,0:T(8,128)(2,1)} %bitcast.21, bf16[512,768]{1,0:T(8,128)(2,1)S(1)} %shard_map.121.grad, bf16[1,6144]{1,0:T(2,128)(2,1)S(1)} %reshape.19.gain), custom_call_target="tpu_custom_call" | custom-call | bytes 17326080 | tf_op jit(solution)/shard_map/pallas_call | solution.py:21
  82.6 3.7 %collective-permute-done.21 = f32[8,512]{1,0:T(8,128)S(1)} collective-permute-done((f32[8,512]{1,0:T(8,128)S(1)}, f32[8,512]{1,0:T(8,128)S(1)}, u32[]{:S(2)}, u32[]{:S(2)}) %collective-permute-start.21) | collective-permute-done | bytes 16416 | tf_op jit(solution)/shard_map/ppermute | solution.py:407
  86.3 2.3 %collective-permute-start.24 = (f32[8,512]{1,0:T(8,128)S(1)}, f32[8,512]{1,0:T(8,128)S(1)}, u32[]{:S(2)}, u32[]{:S(2)}) collective-permute-start(f32[8,512]{1,0:T(8,128)S(1)} %add.16.refs_0_), channel_id=1, source_target_pairs={{0,6},{1,7},{2,4},{3,5},{4,2},{5,3},{6,0},{7,1},{8,14},{9,15},{10,... | collective-permute-start | bytes 49160 | tf_op jit(solution)/shard_map/ppermute | solution.py:409
  88.6 2.7 %collective-permute-start.23 = (f32[8,512]{1,0:T(8,128)S(1)}, f32[8,512]{1,0:T(8,128)S(1)}, u32[]{:S(2)}, u32[]{:S(2)}) collective-permute-start(f32[8,512]{1,0:T(8,128)S(1)} %add.16.refs_0_), channel_id=1, source_target_pairs={{0,4},{1,5},{2,6},{3,7},{4,0},{5,1},{6,2},{7,3},{8,12},{9,13},{10,... | collective-permute-start | bytes 49160 | tf_op jit(solution)/shard_map/ppermute | solution.py:409
  91.4 1.5 collective-permute-start.22
  92.8 3.4 %collective-permute-done.23.refs_2_ = f32[8,512]{1,0:T(8,128)S(1)} collective-permute-done((f32[8,512]{1,0:T(8,128)S(1)}, f32[8,512]{1,0:T(8,128)S(1)}, u32[]{:S(2)}, u32[]{:S(2)}) %collective-permute-start.23) | collective-permute-done | bytes 16416 | tf_op jit(solution)/shard_map/ppermute | solution.py:409
  96.3 2.7 %shard_map.124 = (bf16[512,768]{1,0:T(8,128)(2,1)S(1)}, bf16[512,768]{1,0:T(8,128)(2,1)}) custom-call(s32[6]{0:T(128)S(1)} %stack.51.info, s32[32]{0:T(128)S(1)} %copy-done.3, f32[512,768]{1,0:T(8,128)S(1)} %get-tuple-element.52.projected, bf16[512,768]{1,0:T(8,128)(2,1)S(1)} %shard_map.121.grad, bf16[1,6144]{1,0:T(2,128)(2,1)S(1)} %reshape.19.gain, ...), custom_call_target="tpu_custom_call" | custom-call | bytes 4874240 | tf_op jit(solution)/shard_map/pallas_call | solution.py:21
  99.1 4.3 %shard_map.125 = bf16[8,512,384]{2,1,0:T(8,128)(2,1)} custom-call(bf16[512,768]{1,0:T(8,128)(2,1)S(1)} %get-tuple-element.58.grad_proj.own_grad, bf16[3072,768]{1,0:T(8,128)(2,1)S(1)} %bitcast.24), custom_call_target="tpu_custom_call" | custom-call | bytes 11010048 | tf_op jit(solution)/shard_map/pallas_call | solution.py:21
  103.4 6.3 %shard_map.126 = bf16[4,768,384]{2,1,0:T(8,128)(2,1)S(1)} custom-call(s32[6]{0:T(128)S(1)} %stack.51.info, bf16[512,768]{1,0:T(8,128)(2,1)S(1)} %get-tuple-element.58.grad_proj.own_grad, bf16[512,768]{1,0:T(8,128)(2,1)S(1)} %collective-permute-done.26.other_grad, bf16[512,3072]{1,0:T(8,128)(2,1)} %all-gather.2.cloned.1.call-done.mixed.own_mixed, ...), custom_call_target="tpu_custom_call" | custom-call | bytes 15728640 | tf_op jit(solution)/shard_map/pallas_call | solution.py:21
  109.7 36.3 %all_to_all.5 = bf16[16,192,384]{2,1,0:T(8,128)(2,1)S(1)} all-to-all(bf16[16,192,384]{2,1,0:T(8,128)(2,1)S(1)} %bitcast.25), channel_id=1, replica_groups={{0,16,32,48,64,80,96,112,128,144,160,176,192,208,224,240},{8,24,40,56,7..., dimensions={0} | all-to-all | bytes 4718592 | tf_op jit(solution)/shard_map/all_to_all | solution.py:426
  146.0 0.3 reduce_sum.12
  146.4 2.4 %collective-permute-start.27 = (bf16[192,384]{1,0:T(8,128)(2,1)S(1)}, bf16[192,384]{1,0:T(8,128)(2,1)S(1)}, u32[]{:S(2)}, u32[]{:S(2)}) collective-permute-start(bf16[192,384]{1,0:T(8,128)(2,1)S(1)} %reduce_sum.12), channel_id=1, source_target_pairs={{0,0},{1,32},{2,64},{3,96},{4,128},{5,160},{6,192},{7,224},{8,4},{... | collective-permute-start | bytes 442376 | tf_op jit(solution)/shard_map/ppermute | solution.py:434
  148.7 4.5 %shard_map.128 = bf16[1,1024,768]{2,1,0:T(8,128)(2,1)} custom-call(s32[6]{0:T(128)S(1)} %stack.51.info, s32[32]{0:T(128)S(1)} %copy-done.3, s32[1,1024]{1,0:T(1,128)S(1)} %copy-done.1, bf16[512,768]{1,0:T(8,128)(2,1)} %get-tuple-element.69.rows), custom_call_target="tpu_custom_call" | custom-call | bytes 1581056 | tf_op jit(solution)/shard_map/pallas_call | solution.py:21
  153.3 8.1 %shard_map.127 = (bf16[1,1024,384]{2,1,0:T(8,128)(2,1)}, bf16[1,1024,384]{2,1,0:T(8,128)(2,1)}, bf16[1,1024,384]{2,1,0:T(8,128)(2,1)}) custom-call(s32[6]{0:T(128)S(1)} %stack.51.info, s32[32]{0:T(128)S(1)} %copy-done.3, s32[1,1024]{1,0:T(1,128)} %order.7, bf16[512,384]{1,0:T(8,128)(2,1)} %bitcast.26, bf16[512,384]{1,0:T(8,128)(2,1)} %get-tuple-element.62.query, ...), custom_call_target="tpu_custom_call" | custom-call | bytes 9445376 | tf_op jit(solution)/shard_map/pallas_call | solution.py:21
  161.4 3.1 %collective-permute-done.27 = bf16[192,384]{1,0:T(8,128)(2,1)S(1)} collective-permute-done((bf16[192,384]{1,0:T(8,128)(2,1)S(1)}, bf16[192,384]{1,0:T(8,128)(2,1)S(1)}, u32[]{:S(2)}, u32[]{:S(2)}) %collective-permute-start.27) | collective-permute-done | bytes 147488 | tf_op jit(solution)/shard_map/ppermute | solution.py:434
  164.5 0.7 convert_bitcast_fusion
  (50 shorter events, 0.6 us)
Async XLA Ops:
  7.2 67.6 %all-gather.2.cloned.1.call-start = ((), (), s32[]{:S(2)}) async-start(), calls=%async_computation.2 | async-start | bytes 3538944 | tf_op jit(solution)/shard_map/all_gather | solution.py:399
  7.3 0.7 copy-start.2
  15.4 47.8 %copy-start.5 = (bf16[6144]{0:T(1024)(128)(2,1)S(1)}, bf16[6144]{0:T(1024)(128)(2,1)}, u32[]{:S(2)}) copy-start(bf16[6144]{0:T(1024)(128)(2,1)} %param.12) | copy-start | bytes 36868
  15.4 47.8 %copy-start = (bf16[1,1024,768]{2,1,0:T(8,128)(2,1)S(1)}, bf16[1,1024,768]{2,1,0:T(8,128)(2,1)}, u32[]{:S(2)}) copy-start(bf16[1,1024,768]{2,1,0:T(8,128)(2,1)} %tokens.1) | copy-start | bytes 4718596
  15.5 47.8 %copy-start.1 = (s32[1,1024]{1,0:T(1,128)S(1)}, s32[1,1024]{1,0:T(1,128)}, u32[]{:S(2)}) copy-start(s32[1,1024]{1,0:T(1,128)} %order.7) | copy-start | bytes 12292
  15.5 47.8 %copy-start.3 = (s32[32]{0:T(128)S(1)}, s32[32]{0:T(128)}, u32[]{:S(2)}) copy-start(s32[32]{0:T(128)} %counts.9) | copy-start | bytes 388
  15.5 137.8 %reduce-scatter.2.cloned.1.call-start = ((), (), s32[]{:S(2)}) async-start(), calls=%async_computation.3 | async-start | bytes 3538944 | tf_op jit(solution)/shard_map/reduce_scatter | solution.py:419
  17.0 0.7 collective-permute-start
  17.7 23.2 %collective-permute-start.3 = (bf16[96,384]{1,0:T(8,128)(2,1)S(1)}, bf16[96,384]{1,0:T(8,128)(2,1)S(1)}, u32[]{:S(2)}, u32[]{:S(2)}) collective-permute-start(bf16[96,384]{1,0:T(8,128)(2,1)S(1)} %get-tuple-element.76), channel_id=1, source_target_pairs={{0,128},{8,136},{16,144},{24,152},{32,160},{40,168},{48,176},{56,1... | collective-permute-start | bytes 221192 | tf_op jit(solution)/shard_map/ppermute | solution.py:214
  32.8 8.7 %collective-permute-start.2 = (bf16[96,384]{1,0:T(8,128)(2,1)S(1)}, bf16[96,384]{1,0:T(8,128)(2,1)S(1)}, u32[]{:S(2)}, u32[]{:S(2)}) collective-permute-start(bf16[96,384]{1,0:T(8,128)(2,1)S(1)} %get-tuple-element.76), channel_id=1, source_target_pairs={{0,192},{8,200},{16,208},{24,216},{32,224},{40,232},{48,240},{56,2... | collective-permute-start | bytes 221192 | tf_op jit(solution)/shard_map/ppermute | solution.py:214
  36.6 5.6 %collective-permute-start.1 = (bf16[96,384]{1,0:T(8,128)(2,1)S(1)}, bf16[96,384]{1,0:T(8,128)(2,1)S(1)}, u32[]{:S(2)}, u32[]{:S(2)}) collective-permute-start(bf16[96,384]{1,0:T(8,128)(2,1)S(1)} %get-tuple-element.76), channel_id=1, source_target_pairs={{0,64},{8,72},{16,80},{24,88},{32,96},{40,104},{48,112},{56,120},{... | collective-permute-start | bytes 221192 | tf_op jit(solution)/shard_map/ppermute | solution.py:214
  37.4 5.9 %collective-permute-start.6 = (bf16[96,384]{1,0:T(8,128)(2,1)S(1)}, bf16[96,384]{1,0:T(8,128)(2,1)S(1)}, u32[]{:S(2)}, u32[]{:S(2)}) collective-permute-start(bf16[96,384]{1,0:T(8,128)(2,1)S(1)} %get-tuple-element.77), channel_id=1, source_target_pairs={{0,32},{8,40},{16,48},{24,56},{32,0},{40,8},{48,16},{56,24},{64,96... | collective-permute-start | bytes 221192 | tf_op jit(solution)/shard_map/ppermute | solution.py:214
  39.5 4.6 %collective-permute-start.5 = (bf16[96,384]{1,0:T(8,128)(2,1)S(1)}, bf16[96,384]{1,0:T(8,128)(2,1)S(1)}, u32[]{:S(2)}, u32[]{:S(2)}) collective-permute-start(bf16[96,384]{1,0:T(8,128)(2,1)S(1)} %get-tuple-element.77), channel_id=1, source_target_pairs={{0,48},{8,56},{16,0},{24,8},{32,16},{40,24},{48,32},{56,40},{64,11... | collective-permute-start | bytes 221192 | tf_op jit(solution)/shard_map/ppermute | solution.py:214
  40.9 4.4 %collective-permute-start.4 = (bf16[96,384]{1,0:T(8,128)(2,1)S(1)}, bf16[96,384]{1,0:T(8,128)(2,1)S(1)}, u32[]{:S(2)}, u32[]{:S(2)}) collective-permute-start(bf16[96,384]{1,0:T(8,128)(2,1)S(1)} %get-tuple-element.77), channel_id=1, source_target_pairs={{0,16},{8,24},{16,32},{24,40},{32,48},{40,56},{48,0},{56,8},{64,80... | collective-permute-start | bytes 221192 | tf_op jit(solution)/shard_map/ppermute | solution.py:214
  45.3 6.9 %collective-permute-start.18 = (bf16[4,96,384]{2,1,0:T(8,128)(2,1)S(1)}, bf16[4,96,384]{2,1,0:T(8,128)(2,1)S(1)}, u32[]{:S(2)}, u32[]{:S(2)}) collective-permute-start(bf16[4,96,384]{2,1,0:T(8,128)(2,1)S(1)} %pad_maximum_fusion.1.refs_8_), channel_id=1, source_target_pairs={{0,192},{8,200},{16,208},{24,216},{32,224},{40,232},{48,240},{56,2... | collective-permute-start | bytes 884744 | tf_op jit(solution)/shard_map/ppermute | solution.py:223
  47.9 14.2 %collective-permute-start.16 = (bf16[4,96,384]{2,1,0:T(8,128)(2,1)S(1)}, bf16[4,96,384]{2,1,0:T(8,128)(2,1)S(1)}, u32[]{:S(2)}, u32[]{:S(2)}) collective-permute-start(bf16[4,96,384]{2,1,0:T(8,128)(2,1)S(1)} %pad_maximum_fusion.1.refs_8_), channel_id=1, source_target_pairs={{0,64},{8,72},{16,80},{24,88},{32,96},{40,104},{48,112},{56,120},{... | collective-permute-start | bytes 884744 | tf_op jit(solution)/shard_map/ppermute | solution.py:223
  47.9 14.8 %collective-permute-start.15 = (bf16[4,96,384]{2,1,0:T(8,128)(2,1)S(1)}, bf16[4,96,384]{2,1,0:T(8,128)(2,1)S(1)}, u32[]{:S(2)}, u32[]{:S(2)}) collective-permute-start(bf16[4,96,384]{2,1,0:T(8,128)(2,1)S(1)} %pad_maximum_fusion.1.refs_8_), channel_id=1, source_target_pairs={{0,8},{8,0},{16,24},{24,16},{32,40},{40,32},{48,56},{56,48},{64,72... | collective-permute-start | bytes 884744 | tf_op jit(solution)/shard_map/ppermute | solution.py:226
  47.9 14.8 %collective-permute-start.7 = (bf16[4,96,384]{2,1,0:T(8,128)(2,1)S(1)}, bf16[4,96,384]{2,1,0:T(8,128)(2,1)S(1)}, u32[]{:S(2)}, u32[]{:S(2)}) collective-permute-start(bf16[4,96,384]{2,1,0:T(8,128)(2,1)S(1)} %pad_maximum_fusion.1.refs_8_), channel_id=1, source_target_pairs={{0,128},{8,136},{16,144},{24,152},{32,160},{40,168},{48,176},{56,1... | collective-permute-start | bytes 884744 | tf_op jit(solution)/shard_map/ppermute | solution.py:223
  49.5 16.1 %collective-permute-start.13 = (bf16[4,96,384]{2,1,0:T(8,128)(2,1)S(1)}, bf16[4,96,384]{2,1,0:T(8,128)(2,1)S(1)}, u32[]{:S(2)}, u32[]{:S(2)}) collective-permute-start(bf16[4,96,384]{2,1,0:T(8,128)(2,1)S(1)} %pad_maximum_fusion.refs_0_), channel_id=1, source_target_pairs={{0,32},{8,40},{16,48},{24,56},{32,0},{40,8},{48,16},{56,24},{64,96... | collective-permute-start | bytes 884744 | tf_op jit(solution)/shard_map/ppermute | solution.py:223
  52.2 14.2 %collective-permute-start.11 = (bf16[4,96,384]{2,1,0:T(8,128)(2,1)S(1)}, bf16[4,96,384]{2,1,0:T(8,128)(2,1)S(1)}, u32[]{:S(2)}, u32[]{:S(2)}) collective-permute-start(bf16[4,96,384]{2,1,0:T(8,128)(2,1)S(1)} %pad_maximum_fusion.refs_0_), channel_id=1, source_target_pairs={{0,48},{8,56},{16,0},{24,8},{32,16},{40,24},{48,32},{56,40},{64,11... | collective-permute-start | bytes 884744 | tf_op jit(solution)/shard_map/ppermute | solution.py:223
  62.1 7.1 %collective-permute-start.9 = (bf16[4,96,384]{2,1,0:T(8,128)(2,1)S(1)}, bf16[4,96,384]{2,1,0:T(8,128)(2,1)S(1)}, u32[]{:S(2)}, u32[]{:S(2)}) collective-permute-start(bf16[4,96,384]{2,1,0:T(8,128)(2,1)S(1)} %pad_maximum_fusion.refs_0_), channel_id=1, source_target_pairs={{0,16},{8,24},{16,32},{24,40},{32,48},{40,56},{48,0},{56,8},{64,80... | collective-permute-start | bytes 884744 | tf_op jit(solution)/shard_map/ppermute | solution.py:223
  62.7 6.5 %collective-permute-start.8 = (bf16[4,96,384]{2,1,0:T(8,128)(2,1)S(1)}, bf16[4,96,384]{2,1,0:T(8,128)(2,1)S(1)}, u32[]{:S(2)}, u32[]{:S(2)}) collective-permute-start(bf16[4,96,384]{2,1,0:T(8,128)(2,1)S(1)} %pad_maximum_fusion.refs_0_), channel_id=1, source_target_pairs={{0,8},{8,0},{16,24},{24,16},{32,40},{40,32},{48,56},{56,48},{64,72... | collective-permute-start | bytes 884744 | tf_op jit(solution)/shard_map/ppermute | solution.py:226
  62.7 7.0 %collective-permute-start.19 = (bf16[4,96,384]{2,1,0:T(8,128)(2,1)S(1)}, bf16[4,96,384]{2,1,0:T(8,128)(2,1)S(1)}, u32[]{:S(2)}, u32[]{:S(2)}) collective-permute-start(bf16[4,96,384]{2,1,0:T(8,128)(2,1)S(1)} %collective-permute-done.18.refs_12_), channel_id=1, source_target_pairs={{0,8},{8,0},{16,24},{24,16},{32,40},{40,32},{48,56},{56,48},{64,72... | collective-permute-start | bytes 884744 | tf_op jit(solution)/shard_map/ppermute | solution.py:226
  65.6 4.1 %collective-permute-start.17 = (bf16[4,96,384]{2,1,0:T(8,128)(2,1)S(1)}, bf16[4,96,384]{2,1,0:T(8,128)(2,1)S(1)}, u32[]{:S(2)}, u32[]{:S(2)}) collective-permute-start(bf16[4,96,384]{2,1,0:T(8,128)(2,1)S(1)} %collective-permute-done.16.refs_10_), channel_id=1, source_target_pairs={{0,8},{8,0},{16,24},{24,16},{32,40},{40,32},{48,56},{56,48},{64,72... | collective-permute-start | bytes 884744 | tf_op jit(solution)/shard_map/ppermute | solution.py:226
  66.5 3.3 %collective-permute-start.14 = (bf16[4,96,384]{2,1,0:T(8,128)(2,1)S(1)}, bf16[4,96,384]{2,1,0:T(8,128)(2,1)S(1)}, u32[]{:S(2)}, u32[]{:S(2)}) collective-permute-start(bf16[4,96,384]{2,1,0:T(8,128)(2,1)S(1)} %collective-permute-done.13.refs_6_), channel_id=1, source_target_pairs={{0,8},{8,0},{16,24},{24,16},{32,40},{40,32},{48,56},{56,48},{64,72... | collective-permute-start | bytes 884744 | tf_op jit(solution)/shard_map/ppermute | solution.py:226
  69.2 1.6 collective-permute-start.12
  69.2 2.0 %collective-permute-start.10 = (bf16[4,96,384]{2,1,0:T(8,128)(2,1)S(1)}, bf16[4,96,384]{2,1,0:T(8,128)(2,1)S(1)}, u32[]{:S(2)}, u32[]{:S(2)}) collective-permute-start(bf16[4,96,384]{2,1,0:T(8,128)(2,1)S(1)} %collective-permute-done.9.refs_2_), channel_id=1, source_target_pairs={{0,8},{8,0},{16,24},{24,16},{32,40},{40,32},{48,56},{56,48},{64,72... | collective-permute-start | bytes 884744 | tf_op jit(solution)/shard_map/ppermute | solution.py:226
  69.7 1.9 %collective-permute-start.20 = (bf16[4,96,384]{2,1,0:T(8,128)(2,1)S(1)}, bf16[4,96,384]{2,1,0:T(8,128)(2,1)S(1)}, u32[]{:S(2)}, u32[]{:S(2)}) collective-permute-start(bf16[4,96,384]{2,1,0:T(8,128)(2,1)S(1)} %collective-permute-done.7.refs_14_), channel_id=1, source_target_pairs={{0,8},{8,0},{16,24},{24,16},{32,40},{40,32},{48,56},{56,48},{64,72... | collective-permute-start | bytes 884744 | tf_op jit(solution)/shard_map/ppermute | solution.py:226
  74.8 24.2 %slice-start = ((s8[4718592]{0:T(1024)(128)(4,1)}), s8[4194304]{0:T(1024)(128)(4,1)S(1)}, s32[]{:S(2)}) async-start(s8[4718592]{0:T(1024)(128)(4,1)} %bitcast.22), calls=%async_computation.4 | async-start | bytes 8388608
  74.8 24.2 %slice-start.1 = ((s8[4718592]{0:T(1024)(128)(4,1)}), s8[524288]{0:T(1024)(128)(4,1)S(1)}, s32[]{:S(2)}) async-start(s8[4718592]{0:T(1024)(128)(4,1)} %bitcast.22), calls=%async_computation.5 | async-start | bytes 1048576
  74.8 21.5 %collective-permute-start.25 = (bf16[512,3072]{1,0:T(8,128)(2,1)}, bf16[512,3072]{1,0:T(8,128)(2,1)S(1)}, u32[]{:S(2)}, u32[]{:S(2)}) collective-permute-start(bf16[512,3072]{1,0:T(8,128)(2,1)} %all-gather.2.cloned.1.call-done.mixed.own_mixed), channel_id=1, source_target_pairs={{0,8},{8,0},{16,24},{24,16},{32,40},{40,32},{48,56},{56,48},{64,72... | collective-permute-start | bytes 9437192 | tf_op jit(solution)/shard_map/ppermute | solution.py:411
  82.5 3.8 %collective-permute-start.21 = (f32[8,512]{1,0:T(8,128)S(1)}, f32[8,512]{1,0:T(8,128)S(1)}, u32[]{:S(2)}, u32[]{:S(2)}) collective-permute-start(f32[8,512]{1,0:T(8,128)S(1)} %get-tuple-element.53), channel_id=1, source_target_pairs={{0,1},{1,0},{2,3},{3,2},{4,5},{5,4},{6,7},{7,6},{8,9},{9,8},{10,11... | collective-permute-start | bytes 49160 | tf_op jit(solution)/shard_map/ppermute | solution.py:407
  86.3 6.5 %collective-permute-start.24 = (f32[8,512]{1,0:T(8,128)S(1)}, f32[8,512]{1,0:T(8,128)S(1)}, u32[]{:S(2)}, u32[]{:S(2)}) collective-permute-start(f32[8,512]{1,0:T(8,128)S(1)} %add.16.refs_0_), channel_id=1, source_target_pairs={{0,6},{1,7},{2,4},{3,5},{4,2},{5,3},{6,0},{7,1},{8,14},{9,15},{10,... | collective-permute-start | bytes 49160 | tf_op jit(solution)/shard_map/ppermute | solution.py:409
  88.6 7.6 %collective-permute-start.23 = (f32[8,512]{1,0:T(8,128)S(1)}, f32[8,512]{1,0:T(8,128)S(1)}, u32[]{:S(2)}, u32[]{:S(2)}) collective-permute-start(f32[8,512]{1,0:T(8,128)S(1)} %add.16.refs_0_), channel_id=1, source_target_pairs={{0,4},{1,5},{2,6},{3,7},{4,0},{5,1},{6,2},{7,3},{8,12},{9,13},{10,... | collective-permute-start | bytes 49160 | tf_op jit(solution)/shard_map/ppermute | solution.py:409
  91.4 4.9 %collective-permute-start.22 = (f32[8,512]{1,0:T(8,128)S(1)}, f32[8,512]{1,0:T(8,128)S(1)}, u32[]{:S(2)}, u32[]{:S(2)}) collective-permute-start(f32[8,512]{1,0:T(8,128)S(1)} %add.16.refs_0_), channel_id=1, source_target_pairs={{0,2},{1,3},{2,0},{3,1},{4,6},{5,7},{6,4},{7,5},{8,10},{9,11},{10,... | collective-permute-start | bytes 49160 | tf_op jit(solution)/shard_map/ppermute | solution.py:409
  96.3 2.7 %copy-start.4 = (bf16[512,3072]{1,0:T(8,128)(2,1)}, bf16[512,3072]{1,0:T(8,128)(2,1)S(1)}, u32[]{:S(2)}) copy-start(bf16[512,3072]{1,0:T(8,128)(2,1)S(1)} %collective-permute-done.25.other_mixed) | copy-start | bytes 9437188
  99.0 4.3 %collective-permute-start.26 = (bf16[512,768]{1,0:T(8,128)(2,1)S(1)}, bf16[512,768]{1,0:T(8,128)(2,1)S(1)}, u32[]{:S(2)}, u32[]{:S(2)}) collective-permute-start(bf16[512,768]{1,0:T(8,128)(2,1)S(1)} %get-tuple-element.58.grad_proj.own_grad), channel_id=1, source_target_pairs={{0,8},{8,0},{16,24},{24,16},{32,40},{40,32},{48,56},{56,48},{64,72... | collective-permute-start | bytes 2359304 | tf_op jit(solution)/shard_map/ppermute | solution.py:417
  146.4 18.1 %collective-permute-start.27 = (bf16[192,384]{1,0:T(8,128)(2,1)S(1)}, bf16[192,384]{1,0:T(8,128)(2,1)S(1)}, u32[]{:S(2)}, u32[]{:S(2)}) collective-permute-start(bf16[192,384]{1,0:T(8,128)(2,1)S(1)} %reduce_sum.12), channel_id=1, source_target_pairs={{0,0},{1,32},{2,64},{3,96},{4,128},{5,160},{6,192},{7,224},{8,4},{... | collective-permute-start | bytes 442376 | tf_op jit(solution)/shard_map/ppermute | solution.py:434
Sparse Core Ops, SparseCore 0:
  15.5 48.3 all-gather.1
  103.5 44.8 reduce-scatter.1

commit v4 on v3

--- a/solution.py
+++ b/solution.py
@@ -99,7 +99,9 @@
     )
 
 
-def attend_back_kernel(info, counts, order, grad, query, key, value, weight, grad_q, grad_k, grad_v, place):
+def attend_back_kernel(
+    info, counts, order, grad, query, key, value, weight, normed, grad_q, grad_k, grad_v, normed_out, place
+):
     live = counts[info[0]]
 
     @pl.when(pl.program_id(0) == 0)
@@ -114,22 +116,27 @@
     dq = dot(d_scores, k, (1, 0)).astype(BF)
     dk = dot(d_scores, q, (0, 0)).astype(BF)
     dv = dot(w.astype(BF), g, (0, 0)).astype(BF)
-    out = dot(place[...], jnp.concatenate([dq, dk, dv], axis=1), (1, 0)).astype(BF)
-    grad_q[0], grad_k[0], grad_v[0] = out[:, :128], out[:, 128:256], out[:, 256:]
-
-
-def attend_back(info, counts, order, grad, query, key, value, weight):
+    rows = jnp.concatenate([dq, dk, dv, normed[...]], axis=1)
+    out = dot(place[...], rows, (1, 0)).astype(BF)
+    grad_q[0], grad_k[0], grad_v[0] = out[:, :128], out[:, 128:256], out[:, 256:384]
+    normed_out[0] = out[:, 384:]
+
+
+def attend_back(info, counts, order, grad, query, key, value, weight, normed):
     heads = query.shape[1] // HEAD_DIM
+    width = normed.shape[1]
     token_spec = pl.BlockSpec((1, P_SIZE, HEAD_DIM), lambda h, *_: (0, 0, h))
     row_spec = pl.BlockSpec((KEEP_MAX, HEAD_DIM), lambda h, *_: (0, h))
     token_shape = jax.ShapeDtypeStruct((1, P_SIZE, heads * HEAD_DIM), BF)
     return call(
         attend_back_kernel, (heads,), (info, counts),
         [pl.BlockSpec((1, P_SIZE), lambda h, *_: (0, 0))] + [row_spec] * 4
-        + [pl.BlockSpec((1, KEEP_MAX, KEEP_MAX), lambda h, *_: (h, 0, 0))],
-        [token_spec] * 3, [token_shape] * 3,
+        + [pl.BlockSpec((1, KEEP_MAX, KEEP_MAX), lambda h, *_: (h, 0, 0)),
+           pl.BlockSpec((KEEP_MAX, width // heads), lambda h, *_: (0, h))],
+        [token_spec] * 3 + [pl.BlockSpec((1, P_SIZE, width // heads), lambda h, *_: (0, 0, h))],
+        [token_shape] * 3 + [jax.ShapeDtypeStruct((1, P_SIZE, width), BF)],
         [pltpu.VMEM((P_SIZE, KEEP_MAX), BF)],
-        in_hbm(order), in_hbm(grad), in_hbm(query), in_hbm(key), in_hbm(value), in_hbm(weight), vmem=20,
+        in_hbm(order), in_hbm(grad), in_hbm(query), in_hbm(key), in_hbm(value), in_hbm(weight), in_hbm(normed), vmem=24,
     )
 
 
@@ -150,26 +157,6 @@
         jax.ShapeDtypeStruct((KEEP_MAX, width), BF),
         [pltpu.VMEM((KEEP_MAX, P_SIZE), BF)],
         order, tokens, vmem=12,
-    )
-
-
-def place_kernel(info, counts, order, rows, tokens, place):
-    @pl.when(pl.program_id(0) == 0)
-    def _():
-        place[...] = tokens_by_row(order, counts[info[0]])
-
-    tokens[0] = dot(place[...], rows[...], (1, 0)).astype(BF)
-
-
-def place_rows(info, counts, order, rows):
-    width = rows.shape[1]
-    return call(
-        place_kernel, (width // 256,), (info, counts),
-        [pl.BlockSpec((1, P_SIZE), lambda j, *_: (0, 0)), pl.BlockSpec((KEEP_MAX, 256), lambda j, *_: (0, j))],
-        pl.BlockSpec((1, P_SIZE, 256), lambda j, *_: (0, 0, j)),
-        jax.ShapeDtypeStruct((1, P_SIZE, width), BF),
-        [pltpu.VMEM((P_SIZE, KEEP_MAX), BF)],
-        order, in_hbm(rows), vmem=12,
     )
 
 
@@ -391,11 +378,11 @@
     chips = [(y, x, core) for y in range(4) for x in range(4) for core in range(2)]
     swap = [(dp_index(y, x, c), dp_index(y, x, 1 - c)) for y, x, c in chips]
 
+    parts = fetch_columns(info, out_proj, chips)
     mixed, query_c, key_c, value_c, weights = attend(
         info, keep_count, keep_order, query_heads, key_heads, value_heads
     )
-    later, mixed = lax.optimization_barrier((info, mixed))
-    parts = fetch_columns(later, out_proj, chips)
+    mixed, parts = lax.optimization_barrier((mixed, parts))
     mixed_all = lax.all_gather(mixed, "mp", axis=1, tiled=True)
     pieces, (grad_c, gain) = spread_columns(
         parts, chips, info,
@@ -404,10 +391,11 @@
     columns = assemble(info, pieces, ranks)
     mixed_all, grad_c, columns = lax.optimization_barrier((mixed_all, grad_c, columns))
     projected, sums = project(info, mixed_all, columns, grad_c, gain)
-    pair_sums = sums + lax.ppermute(sums, "mp", [(m, m ^ 1) for m in range(ranks)])
-    all_sums = [pair_sums] + [
-        lax.ppermute(pair_sums, "mp", [(m, m ^ s) for m in range(ranks)]) for s in range(2, ranks, 2)
-    ]
+    def swapped(values, bits):
+        return lax.ppermute(values, "mp", [(m, m ^ bits) for m in range(ranks)])
+
+    four_sums = sums + swapped(sums, 1) + swapped(sums, 3) + swapped(sums, 2)
+    all_sums = [four_sums, swapped(four_sums, 7)]
     other_mixed = lax.ppermute(mixed_all, "dp", swap)
     all_sums, other_mixed = lax.optimization_barrier((all_sums, other_mixed))
     grad_proj, normed_c = grad_rows(
@@ -418,7 +406,6 @@
     mixed_grad, other_grad = lax.optimization_barrier((mixed_grad, other_grad))
     grad_mixed = lax.psum_scatter(mixed_grad, "mp", scatter_dimension=0, tiled=True)[0]
 
-    normed = place_rows(info, keep_count, keep_order, normed_c)
     pair = outer(info, grad_proj, other_grad, mixed_all, other_mixed)
     width, depth = pair.shape[1], pair.shape[2]
     pair = pair.reshape(16, width // 4, depth)
@@ -433,8 +420,10 @@
     ]
     total = lax.ppermute(total, ("dp", "mp"), home)
 
-    grads = attend_back(info, keep_count, keep_order, grad_mixed, query_c, key_c, value_c, weights)
-    total, grads, normed = lax.optimization_barrier((total, grads, normed))
+    *grads, normed = attend_back(
+        info, keep_count, keep_order, grad_mixed, query_c, key_c, value_c, weights, normed_c
+    )
+    total, grads = lax.optimization_barrier((total, grads))
     return (normed, *grads, total.astype(F32).T)
 
 

time: 174 us -> 167 us (0.960); the launches traced: 172 us -> 167 us
  starting transfers between devices: 43.5 us -> 34.3 us
  waiting for transfers between devices: 28 us -> 34.9 us
  Pallas kernels: 47.9 us -> 44.5 us
    ppermute x6, starting transfers between devices: 23.8 us -> 17 us  [spread_columns(): lax.ppermute(part, 'dp', along[way][s])]
    ppermute x1, waiting for transfers between devices: 3.1 us -> 6.66 us  [on_device(): total = lax.ppermute(total, ('dp', 'mp'), home)]
    pallas_call x10 -> x9, Pallas kernels: 47.9 us -> 44.5 us  [call(): pl.pallas_call(kernel, grid_spec=pltpu.PrefetchScalarGridSpec(num_scalar_...]
    all_gather x1, waiting for transfers between devices: 0.01 us -> 3.32 us  [on_device(): mixed_all = lax.all_gather(mixed, 'mp', axis=1, tiled=True)]
  transfers between devices with their start and end apart: 30 -> 30, of which waited for: 14 -> 15; matrix products, arithmetic and copies ran while one was open for 0% -> 0% of each run, Pallas kernels for 22% -> 24%
where the time goes in v4:
time: 167 us
  Pallas kernels  44.5 us (27%)
  blocking collectives  37.7 us (23%)
  waiting for transfers between devices  34.9 us (21%)
  starting transfers between devices  34.3 us (21%)
  between operations  14.3 us (9%)
    pallas_call x9, Pallas kernels, call(): pl.pallas_call(kernel, grid_spec=pltpu.PrefetchScalarGridSpec(num_scalar_...  44.5 us
    all_to_all x1, blocking collectives, on_device(): lax.all_to_all(pair, 'dp', split_axis=0, concat_axis=0, tiled=True, axis_...  37.7 us
    ppermute x6, starting transfers between devices, spread_columns(): lax.ppermute(part, 'dp', along[way][s])  17 us
    ppermute x6, waiting for transfers between devices, spread_columns(): piece = four if s == 0 else lax.ppermute(four, 'dp', along[way][s])  12.2 us
    ppermute x6, starting transfers between devices, spread_columns(): piece = four if s == 0 else lax.ppermute(four, 'dp', along[way][s])  7.59 us
    ppermute x4, waiting for transfers between devices, swapped(): return lax.ppermute(values, 'mp', [(m, m ^ bits) for m in range(ranks)])  7.18 us
    ppermute x1, waiting for transfers between devices, on_device(): total = lax.ppermute(total, ('dp', 'mp'), home)  6.66 us
    ppermute x4, starting transfers between devices, swapped(): return lax.ppermute(values, 'mp', [(m, m ^ bits) for m in range(ranks)])  5.21 us
  transfers between devices with their start and end apart: 30, of which 15 were waited for; matrix products, arithmetic and copies ran while one was open for 0% of the time, Pallas kernels for 24%

profile of v4, /device:TPU:2, one launch (start us, length us, event | category | flops | bytes accessed | tf_op | source)
XLA Modules:
  0.0 167.0 jit_solution(16637284867799479559)
XLA Ops:
  7.4 1.5 shard_map.120
  8.9 0.8 collective-permute-start
  9.7 7.4 %shard_map.119 = (bf16[512,384]{1,0:T(8,128)(2,1)}, bf16[512,384]{1,0:T(8,128)(2,1)}, bf16[512,384]{1,0:T(8,128)(2,1)}, bf16[512,384]{1,0:T(8,128)(2,1)}, f32[3,512,512]{2,1,0:T(8,128)}) custom-call(s32[6]{0:T(128)S(1)} %stack.57.info, s32[32]{0:T(128)S(1)} %copy-done.2, s32[1,1024]{1,0:T(1,128)} %order.5, bf16[1,1024,384]{2,1,0:T(8,128)(2,1)} %query.1, ...), custom_call_target="tpu_custom_call" | custom-call | bytes 4726784 | tf_op jit(solution)/shard_map/pallas_call | solution.py:21
  17.2 10.8 %collective-permute-start.3 = (bf16[96,384]{1,0:T(8,128)(2,1)S(1)}, bf16[96,384]{1,0:T(8,128)(2,1)S(1)}, u32[]{:S(2)}, u32[]{:S(2)}) collective-permute-start(bf16[96,384]{1,0:T(8,128)(2,1)S(1)} %get-tuple-element.41), channel_id=1, source_target_pairs={{0,128},{8,136},{16,144},{24,152},{32,160},{40,168},{48,176},{56,1... | collective-permute-start | bytes 221192 | tf_op jit(solution)/shard_map/ppermute | solution.py:201
  28.0 0.6 collective-permute-start.2
  28.6 1.4 collective-permute-start.1
  30.1 2.1 %collective-permute-start.6 = (bf16[96,384]{1,0:T(8,128)(2,1)S(1)}, bf16[96,384]{1,0:T(8,128)(2,1)S(1)}, u32[]{:S(2)}, u32[]{:S(2)}) collective-permute-start(bf16[96,384]{1,0:T(8,128)(2,1)S(1)} %get-tuple-element.42), channel_id=1, source_target_pairs={{0,32},{8,40},{16,48},{24,56},{32,0},{40,8},{48,16},{56,24},{64,96... | collective-permute-start | bytes 221192 | tf_op jit(solution)/shard_map/ppermute | solution.py:201
  32.2 1.4 collective-permute-start.5
  33.6 0.6 collective-permute-start.4
  34.3 1.7 collective-permute-done.6
  35.9 0.8 collective-permute-done.5
  36.7 1.3 collective-permute-done.4
  38.0 1.9 %collective-permute-start.18 = (bf16[4,96,384]{2,1,0:T(8,128)(2,1)S(1)}, bf16[4,96,384]{2,1,0:T(8,128)(2,1)S(1)}, u32[]{:S(2)}, u32[]{:S(2)}) collective-permute-start(bf16[4,96,384]{2,1,0:T(8,128)(2,1)S(1)} %pad_maximum_fusion.1.refs_8_), channel_id=1, source_target_pairs={{0,192},{8,200},{16,208},{24,216},{32,224},{40,232},{48,240},{56,2... | collective-permute-start | bytes 884744 | tf_op jit(solution)/shard_map/ppermute | solution.py:210
  39.9 0.2 collective-permute-start.16
  40.1 1.3 collective-permute-start.7
  41.5 1.2 collective-permute-start.13
  42.7 2.2 %collective-permute-done.18.refs_12_ = bf16[4,96,384]{2,1,0:T(8,128)(2,1)S(1)} collective-permute-done((bf16[4,96,384]{2,1,0:T(8,128)(2,1)S(1)}, bf16[4,96,384]{2,1,0:T(8,128)(2,1)S(1)}, u32[]{:S(2)}, u32[]{:S(2)}) %collective-permute-start.18) | collective-permute-done | bytes 294944 | tf_op jit(solution)/shard_map/ppermute | solution.py:210
  44.8 2.4 %collective-permute-start.11 = (bf16[4,96,384]{2,1,0:T(8,128)(2,1)S(1)}, bf16[4,96,384]{2,1,0:T(8,128)(2,1)S(1)}, u32[]{:S(2)}, u32[]{:S(2)}) collective-permute-start(bf16[4,96,384]{2,1,0:T(8,128)(2,1)S(1)} %pad_maximum_fusion.refs_0_), channel_id=1, source_target_pairs={{0,48},{8,56},{16,0},{24,8},{32,16},{40,24},{48,32},{56,40},{64,11... | collective-permute-start | bytes 884744 | tf_op jit(solution)/shard_map/ppermute | solution.py:210
  47.2 7.0 %collective-permute-done.16.refs_10_ = bf16[4,96,384]{2,1,0:T(8,128)(2,1)S(1)} collective-permute-done((bf16[4,96,384]{2,1,0:T(8,128)(2,1)S(1)}, bf16[4,96,384]{2,1,0:T(8,128)(2,1)S(1)}, u32[]{:S(2)}, u32[]{:S(2)}) %collective-permute-start.16) | collective-permute-done | bytes 294944 | tf_op jit(solution)/shard_map/ppermute | solution.py:210
  54.2 0.6 collective-permute-start.9
  54.8 0.5 collective-permute-start.19
  55.3 2.4 %shard_map.121.grad = bf16[512,768]{1,0:T(8,128)(2,1)S(1)} custom-call(s32[6]{0:T(128)S(1)} %stack.57.info, s32[32]{0:T(128)S(1)} %copy-done.2, s32[1,1024]{1,0:T(1,128)S(1)} %copy-done.1, bf16[1,1024,768]{2,1,0:T(8,128)(2,1)S(1)} %copy-done), custom_call_target="tpu_custom_call" | custom-call | bytes 3153920 | tf_op jit(solution)/shard_map/pallas_call | solution.py:21
  57.7 0.4 collective-permute-start.17
  58.1 0.3 collective-permute-done.11.refs_4_
  58.6 2.7 %collective-permute-done.9.refs_2_ = bf16[4,96,384]{2,1,0:T(8,128)(2,1)S(1)} collective-permute-done((bf16[4,96,384]{2,1,0:T(8,128)(2,1)S(1)}, bf16[4,96,384]{2,1,0:T(8,128)(2,1)S(1)}, u32[]{:S(2)}, u32[]{:S(2)}) %collective-permute-start.9) | collective-permute-done | bytes 294944 | tf_op jit(solution)/shard_map/ppermute | solution.py:210
  61.2 0.5 collective-permute-start.10
  61.8 1.0 collective-permute-done.12.refs_5_
  62.8 0.4 collective-permute-done.10.refs_3_
  63.2 0.4 collective-permute-done.20.refs_15_
  63.7 3.2 %shard_map.122 = bf16[8,384,768]{2,1,0:T(8,128)(2,1)} custom-call(s32[6]{0:T(128)S(1)} %stack.57.info, bf16[4,96,384]{2,1,0:T(8,128)(2,1)S(1)} %pad_maximum_fusion.refs_0_, bf16[4,96,384]{2,1,0:T(8,128)(2,1)S(1)} %collective-permute-done.8.refs_1_, bf16[4,96,384]{2,1,0:T(8,128)(2,1)S(1)} %collective-permute-done.9.refs_2_, ...), custom_call_target="tpu_custom_call" | custom-call | bytes 9437184 | tf_op jit(solution)/shard_map/pallas_call | solution.py:21
  66.9 3.3 %all-gather.2.cloned.1.call-done.mixed.own_mixed = bf16[512,3072]{1,0:T(8,128)(2,1)} async-done(((bf16[512,384]{1,0:T(8,128)(2,1)}), bf16[512,3072]{1,0:T(8,128)(2,1)}) %all-gather.2.cloned.1.call-update) | async-done | bytes 3145744 | tf_op jit(solution)/shard_map/all_gather | solution.py:386
  70.2 7.4 %shard_map.123 = (f32[512,768]{1,0:T(8,128)S(1)}, f32[8,512]{1,0:T(8,128)S(1)}) custom-call(s32[6]{0:T(128)S(1)} %stack.57.info, bf16[512,3072]{1,0:T(8,128)(2,1)} %all-gather.2.cloned.1.call-done.mixed.own_mixed, bf16[3072,768]{1,0:T(8,128)(2,1)} %bitcast.23, bf16[512,768]{1,0:T(8,128)(2,1)S(1)} %shard_map.121.grad, bf16[1,6144]{1,0:T(2,128)(2,1)S(1)} %reshape.19.gain), custom_call_target="tpu_custom_call" | custom-call | bytes 17326080 | tf_op jit(solution)/shard_map/pallas_call | solution.py:21
  77.6 1.8 %collective-permute-start.23 = (f32[8,512]{1,0:T(8,128)S(1)}, f32[8,512]{1,0:T(8,128)S(1)}, u32[]{:S(2)}, u32[]{:S(2)}) collective-permute-start(f32[8,512]{1,0:T(8,128)S(1)} %get-tuple-element.53), channel_id=1, source_target_pairs={{0,2},{1,3},{2,0},{3,1},{4,6},{5,7},{6,4},{7,5},{8,10},{9,11},{10,... | collective-permute-start | bytes 49160 | tf_op jit(solution)/shard_map/ppermute | solution.py:395
  79.4 1.5 collective-permute-start.22
  80.8 0.3 collective-permute-start.21
  81.1 1.1 collective-permute-done.23
  82.3 2.6 %collective-permute-done.22 = f32[8,512]{1,0:T(8,128)S(1)} collective-permute-done((f32[8,512]{1,0:T(8,128)S(1)}, f32[8,512]{1,0:T(8,128)S(1)}, u32[]{:S(2)}, u32[]{:S(2)}) %collective-permute-start.22) | collective-permute-done | bytes 16416 | tf_op jit(solution)/shard_map/ppermute | solution.py:395
  84.9 1.6 collective-permute-start.24
  86.6 3.4 %collective-permute-done.24.refs_1_ = f32[8,512]{1,0:T(8,128)S(1)} collective-permute-done((f32[8,512]{1,0:T(8,128)S(1)}, f32[8,512]{1,0:T(8,128)S(1)}, u32[]{:S(2)}, u32[]{:S(2)}) %collective-permute-start.24) | collective-permute-done | bytes 16416 | tf_op jit(solution)/shard_map/ppermute | solution.py:395
  90.0 2.7 %shard_map.124 = (bf16[512,768]{1,0:T(8,128)(2,1)S(1)}, bf16[512,768]{1,0:T(8,128)(2,1)}) custom-call(s32[6]{0:T(128)S(1)} %stack.57.info, s32[32]{0:T(128)S(1)} %copy-done.2, f32[512,768]{1,0:T(8,128)S(1)} %get-tuple-element.52.projected, bf16[512,768]{1,0:T(8,128)(2,1)S(1)} %shard_map.121.grad, bf16[1,6144]{1,0:T(2,128)(2,1)S(1)} %reshape.19.gain, ...), custom_call_target="tpu_custom_call" | custom-call | bytes 4808704 | tf_op jit(solution)/shard_map/pallas_call | solution.py:21
  92.7 4.3 %shard_map.125 = bf16[8,512,384]{2,1,0:T(8,128)(2,1)} custom-call(bf16[512,768]{1,0:T(8,128)(2,1)S(1)} %get-tuple-element.56.grad_proj.own_grad, bf16[3072,768]{1,0:T(8,128)(2,1)S(1)} %bitcast.26), custom_call_target="tpu_custom_call" | custom-call | bytes 11010048 | tf_op jit(solution)/shard_map/pallas_call | solution.py:21
  97.0 6.3 %shard_map.127 = bf16[4,768,384]{2,1,0:T(8,128)(2,1)S(1)} custom-call(s32[6]{0:T(128)S(1)} %stack.57.info, bf16[512,768]{1,0:T(8,128)(2,1)S(1)} %get-tuple-element.56.grad_proj.own_grad, bf16[512,768]{1,0:T(8,128)(2,1)S(1)} %collective-permute-done.26.other_grad, bf16[512,3072]{1,0:T(8,128)(2,1)} %all-gather.2.cloned.1.call-done.mixed.own_mixed, ...), custom_call_target="tpu_custom_call" | custom-call | bytes 15728640 | tf_op jit(solution)/shard_map/pallas_call | solution.py:21
  103.3 37.7 %all_to_all.5 = bf16[16,192,384]{2,1,0:T(8,128)(2,1)S(1)} all-to-all(bf16[16,192,384]{2,1,0:T(8,128)(2,1)S(1)} %bitcast.27), channel_id=1, replica_groups={{0,16,32,48,64,80,96,112,128,144,160,176,192,208,224,240},{8,24,40,56,7..., dimensions={0} | all-to-all | bytes 4718592 | tf_op jit(solution)/shard_map/all_to_all | solution.py:413
  141.0 0.3 reduce_sum.12
  141.3 2.0 %collective-permute-start.27 = (bf16[192,384]{1,0:T(8,128)(2,1)S(1)}, bf16[192,384]{1,0:T(8,128)(2,1)S(1)}, u32[]{:S(2)}, u32[]{:S(2)}) collective-permute-start(bf16[192,384]{1,0:T(8,128)(2,1)S(1)} %reduce_sum.12), channel_id=1, source_target_pairs={{0,0},{1,32},{2,64},{3,96},{4,128},{5,160},{6,192},{7,224},{8,4},{... | collective-permute-start | bytes 442376 | tf_op jit(solution)/shard_map/ppermute | solution.py:421
  143.4 9.4 %shard_map.126 = (bf16[1,1024,384]{2,1,0:T(8,128)(2,1)}, bf16[1,1024,384]{2,1,0:T(8,128)(2,1)}, bf16[1,1024,384]{2,1,0:T(8,128)(2,1)}, bf16[1,1024,768]{2,1,0:T(8,128)(2,1)}) custom-call(s32[6]{0:T(128)S(1)} %stack.57.info, s32[32]{0:T(128)S(1)} %copy-done.2, s32[1,1024]{1,0:T(1,128)} %order.5, bf16[512,384]{1,0:T(8,128)(2,1)} %bitcast.28, ...), custom_call_target="tpu_custom_call" | custom-call | bytes 11018240 | tf_op jit(solution)/shard_map/pallas_call | solution.py:21
  152.8 6.7 %collective-permute-done.27 = bf16[192,384]{1,0:T(8,128)(2,1)S(1)} collective-permute-done((bf16[192,384]{1,0:T(8,128)(2,1)S(1)}, bf16[192,384]{1,0:T(8,128)(2,1)S(1)}, u32[]{:S(2)}, u32[]{:S(2)}) %collective-permute-start.27) | collective-permute-done | bytes 147488 | tf_op jit(solution)/shard_map/ppermute | solution.py:421
  159.4 0.7 convert_bitcast_fusion
  (47 shorter events, 0.7 us)
Async XLA Ops:
  7.2 2.5 %copy-start.2 = (s32[32]{0:T(128)S(1)}, s32[32]{0:T(128)}, u32[]{:S(2)}) copy-start(s32[32]{0:T(128)} %counts.7) | copy-start | bytes 388
  7.2 63.0 %all-gather.2.cloned.1.call-start = ((), (), s32[]{:S(2)}) async-start(), calls=%async_computation.2 | async-start | bytes 3538944 | tf_op jit(solution)/shard_map/all_gather | solution.py:386
  8.8 46.5 %copy-start.4 = (bf16[6144]{0:T(1024)(128)(2,1)S(1)}, bf16[6144]{0:T(1024)(128)(2,1)}, u32[]{:S(2)}) copy-start(bf16[6144]{0:T(1024)(128)(2,1)} %param.12) | copy-start | bytes 36868
  8.8 46.5 %copy-start = (bf16[1,1024,768]{2,1,0:T(8,128)(2,1)S(1)}, bf16[1,1024,768]{2,1,0:T(8,128)(2,1)}, u32[]{:S(2)}) copy-start(bf16[1,1024,768]{2,1,0:T(8,128)(2,1)} %tokens.1) | copy-start | bytes 4718596
  8.9 46.5 %copy-start.1 = (s32[1,1024]{1,0:T(1,128)S(1)}, s32[1,1024]{1,0:T(1,128)}, u32[]{:S(2)}) copy-start(s32[1,1024]{1,0:T(1,128)} %order.5) | copy-start | bytes 12292
  8.9 8.2 %collective-permute-start = (bf16[2,96,384]{2,1,0:T(8,128)(2,1)S(1)}, bf16[2,96,384]{2,1,0:T(8,128)(2,1)S(1)}, u32[]{:S(2)}, u32[]{:S(2)}) collective-permute-start(bf16[2,96,384]{2,1,0:T(8,128)(2,1)S(1)} %shard_map.120), channel_id=1, source_target_pairs={{0,0},{1,1},{2,2},{3,3},{4,4},{5,5},{6,6},{7,7},{8,12},{9,13},{10,... | collective-permute-start | bytes 442376 | tf_op jit(solution)/shard_map/ppermute | solution.py:189
  17.2 126.2 %reduce-scatter.2.cloned.1.call-start = ((), (), s32[]{:S(2)}) async-start(), calls=%async_computation.3 | async-start | bytes 3538944 | tf_op jit(solution)/shard_map/reduce_scatter | solution.py:407
  17.2 16.4 %collective-permute-start.3 = (bf16[96,384]{1,0:T(8,128)(2,1)S(1)}, bf16[96,384]{1,0:T(8,128)(2,1)S(1)}, u32[]{:S(2)}, u32[]{:S(2)}) collective-permute-start(bf16[96,384]{1,0:T(8,128)(2,1)S(1)} %get-tuple-element.41), channel_id=1, source_target_pairs={{0,128},{8,136},{16,144},{24,152},{32,160},{40,168},{48,176},{56,1... | collective-permute-start | bytes 221192 | tf_op jit(solution)/shard_map/ppermute | solution.py:201
  28.0 6.2 %collective-permute-start.2 = (bf16[96,384]{1,0:T(8,128)(2,1)S(1)}, bf16[96,384]{1,0:T(8,128)(2,1)S(1)}, u32[]{:S(2)}, u32[]{:S(2)}) collective-permute-start(bf16[96,384]{1,0:T(8,128)(2,1)S(1)} %get-tuple-element.41), channel_id=1, source_target_pairs={{0,192},{8,200},{16,208},{24,216},{32,224},{40,232},{48,240},{56,2... | collective-permute-start | bytes 221192 | tf_op jit(solution)/shard_map/ppermute | solution.py:201
  28.6 5.6 %collective-permute-start.1 = (bf16[96,384]{1,0:T(8,128)(2,1)S(1)}, bf16[96,384]{1,0:T(8,128)(2,1)S(1)}, u32[]{:S(2)}, u32[]{:S(2)}) collective-permute-start(bf16[96,384]{1,0:T(8,128)(2,1)S(1)} %get-tuple-element.41), channel_id=1, source_target_pairs={{0,64},{8,72},{16,80},{24,88},{32,96},{40,104},{48,112},{56,120},{... | collective-permute-start | bytes 221192 | tf_op jit(solution)/shard_map/ppermute | solution.py:201
  30.1 5.9 %collective-permute-start.6 = (bf16[96,384]{1,0:T(8,128)(2,1)S(1)}, bf16[96,384]{1,0:T(8,128)(2,1)S(1)}, u32[]{:S(2)}, u32[]{:S(2)}) collective-permute-start(bf16[96,384]{1,0:T(8,128)(2,1)S(1)} %get-tuple-element.42), channel_id=1, source_target_pairs={{0,32},{8,40},{16,48},{24,56},{32,0},{40,8},{48,16},{56,24},{64,96... | collective-permute-start | bytes 221192 | tf_op jit(solution)/shard_map/ppermute | solution.py:201
  32.2 4.5 %collective-permute-start.5 = (bf16[96,384]{1,0:T(8,128)(2,1)S(1)}, bf16[96,384]{1,0:T(8,128)(2,1)S(1)}, u32[]{:S(2)}, u32[]{:S(2)}) collective-permute-start(bf16[96,384]{1,0:T(8,128)(2,1)S(1)} %get-tuple-element.42), channel_id=1, source_target_pairs={{0,48},{8,56},{16,0},{24,8},{32,16},{40,24},{48,32},{56,40},{64,11... | collective-permute-start | bytes 221192 | tf_op jit(solution)/shard_map/ppermute | solution.py:201
  33.6 4.4 %collective-permute-start.4 = (bf16[96,384]{1,0:T(8,128)(2,1)S(1)}, bf16[96,384]{1,0:T(8,128)(2,1)S(1)}, u32[]{:S(2)}, u32[]{:S(2)}) collective-permute-start(bf16[96,384]{1,0:T(8,128)(2,1)S(1)} %get-tuple-element.42), channel_id=1, source_target_pairs={{0,16},{8,24},{16,32},{24,40},{32,48},{40,56},{48,0},{56,8},{64,80... | collective-permute-start | bytes 221192 | tf_op jit(solution)/shard_map/ppermute | solution.py:201
  38.0 6.8 %collective-permute-start.18 = (bf16[4,96,384]{2,1,0:T(8,128)(2,1)S(1)}, bf16[4,96,384]{2,1,0:T(8,128)(2,1)S(1)}, u32[]{:S(2)}, u32[]{:S(2)}) collective-permute-start(bf16[4,96,384]{2,1,0:T(8,128)(2,1)S(1)} %pad_maximum_fusion.1.refs_8_), channel_id=1, source_target_pairs={{0,192},{8,200},{16,208},{24,216},{32,224},{40,232},{48,240},{56,2... | collective-permute-start | bytes 884744 | tf_op jit(solution)/shard_map/ppermute | solution.py:210
  39.9 14.3 %collective-permute-start.16 = (bf16[4,96,384]{2,1,0:T(8,128)(2,1)S(1)}, bf16[4,96,384]{2,1,0:T(8,128)(2,1)S(1)}, u32[]{:S(2)}, u32[]{:S(2)}) collective-permute-start(bf16[4,96,384]{2,1,0:T(8,128)(2,1)S(1)} %pad_maximum_fusion.1.refs_8_), channel_id=1, source_target_pairs={{0,64},{8,72},{16,80},{24,88},{32,96},{40,104},{48,112},{56,120},{... | collective-permute-start | bytes 884744 | tf_op jit(solution)/shard_map/ppermute | solution.py:210
  40.1 14.6 %collective-permute-start.15 = (bf16[4,96,384]{2,1,0:T(8,128)(2,1)S(1)}, bf16[4,96,384]{2,1,0:T(8,128)(2,1)S(1)}, u32[]{:S(2)}, u32[]{:S(2)}) collective-permute-start(bf16[4,96,384]{2,1,0:T(8,128)(2,1)S(1)} %pad_maximum_fusion.1.refs_8_), channel_id=1, source_target_pairs={{0,8},{8,0},{16,24},{24,16},{32,40},{40,32},{48,56},{56,48},{64,72... | collective-permute-start | bytes 884744 | tf_op jit(solution)/shard_map/ppermute | solution.py:213
  40.1 14.7 %collective-permute-start.7 = (bf16[4,96,384]{2,1,0:T(8,128)(2,1)S(1)}, bf16[4,96,384]{2,1,0:T(8,128)(2,1)S(1)}, u32[]{:S(2)}, u32[]{:S(2)}) collective-permute-start(bf16[4,96,384]{2,1,0:T(8,128)(2,1)S(1)} %pad_maximum_fusion.1.refs_8_), channel_id=1, source_target_pairs={{0,128},{8,136},{16,144},{24,152},{32,160},{40,168},{48,176},{56,1... | collective-permute-start | bytes 884744 | tf_op jit(solution)/shard_map/ppermute | solution.py:210
  41.5 16.3 %collective-permute-start.13 = (bf16[4,96,384]{2,1,0:T(8,128)(2,1)S(1)}, bf16[4,96,384]{2,1,0:T(8,128)(2,1)S(1)}, u32[]{:S(2)}, u32[]{:S(2)}) collective-permute-start(bf16[4,96,384]{2,1,0:T(8,128)(2,1)S(1)} %pad_maximum_fusion.refs_0_), channel_id=1, source_target_pairs={{0,32},{8,40},{16,48},{24,56},{32,0},{40,8},{48,16},{56,24},{64,96... | collective-permute-start | bytes 884744 | tf_op jit(solution)/shard_map/ppermute | solution.py:210
  44.8 13.6 %collective-permute-start.11 = (bf16[4,96,384]{2,1,0:T(8,128)(2,1)S(1)}, bf16[4,96,384]{2,1,0:T(8,128)(2,1)S(1)}, u32[]{:S(2)}, u32[]{:S(2)}) collective-permute-start(bf16[4,96,384]{2,1,0:T(8,128)(2,1)S(1)} %pad_maximum_fusion.refs_0_), channel_id=1, source_target_pairs={{0,48},{8,56},{16,0},{24,8},{32,16},{40,24},{48,32},{56,40},{64,11... | collective-permute-start | bytes 884744 | tf_op jit(solution)/shard_map/ppermute | solution.py:210
  54.2 7.1 %collective-permute-start.9 = (bf16[4,96,384]{2,1,0:T(8,128)(2,1)S(1)}, bf16[4,96,384]{2,1,0:T(8,128)(2,1)S(1)}, u32[]{:S(2)}, u32[]{:S(2)}) collective-permute-start(bf16[4,96,384]{2,1,0:T(8,128)(2,1)S(1)} %pad_maximum_fusion.refs_0_), channel_id=1, source_target_pairs={{0,16},{8,24},{16,32},{24,40},{32,48},{40,56},{48,0},{56,8},{64,80... | collective-permute-start | bytes 884744 | tf_op jit(solution)/shard_map/ppermute | solution.py:210
  54.8 6.5 %collective-permute-start.8 = (bf16[4,96,384]{2,1,0:T(8,128)(2,1)S(1)}, bf16[4,96,384]{2,1,0:T(8,128)(2,1)S(1)}, u32[]{:S(2)}, u32[]{:S(2)}) collective-permute-start(bf16[4,96,384]{2,1,0:T(8,128)(2,1)S(1)} %pad_maximum_fusion.refs_0_), channel_id=1, source_target_pairs={{0,8},{8,0},{16,24},{24,16},{32,40},{40,32},{48,56},{56,48},{64,72... | collective-permute-start | bytes 884744 | tf_op jit(solution)/shard_map/ppermute | solution.py:213
  54.8 7.0 %collective-permute-start.19 = (bf16[4,96,384]{2,1,0:T(8,128)(2,1)S(1)}, bf16[4,96,384]{2,1,0:T(8,128)(2,1)S(1)}, u32[]{:S(2)}, u32[]{:S(2)}) collective-permute-start(bf16[4,96,384]{2,1,0:T(8,128)(2,1)S(1)} %collective-permute-done.18.refs_12_), channel_id=1, source_target_pairs={{0,8},{8,0},{16,24},{24,16},{32,40},{40,32},{48,56},{56,48},{64,72... | collective-permute-start | bytes 884744 | tf_op jit(solution)/shard_map/ppermute | solution.py:213
  57.7 4.1 %collective-permute-start.17 = (bf16[4,96,384]{2,1,0:T(8,128)(2,1)S(1)}, bf16[4,96,384]{2,1,0:T(8,128)(2,1)S(1)}, u32[]{:S(2)}, u32[]{:S(2)}) collective-permute-start(bf16[4,96,384]{2,1,0:T(8,128)(2,1)S(1)} %collective-permute-done.16.refs_10_), channel_id=1, source_target_pairs={{0,8},{8,0},{16,24},{24,16},{32,40},{40,32},{48,56},{56,48},{64,72... | collective-permute-start | bytes 884744 | tf_op jit(solution)/shard_map/ppermute | solution.py:213
  58.4 3.4 %collective-permute-start.14 = (bf16[4,96,384]{2,1,0:T(8,128)(2,1)S(1)}, bf16[4,96,384]{2,1,0:T(8,128)(2,1)S(1)}, u32[]{:S(2)}, u32[]{:S(2)}) collective-permute-start(bf16[4,96,384]{2,1,0:T(8,128)(2,1)S(1)} %collective-permute-done.13.refs_6_), channel_id=1, source_target_pairs={{0,8},{8,0},{16,24},{24,16},{32,40},{40,32},{48,56},{56,48},{64,72... | collective-permute-start | bytes 884744 | tf_op jit(solution)/shard_map/ppermute | solution.py:213
  61.2 1.6 collective-permute-start.12
  61.2 2.0 %collective-permute-start.10 = (bf16[4,96,384]{2,1,0:T(8,128)(2,1)S(1)}, bf16[4,96,384]{2,1,0:T(8,128)(2,1)S(1)}, u32[]{:S(2)}, u32[]{:S(2)}) collective-permute-start(bf16[4,96,384]{2,1,0:T(8,128)(2,1)S(1)} %collective-permute-done.9.refs_2_), channel_id=1, source_target_pairs={{0,8},{8,0},{16,24},{24,16},{32,40},{40,32},{48,56},{56,48},{64,72... | collective-permute-start | bytes 884744 | tf_op jit(solution)/shard_map/ppermute | solution.py:213
  61.7 1.9 %collective-permute-start.20 = (bf16[4,96,384]{2,1,0:T(8,128)(2,1)S(1)}, bf16[4,96,384]{2,1,0:T(8,128)(2,1)S(1)}, u32[]{:S(2)}, u32[]{:S(2)}) collective-permute-start(bf16[4,96,384]{2,1,0:T(8,128)(2,1)S(1)} %collective-permute-done.7.refs_14_), channel_id=1, source_target_pairs={{0,8},{8,0},{16,24},{24,16},{32,40},{40,32},{48,56},{56,48},{64,72... | collective-permute-start | bytes 884744 | tf_op jit(solution)/shard_map/ppermute | solution.py:213
  70.2 22.5 %slice-start = ((s8[4718592]{0:T(1024)(128)(4,1)}), s8[4194304]{0:T(1024)(128)(4,1)S(1)}, s32[]{:S(2)}) async-start(s8[4718592]{0:T(1024)(128)(4,1)} %bitcast.24), calls=%async_computation.4 | async-start | bytes 8388608
  70.2 22.5 %slice-start.1 = ((s8[4718592]{0:T(1024)(128)(4,1)}), s8[524288]{0:T(1024)(128)(4,1)S(1)}, s32[]{:S(2)}) async-start(s8[4718592]{0:T(1024)(128)(4,1)} %bitcast.24), calls=%async_computation.5 | async-start | bytes 1048576
  70.2 19.8 %collective-permute-start.25 = (bf16[512,3072]{1,0:T(8,128)(2,1)}, bf16[512,3072]{1,0:T(8,128)(2,1)S(1)}, u32[]{:S(2)}, u32[]{:S(2)}) collective-permute-start(bf16[512,3072]{1,0:T(8,128)(2,1)} %all-gather.2.cloned.1.call-done.mixed.own_mixed), channel_id=1, source_target_pairs={{0,8},{8,0},{16,24},{24,16},{32,40},{40,32},{48,56},{56,48},{64,72... | collective-permute-start | bytes 9437192 | tf_op jit(solution)/shard_map/ppermute | solution.py:399
  77.6 4.7 %collective-permute-start.23 = (f32[8,512]{1,0:T(8,128)S(1)}, f32[8,512]{1,0:T(8,128)S(1)}, u32[]{:S(2)}, u32[]{:S(2)}) collective-permute-start(f32[8,512]{1,0:T(8,128)S(1)} %get-tuple-element.53), channel_id=1, source_target_pairs={{0,2},{1,3},{2,0},{3,1},{4,6},{5,7},{6,4},{7,5},{8,10},{9,11},{10,... | collective-permute-start | bytes 49160 | tf_op jit(solution)/shard_map/ppermute | solution.py:395
  79.4 5.5 %collective-permute-start.22 = (f32[8,512]{1,0:T(8,128)S(1)}, f32[8,512]{1,0:T(8,128)S(1)}, u32[]{:S(2)}, u32[]{:S(2)}) collective-permute-start(f32[8,512]{1,0:T(8,128)S(1)} %get-tuple-element.53), channel_id=1, source_target_pairs={{0,3},{1,2},{2,1},{3,0},{4,7},{5,6},{6,5},{7,4},{8,11},{9,10},{10,... | collective-permute-start | bytes 49160 | tf_op jit(solution)/shard_map/ppermute | solution.py:395
  80.8 4.1 %collective-permute-start.21 = (f32[8,512]{1,0:T(8,128)S(1)}, f32[8,512]{1,0:T(8,128)S(1)}, u32[]{:S(2)}, u32[]{:S(2)}) collective-permute-start(f32[8,512]{1,0:T(8,128)S(1)} %get-tuple-element.53), channel_id=1, source_target_pairs={{0,1},{1,0},{2,3},{3,2},{4,5},{5,4},{6,7},{7,6},{8,9},{9,8},{10,11... | collective-permute-start | bytes 49160 | tf_op jit(solution)/shard_map/ppermute | solution.py:395
  84.9 5.0 %collective-permute-start.24 = (f32[8,512]{1,0:T(8,128)S(1)}, f32[8,512]{1,0:T(8,128)S(1)}, u32[]{:S(2)}, u32[]{:S(2)}) collective-permute-start(f32[8,512]{1,0:T(8,128)S(1)} %add_add_fusion.refs_0_), channel_id=1, source_target_pairs={{0,7},{1,6},{2,5},{3,4},{4,3},{5,2},{6,1},{7,0},{8,15},{9,14},{10,... | collective-permute-start | bytes 49160 | tf_op jit(solution)/shard_map/ppermute | solution.py:395
  90.0 2.7 %copy-start.3 = (bf16[512,3072]{1,0:T(8,128)(2,1)}, bf16[512,3072]{1,0:T(8,128)(2,1)S(1)}, u32[]{:S(2)}) copy-start(bf16[512,3072]{1,0:T(8,128)(2,1)S(1)} %collective-permute-done.25.other_mixed) | copy-start | bytes 9437188
  92.7 4.3 %collective-permute-start.26 = (bf16[512,768]{1,0:T(8,128)(2,1)S(1)}, bf16[512,768]{1,0:T(8,128)(2,1)S(1)}, u32[]{:S(2)}, u32[]{:S(2)}) collective-permute-start(bf16[512,768]{1,0:T(8,128)(2,1)S(1)} %get-tuple-element.56.grad_proj.own_grad), channel_id=1, source_target_pairs={{0,8},{8,0},{16,24},{24,16},{32,40},{40,32},{48,56},{56,48},{64,72... | collective-permute-start | bytes 2359304 | tf_op jit(solution)/shard_map/ppermute | solution.py:405
  141.3 18.1 %collective-permute-start.27 = (bf16[192,384]{1,0:T(8,128)(2,1)S(1)}, bf16[192,384]{1,0:T(8,128)(2,1)S(1)}, u32[]{:S(2)}, u32[]{:S(2)}) collective-permute-start(bf16[192,384]{1,0:T(8,128)(2,1)S(1)} %reduce_sum.12), channel_id=1, source_target_pairs={{0,0},{1,32},{2,64},{3,96},{4,128},{5,160},{6,192},{7,224},{8,4},{... | collective-permute-start | bytes 442376 | tf_op jit(solution)/shard_map/ppermute | solution.py:421
Sparse Core Ops, SparseCore 0:
  17.3 52.8 all-gather.1
  97.2 45.8 reduce-scatter.1

commit v5 on v4

--- a/solution.py
+++ b/solution.py
@@ -269,7 +269,7 @@
 
 def project(info, mixed, weight, grad, gain):
     depth, width = weight.shape
-    block = 768
+    block = 1536
     return call(
         project_kernel, (depth // block,), (info,),
         [
@@ -280,7 +280,7 @@
         ],
         [pl.BlockSpec((KEEP_MAX, width), lambda k, i: (0, 0)), pl.BlockSpec((8, KEEP_MAX), lambda k, i: (0, 0))],
         [jax.ShapeDtypeStruct((KEEP_MAX, width), F32), jax.ShapeDtypeStruct((8, KEEP_MAX), F32)],
-        [], in_hbm(mixed), in_hbm(weight), grad, gain, vmem=18,
+        [], in_hbm(mixed), in_hbm(weight), grad, gain, vmem=26,
     )
 
 
@@ -340,25 +340,25 @@
         turned[:, :KEEP_MAX] = jnp.transpose(own_grad[...])
         turned[:, KEEP_MAX:] = jnp.transpose(other_grad[...])
 
-    rows = jnp.concatenate([own_mixed[...], other_mixed[...]], axis=0)
-    out[0] = dot(turned[...], rows, (1, 0)).astype(BF)
+    product = dot(turned[:, :KEEP_MAX], own_mixed[...], (1, 0))
+    product = product + dot(turned[:, KEEP_MAX:], other_mixed[...], (1, 0))
+    width = out.shape[2]
+    for j in range(out.shape[0]):
+        out[j] = product[:, j * width:(j + 1) * width].astype(BF)
 
 
 def outer(info, own_grad, other_grad, mixed, other_mixed):
     width = own_grad.shape[1]
     block = mixed.shape[1] // 8
     grad_spec = pl.BlockSpec((KEEP_MAX, width), lambda j, i: (0, 0))
-    return call(
-        outer_kernel, (4,), (info,),
-        [
-            grad_spec, grad_spec,
-            pl.BlockSpec((KEEP_MAX, block), lambda j, i: (0, i[4] * 4 + j)),
-            pl.BlockSpec((KEEP_MAX, block), lambda j, i: (0, i[4] * 4 + j)),
-        ],
-        pl.BlockSpec((1, width, block), lambda j, i: (j, 0, 0)),
+    mixed_spec = pl.BlockSpec((KEEP_MAX, 2 * block), lambda j, i: (0, i[4] * 2 + j))
+    return call(
+        outer_kernel, (2,), (info,),
+        [grad_spec, grad_spec, mixed_spec, mixed_spec],
+        pl.BlockSpec((2, width, block), lambda j, i: (j, 0, 0)),
         jax.ShapeDtypeStruct((4, width, block), BF),
         [pltpu.VMEM((width, 2 * KEEP_MAX), BF)],
-        own_grad, other_grad, in_hbm(mixed), in_hbm(other_mixed), vmem=16,
+        own_grad, other_grad, in_hbm(mixed), in_hbm(other_mixed), vmem=22,
     )
 
 

time: 167 us -> 166 us (level)
  transfers between devices with their start and end apart: 30 -> 30, of which waited for: 15 -> 16; matrix products, arithmetic and copies ran while one was open for 0% -> 0% of each run, Pallas kernels for 24% -> 24%
where the time goes in v5:
time: 166 us
  Pallas kernels  43.1 us (26%)
  blocking collectives  37.7 us (23%)
  waiting for transfers between devices  34.9 us (21%)
  starting transfers between devices  34.3 us (21%)
  between operations  14.3 us (9%)
    pallas_call x9, Pallas kernels, call(): pl.pallas_call(kernel, grid_spec=pltpu.PrefetchScalarGridSpec(num_scalar_...  43.1 us
    all_to_all x1, blocking collectives, on_device(): lax.all_to_all(pair, 'dp', split_axis=0, concat_axis=0, tiled=True, axis_...  37.7 us
    ppermute x6, starting transfers between devices, spread_columns(): lax.ppermute(part, 'dp', along[way][s])  17 us
    ppermute x6, waiting for transfers between devices, spread_columns(): piece = four if s == 0 else lax.ppermute(four, 'dp', along[way][s])  12.2 us
    ppermute x6, starting transfers between devices, spread_columns(): piece = four if s == 0 else lax.ppermute(four, 'dp', along[way][s])  7.59 us
    ppermute x4, waiting for transfers between devices, swapped(): return lax.ppermute(values, 'mp', [(m, m ^ bits) for m in range(ranks)])  7.18 us
    ppermute x1, waiting for transfers between devices, on_device(): total = lax.ppermute(total, ('dp', 'mp'), home)  5.93 us
    ppermute x4, starting transfers between devices, swapped(): return lax.ppermute(values, 'mp', [(m, m ^ bits) for m in range(ranks)])  5.21 us
  transfers between devices with their start and end apart: 30, of which 16 were waited for; matrix products, arithmetic and copies ran while one was open for 0% of the time, Pallas kernels for 24%

profile of v5, /device:TPU:2, one launch (start us, length us, event | category | flops | bytes accessed | tf_op | source)
XLA Modules:
  0.0 165.6 jit_solution(13253420411762554168)
XLA Ops:
  7.4 1.5 shard_map.120
  8.9 0.8 collective-permute-start
  9.7 7.4 %shard_map.119 = (bf16[512,384]{1,0:T(8,128)(2,1)}, bf16[512,384]{1,0:T(8,128)(2,1)}, bf16[512,384]{1,0:T(8,128)(2,1)}, bf16[512,384]{1,0:T(8,128)(2,1)}, f32[3,512,512]{2,1,0:T(8,128)}) custom-call(s32[6]{0:T(128)S(1)} %stack.57.info, s32[32]{0:T(128)S(1)} %copy-done.2, s32[1,1024]{1,0:T(1,128)} %order.5, bf16[1,1024,384]{2,1,0:T(8,128)(2,1)} %query.1, ...), custom_call_target="tpu_custom_call" | custom-call | bytes 4726784 | tf_op jit(solution)/shard_map/pallas_call | solution.py:21
  17.2 10.8 %collective-permute-start.3 = (bf16[96,384]{1,0:T(8,128)(2,1)S(1)}, bf16[96,384]{1,0:T(8,128)(2,1)S(1)}, u32[]{:S(2)}, u32[]{:S(2)}) collective-permute-start(bf16[96,384]{1,0:T(8,128)(2,1)S(1)} %get-tuple-element.41), channel_id=1, source_target_pairs={{0,128},{8,136},{16,144},{24,152},{32,160},{40,168},{48,176},{56,1... | collective-permute-start | bytes 221192 | tf_op jit(solution)/shard_map/ppermute | solution.py:201
  28.0 0.6 collective-permute-start.2
  28.6 1.4 collective-permute-start.1
  30.1 2.1 %collective-permute-start.6 = (bf16[96,384]{1,0:T(8,128)(2,1)S(1)}, bf16[96,384]{1,0:T(8,128)(2,1)S(1)}, u32[]{:S(2)}, u32[]{:S(2)}) collective-permute-start(bf16[96,384]{1,0:T(8,128)(2,1)S(1)} %get-tuple-element.42), channel_id=1, source_target_pairs={{0,32},{8,40},{16,48},{24,56},{32,0},{40,8},{48,16},{56,24},{64,96... | collective-permute-start | bytes 221192 | tf_op jit(solution)/shard_map/ppermute | solution.py:201
  32.2 1.4 collective-permute-start.5
  33.6 0.6 collective-permute-start.4
  34.3 1.7 %collective-permute-done.6 = bf16[96,384]{1,0:T(8,128)(2,1)S(1)} collective-permute-done((bf16[96,384]{1,0:T(8,128)(2,1)S(1)}, bf16[96,384]{1,0:T(8,128)(2,1)S(1)}, u32[]{:S(2)}, u32[]{:S(2)}) %collective-permute-start.6) | collective-permute-done | bytes 73760 | tf_op jit(solution)/shard_map/ppermute | solution.py:201
  35.9 0.8 collective-permute-done.5
  36.7 1.3 collective-permute-done.4
  38.0 1.9 %collective-permute-start.18 = (bf16[4,96,384]{2,1,0:T(8,128)(2,1)S(1)}, bf16[4,96,384]{2,1,0:T(8,128)(2,1)S(1)}, u32[]{:S(2)}, u32[]{:S(2)}) collective-permute-start(bf16[4,96,384]{2,1,0:T(8,128)(2,1)S(1)} %pad_maximum_fusion.1.refs_8_), channel_id=1, source_target_pairs={{0,192},{8,200},{16,208},{24,216},{32,224},{40,232},{48,240},{56,2... | collective-permute-start | bytes 884744 | tf_op jit(solution)/shard_map/ppermute | solution.py:210
  40.1 1.3 collective-permute-start.7
  41.5 1.2 collective-permute-start.13
  42.7 2.2 %collective-permute-done.18.refs_12_ = bf16[4,96,384]{2,1,0:T(8,128)(2,1)S(1)} collective-permute-done((bf16[4,96,384]{2,1,0:T(8,128)(2,1)S(1)}, bf16[4,96,384]{2,1,0:T(8,128)(2,1)S(1)}, u32[]{:S(2)}, u32[]{:S(2)}) %collective-permute-start.18) | collective-permute-done | bytes 294944 | tf_op jit(solution)/shard_map/ppermute | solution.py:210
  44.8 2.4 %collective-permute-start.11 = (bf16[4,96,384]{2,1,0:T(8,128)(2,1)S(1)}, bf16[4,96,384]{2,1,0:T(8,128)(2,1)S(1)}, u32[]{:S(2)}, u32[]{:S(2)}) collective-permute-start(bf16[4,96,384]{2,1,0:T(8,128)(2,1)S(1)} %pad_maximum_fusion.refs_0_), channel_id=1, source_target_pairs={{0,48},{8,56},{16,0},{24,8},{32,16},{40,24},{48,32},{56,40},{64,11... | collective-permute-start | bytes 884744 | tf_op jit(solution)/shard_map/ppermute | solution.py:210
  47.2 7.0 %collective-permute-done.16.refs_10_ = bf16[4,96,384]{2,1,0:T(8,128)(2,1)S(1)} collective-permute-done((bf16[4,96,384]{2,1,0:T(8,128)(2,1)S(1)}, bf16[4,96,384]{2,1,0:T(8,128)(2,1)S(1)}, u32[]{:S(2)}, u32[]{:S(2)}) %collective-permute-start.16) | collective-permute-done | bytes 294944 | tf_op jit(solution)/shard_map/ppermute | solution.py:210
  54.2 0.6 collective-permute-start.9
  54.8 0.5 collective-permute-start.19
  55.3 2.4 %shard_map.121.grad = bf16[512,768]{1,0:T(8,128)(2,1)S(1)} custom-call(s32[6]{0:T(128)S(1)} %stack.57.info, s32[32]{0:T(128)S(1)} %copy-done.2, s32[1,1024]{1,0:T(1,128)S(1)} %copy-done.1, bf16[1,1024,768]{2,1,0:T(8,128)(2,1)S(1)} %copy-done), custom_call_target="tpu_custom_call" | custom-call | bytes 3153920 | tf_op jit(solution)/shard_map/pallas_call | solution.py:21
  57.7 0.4 collective-permute-start.17
  58.1 0.3 collective-permute-done.11.refs_4_
  58.6 2.7 %collective-permute-done.9.refs_2_ = bf16[4,96,384]{2,1,0:T(8,128)(2,1)S(1)} collective-permute-done((bf16[4,96,384]{2,1,0:T(8,128)(2,1)S(1)}, bf16[4,96,384]{2,1,0:T(8,128)(2,1)S(1)}, u32[]{:S(2)}, u32[]{:S(2)}) %collective-permute-start.9) | collective-permute-done | bytes 294944 | tf_op jit(solution)/shard_map/ppermute | solution.py:210
  61.2 0.5 collective-permute-start.10
  61.8 1.0 collective-permute-done.12.refs_5_
  62.8 0.4 collective-permute-done.10.refs_3_
  63.2 0.4 collective-permute-done.20.refs_15_
  63.7 3.2 %shard_map.122 = bf16[8,384,768]{2,1,0:T(8,128)(2,1)} custom-call(s32[6]{0:T(128)S(1)} %stack.57.info, bf16[4,96,384]{2,1,0:T(8,128)(2,1)S(1)} %pad_maximum_fusion.refs_0_, bf16[4,96,384]{2,1,0:T(8,128)(2,1)S(1)} %collective-permute-done.8.refs_1_, bf16[4,96,384]{2,1,0:T(8,128)(2,1)S(1)} %collective-permute-done.9.refs_2_, ...), custom_call_target="tpu_custom_call" | custom-call | bytes 9437184 | tf_op jit(solution)/shard_map/pallas_call | solution.py:21
  66.9 3.3 %all-gather.2.cloned.1.call-done.mixed.own_mixed = bf16[512,3072]{1,0:T(8,128)(2,1)} async-done(((bf16[512,384]{1,0:T(8,128)(2,1)}), bf16[512,3072]{1,0:T(8,128)(2,1)}) %all-gather.2.cloned.1.call-update) | async-done | bytes 3145744 | tf_op jit(solution)/shard_map/all_gather | solution.py:386
  70.2 7.0 %shard_map.123 = (f32[512,768]{1,0:T(8,128)S(1)}, f32[8,512]{1,0:T(8,128)S(1)}) custom-call(s32[6]{0:T(128)S(1)} %stack.57.info, bf16[512,3072]{1,0:T(8,128)(2,1)} %all-gather.2.cloned.1.call-done.mixed.own_mixed, bf16[3072,768]{1,0:T(8,128)(2,1)} %bitcast.23, bf16[512,768]{1,0:T(8,128)(2,1)S(1)} %shard_map.121.grad, bf16[1,6144]{1,0:T(2,128)(2,1)S(1)} %reshape.19.gain), custom_call_target="tpu_custom_call" | custom-call | bytes 17326080 | tf_op jit(solution)/shard_map/pallas_call | solution.py:21
  77.2 1.8 %collective-permute-start.23 = (f32[8,512]{1,0:T(8,128)S(1)}, f32[8,512]{1,0:T(8,128)S(1)}, u32[]{:S(2)}, u32[]{:S(2)}) collective-permute-start(f32[8,512]{1,0:T(8,128)S(1)} %get-tuple-element.53), channel_id=1, source_target_pairs={{0,2},{1,3},{2,0},{3,1},{4,6},{5,7},{6,4},{7,5},{8,10},{9,11},{10,... | collective-permute-start | bytes 49160 | tf_op jit(solution)/shard_map/ppermute | solution.py:395
  79.0 1.5 collective-permute-start.22
  80.5 0.3 collective-permute-start.21
  80.8 1.1 collective-permute-done.23
  82.0 2.6 %collective-permute-done.22 = f32[8,512]{1,0:T(8,128)S(1)} collective-permute-done((f32[8,512]{1,0:T(8,128)S(1)}, f32[8,512]{1,0:T(8,128)S(1)}, u32[]{:S(2)}, u32[]{:S(2)}) %collective-permute-start.22) | collective-permute-done | bytes 16416 | tf_op jit(solution)/shard_map/ppermute | solution.py:395
  84.6 1.6 collective-permute-start.24
  86.2 3.4 %collective-permute-done.24.refs_1_ = f32[8,512]{1,0:T(8,128)S(1)} collective-permute-done((f32[8,512]{1,0:T(8,128)S(1)}, f32[8,512]{1,0:T(8,128)S(1)}, u32[]{:S(2)}, u32[]{:S(2)}) %collective-permute-start.24) | collective-permute-done | bytes 16416 | tf_op jit(solution)/shard_map/ppermute | solution.py:395
  89.6 2.7 %shard_map.124 = (bf16[512,768]{1,0:T(8,128)(2,1)S(1)}, bf16[512,768]{1,0:T(8,128)(2,1)}) custom-call(s32[6]{0:T(128)S(1)} %stack.57.info, s32[32]{0:T(128)S(1)} %copy-done.2, f32[512,768]{1,0:T(8,128)S(1)} %get-tuple-element.52.projected, bf16[512,768]{1,0:T(8,128)(2,1)S(1)} %shard_map.121.grad, bf16[1,6144]{1,0:T(2,128)(2,1)S(1)} %reshape.19.gain, ...), custom_call_target="tpu_custom_call" | custom-call | bytes 4808704 | tf_op jit(solution)/shard_map/pallas_call | solution.py:21
  92.4 4.3 %shard_map.125 = bf16[8,512,384]{2,1,0:T(8,128)(2,1)} custom-call(bf16[512,768]{1,0:T(8,128)(2,1)S(1)} %get-tuple-element.56.grad_proj.own_grad, bf16[3072,768]{1,0:T(8,128)(2,1)S(1)} %bitcast.26), custom_call_target="tpu_custom_call" | custom-call | bytes 11010048 | tf_op jit(solution)/shard_map/pallas_call | solution.py:21
  96.7 5.2 %shard_map.127 = bf16[4,768,384]{2,1,0:T(8,128)(2,1)S(1)} custom-call(s32[6]{0:T(128)S(1)} %stack.57.info, bf16[512,768]{1,0:T(8,128)(2,1)S(1)} %get-tuple-element.56.grad_proj.own_grad, bf16[512,768]{1,0:T(8,128)(2,1)S(1)} %collective-permute-done.26.other_grad, bf16[512,3072]{1,0:T(8,128)(2,1)} %all-gather.2.cloned.1.call-done.mixed.own_mixed, ...), custom_call_target="tpu_custom_call" | custom-call | bytes 15728640 | tf_op jit(solution)/shard_map/pallas_call | solution.py:21
  102.0 37.7 %all_to_all.5 = bf16[16,192,384]{2,1,0:T(8,128)(2,1)S(1)} all-to-all(bf16[16,192,384]{2,1,0:T(8,128)(2,1)S(1)} %bitcast.27), channel_id=1, replica_groups={{0,16,32,48,64,80,96,112,128,144,160,176,192,208,224,240},{8,24,40,56,7..., dimensions={0} | all-to-all | bytes 4718592 | tf_op jit(solution)/shard_map/all_to_all | solution.py:413
  139.6 0.3 reduce_sum.12
  140.0 2.0 %collective-permute-start.27 = (bf16[192,384]{1,0:T(8,128)(2,1)S(1)}, bf16[192,384]{1,0:T(8,128)(2,1)S(1)}, u32[]{:S(2)}, u32[]{:S(2)}) collective-permute-start(bf16[192,384]{1,0:T(8,128)(2,1)S(1)} %reduce_sum.12), channel_id=1, source_target_pairs={{0,0},{1,32},{2,64},{3,96},{4,128},{5,160},{6,192},{7,224},{8,4},{... | collective-permute-start | bytes 442376 | tf_op jit(solution)/shard_map/ppermute | solution.py:421
  142.0 0.8 reduce-scatter.2.cloned.1.call-done
  142.8 9.3 %shard_map.126 = (bf16[1,1024,384]{2,1,0:T(8,128)(2,1)}, bf16[1,1024,384]{2,1,0:T(8,128)(2,1)}, bf16[1,1024,384]{2,1,0:T(8,128)(2,1)}, bf16[1,1024,768]{2,1,0:T(8,128)(2,1)}) custom-call(s32[6]{0:T(128)S(1)} %stack.57.info, s32[32]{0:T(128)S(1)} %copy-done.2, s32[1,1024]{1,0:T(1,128)} %order.5, bf16[512,384]{1,0:T(8,128)(2,1)} %bitcast.28, ...), custom_call_target="tpu_custom_call" | custom-call | bytes 11018240 | tf_op jit(solution)/shard_map/pallas_call | solution.py:21
  152.1 5.9 %collective-permute-done.27 = bf16[192,384]{1,0:T(8,128)(2,1)S(1)} collective-permute-done((bf16[192,384]{1,0:T(8,128)(2,1)S(1)}, bf16[192,384]{1,0:T(8,128)(2,1)S(1)}, u32[]{:S(2)}, u32[]{:S(2)}) %collective-permute-start.27) | collective-permute-done | bytes 147488 | tf_op jit(solution)/shard_map/ppermute | solution.py:421
  158.0 0.7 convert_bitcast_fusion
  (47 shorter events, 0.8 us)
Async XLA Ops:
  7.2 2.5 %copy-start.2 = (s32[32]{0:T(128)S(1)}, s32[32]{0:T(128)}, u32[]{:S(2)}) copy-start(s32[32]{0:T(128)} %counts.7) | copy-start | bytes 388
  7.2 63.0 %all-gather.2.cloned.1.call-start = ((), (), s32[]{:S(2)}) async-start(), calls=%async_computation.2 | async-start | bytes 3538944 | tf_op jit(solution)/shard_map/all_gather | solution.py:386
  8.8 46.5 %copy-start.4 = (bf16[6144]{0:T(1024)(128)(2,1)S(1)}, bf16[6144]{0:T(1024)(128)(2,1)}, u32[]{:S(2)}) copy-start(bf16[6144]{0:T(1024)(128)(2,1)} %param.12) | copy-start | bytes 36868
  8.8 46.5 %copy-start = (bf16[1,1024,768]{2,1,0:T(8,128)(2,1)S(1)}, bf16[1,1024,768]{2,1,0:T(8,128)(2,1)}, u32[]{:S(2)}) copy-start(bf16[1,1024,768]{2,1,0:T(8,128)(2,1)} %tokens.1) | copy-start | bytes 4718596
  8.9 46.5 %copy-start.1 = (s32[1,1024]{1,0:T(1,128)S(1)}, s32[1,1024]{1,0:T(1,128)}, u32[]{:S(2)}) copy-start(s32[1,1024]{1,0:T(1,128)} %order.5) | copy-start | bytes 12292
  8.9 8.2 %collective-permute-start = (bf16[2,96,384]{2,1,0:T(8,128)(2,1)S(1)}, bf16[2,96,384]{2,1,0:T(8,128)(2,1)S(1)}, u32[]{:S(2)}, u32[]{:S(2)}) collective-permute-start(bf16[2,96,384]{2,1,0:T(8,128)(2,1)S(1)} %shard_map.120), channel_id=1, source_target_pairs={{0,0},{1,1},{2,2},{3,3},{4,4},{5,5},{6,6},{7,7},{8,12},{9,13},{10,... | collective-permute-start | bytes 442376 | tf_op jit(solution)/shard_map/ppermute | solution.py:189
  17.2 125.6 %reduce-scatter.2.cloned.1.call-start = ((), (), s32[]{:S(2)}) async-start(), calls=%async_computation.3 | async-start | bytes 3538944 | tf_op jit(solution)/shard_map/reduce_scatter | solution.py:407
  17.2 16.4 %collective-permute-start.3 = (bf16[96,384]{1,0:T(8,128)(2,1)S(1)}, bf16[96,384]{1,0:T(8,128)(2,1)S(1)}, u32[]{:S(2)}, u32[]{:S(2)}) collective-permute-start(bf16[96,384]{1,0:T(8,128)(2,1)S(1)} %get-tuple-element.41), channel_id=1, source_target_pairs={{0,128},{8,136},{16,144},{24,152},{32,160},{40,168},{48,176},{56,1... | collective-permute-start | bytes 221192 | tf_op jit(solution)/shard_map/ppermute | solution.py:201
  28.0 6.2 %collective-permute-start.2 = (bf16[96,384]{1,0:T(8,128)(2,1)S(1)}, bf16[96,384]{1,0:T(8,128)(2,1)S(1)}, u32[]{:S(2)}, u32[]{:S(2)}) collective-permute-start(bf16[96,384]{1,0:T(8,128)(2,1)S(1)} %get-tuple-element.41), channel_id=1, source_target_pairs={{0,192},{8,200},{16,208},{24,216},{32,224},{40,232},{48,240},{56,2... | collective-permute-start | bytes 221192 | tf_op jit(solution)/shard_map/ppermute | solution.py:201
  28.6 5.6 %collective-permute-start.1 = (bf16[96,384]{1,0:T(8,128)(2,1)S(1)}, bf16[96,384]{1,0:T(8,128)(2,1)S(1)}, u32[]{:S(2)}, u32[]{:S(2)}) collective-permute-start(bf16[96,384]{1,0:T(8,128)(2,1)S(1)} %get-tuple-element.41), channel_id=1, source_target_pairs={{0,64},{8,72},{16,80},{24,88},{32,96},{40,104},{48,112},{56,120},{... | collective-permute-start | bytes 221192 | tf_op jit(solution)/shard_map/ppermute | solution.py:201
  30.1 5.9 %collective-permute-start.6 = (bf16[96,384]{1,0:T(8,128)(2,1)S(1)}, bf16[96,384]{1,0:T(8,128)(2,1)S(1)}, u32[]{:S(2)}, u32[]{:S(2)}) collective-permute-start(bf16[96,384]{1,0:T(8,128)(2,1)S(1)} %get-tuple-element.42), channel_id=1, source_target_pairs={{0,32},{8,40},{16,48},{24,56},{32,0},{40,8},{48,16},{56,24},{64,96... | collective-permute-start | bytes 221192 | tf_op jit(solution)/shard_map/ppermute | solution.py:201
  32.2 4.5 %collective-permute-start.5 = (bf16[96,384]{1,0:T(8,128)(2,1)S(1)}, bf16[96,384]{1,0:T(8,128)(2,1)S(1)}, u32[]{:S(2)}, u32[]{:S(2)}) collective-permute-start(bf16[96,384]{1,0:T(8,128)(2,1)S(1)} %get-tuple-element.42), channel_id=1, source_target_pairs={{0,48},{8,56},{16,0},{24,8},{32,16},{40,24},{48,32},{56,40},{64,11... | collective-permute-start | bytes 221192 | tf_op jit(solution)/shard_map/ppermute | solution.py:201
  33.6 4.4 %collective-permute-start.4 = (bf16[96,384]{1,0:T(8,128)(2,1)S(1)}, bf16[96,384]{1,0:T(8,128)(2,1)S(1)}, u32[]{:S(2)}, u32[]{:S(2)}) collective-permute-start(bf16[96,384]{1,0:T(8,128)(2,1)S(1)} %get-tuple-element.42), channel_id=1, source_target_pairs={{0,16},{8,24},{16,32},{24,40},{32,48},{40,56},{48,0},{56,8},{64,80... | collective-permute-start | bytes 221192 | tf_op jit(solution)/shard_map/ppermute | solution.py:201
  38.0 6.8 %collective-permute-start.18 = (bf16[4,96,384]{2,1,0:T(8,128)(2,1)S(1)}, bf16[4,96,384]{2,1,0:T(8,128)(2,1)S(1)}, u32[]{:S(2)}, u32[]{:S(2)}) collective-permute-start(bf16[4,96,384]{2,1,0:T(8,128)(2,1)S(1)} %pad_maximum_fusion.1.refs_8_), channel_id=1, source_target_pairs={{0,192},{8,200},{16,208},{24,216},{32,224},{40,232},{48,240},{56,2... | collective-permute-start | bytes 884744 | tf_op jit(solution)/shard_map/ppermute | solution.py:210
  39.9 14.3 %collective-permute-start.16 = (bf16[4,96,384]{2,1,0:T(8,128)(2,1)S(1)}, bf16[4,96,384]{2,1,0:T(8,128)(2,1)S(1)}, u32[]{:S(2)}, u32[]{:S(2)}) collective-permute-start(bf16[4,96,384]{2,1,0:T(8,128)(2,1)S(1)} %pad_maximum_fusion.1.refs_8_), channel_id=1, source_target_pairs={{0,64},{8,72},{16,80},{24,88},{32,96},{40,104},{48,112},{56,120},{... | collective-permute-start | bytes 884744 | tf_op jit(solution)/shard_map/ppermute | solution.py:210
  40.1 14.6 %collective-permute-start.15 = (bf16[4,96,384]{2,1,0:T(8,128)(2,1)S(1)}, bf16[4,96,384]{2,1,0:T(8,128)(2,1)S(1)}, u32[]{:S(2)}, u32[]{:S(2)}) collective-permute-start(bf16[4,96,384]{2,1,0:T(8,128)(2,1)S(1)} %pad_maximum_fusion.1.refs_8_), channel_id=1, source_target_pairs={{0,8},{8,0},{16,24},{24,16},{32,40},{40,32},{48,56},{56,48},{64,72... | collective-permute-start | bytes 884744 | tf_op jit(solution)/shard_map/ppermute | solution.py:213
  40.1 14.7 %collective-permute-start.7 = (bf16[4,96,384]{2,1,0:T(8,128)(2,1)S(1)}, bf16[4,96,384]{2,1,0:T(8,128)(2,1)S(1)}, u32[]{:S(2)}, u32[]{:S(2)}) collective-permute-start(bf16[4,96,384]{2,1,0:T(8,128)(2,1)S(1)} %pad_maximum_fusion.1.refs_8_), channel_id=1, source_target_pairs={{0,128},{8,136},{16,144},{24,152},{32,160},{40,168},{48,176},{56,1... | collective-permute-start | bytes 884744 | tf_op jit(solution)/shard_map/ppermute | solution.py:210
  41.5 16.3 %collective-permute-start.13 = (bf16[4,96,384]{2,1,0:T(8,128)(2,1)S(1)}, bf16[4,96,384]{2,1,0:T(8,128)(2,1)S(1)}, u32[]{:S(2)}, u32[]{:S(2)}) collective-permute-start(bf16[4,96,384]{2,1,0:T(8,128)(2,1)S(1)} %pad_maximum_fusion.refs_0_), channel_id=1, source_target_pairs={{0,32},{8,40},{16,48},{24,56},{32,0},{40,8},{48,16},{56,24},{64,96... | collective-permute-start | bytes 884744 | tf_op jit(solution)/shard_map/ppermute | solution.py:210
  44.8 13.6 %collective-permute-start.11 = (bf16[4,96,384]{2,1,0:T(8,128)(2,1)S(1)}, bf16[4,96,384]{2,1,0:T(8,128)(2,1)S(1)}, u32[]{:S(2)}, u32[]{:S(2)}) collective-permute-start(bf16[4,96,384]{2,1,0:T(8,128)(2,1)S(1)} %pad_maximum_fusion.refs_0_), channel_id=1, source_target_pairs={{0,48},{8,56},{16,0},{24,8},{32,16},{40,24},{48,32},{56,40},{64,11... | collective-permute-start | bytes 884744 | tf_op jit(solution)/shard_map/ppermute | solution.py:210
  54.2 7.1 %collective-permute-start.9 = (bf16[4,96,384]{2,1,0:T(8,128)(2,1)S(1)}, bf16[4,96,384]{2,1,0:T(8,128)(2,1)S(1)}, u32[]{:S(2)}, u32[]{:S(2)}) collective-permute-start(bf16[4,96,384]{2,1,0:T(8,128)(2,1)S(1)} %pad_maximum_fusion.refs_0_), channel_id=1, source_target_pairs={{0,16},{8,24},{16,32},{24,40},{32,48},{40,56},{48,0},{56,8},{64,80... | collective-permute-start | bytes 884744 | tf_op jit(solution)/shard_map/ppermute | solution.py:210
  54.8 6.5 %collective-permute-start.8 = (bf16[4,96,384]{2,1,0:T(8,128)(2,1)S(1)}, bf16[4,96,384]{2,1,0:T(8,128)(2,1)S(1)}, u32[]{:S(2)}, u32[]{:S(2)}) collective-permute-start(bf16[4,96,384]{2,1,0:T(8,128)(2,1)S(1)} %pad_maximum_fusion.refs_0_), channel_id=1, source_target_pairs={{0,8},{8,0},{16,24},{24,16},{32,40},{40,32},{48,56},{56,48},{64,72... | collective-permute-start | bytes 884744 | tf_op jit(solution)/shard_map/ppermute | solution.py:213
  54.8 7.0 %collective-permute-start.19 = (bf16[4,96,384]{2,1,0:T(8,128)(2,1)S(1)}, bf16[4,96,384]{2,1,0:T(8,128)(2,1)S(1)}, u32[]{:S(2)}, u32[]{:S(2)}) collective-permute-start(bf16[4,96,384]{2,1,0:T(8,128)(2,1)S(1)} %collective-permute-done.18.refs_12_), channel_id=1, source_target_pairs={{0,8},{8,0},{16,24},{24,16},{32,40},{40,32},{48,56},{56,48},{64,72... | collective-permute-start | bytes 884744 | tf_op jit(solution)/shard_map/ppermute | solution.py:213
  57.7 4.1 %collective-permute-start.17 = (bf16[4,96,384]{2,1,0:T(8,128)(2,1)S(1)}, bf16[4,96,384]{2,1,0:T(8,128)(2,1)S(1)}, u32[]{:S(2)}, u32[]{:S(2)}) collective-permute-start(bf16[4,96,384]{2,1,0:T(8,128)(2,1)S(1)} %collective-permute-done.16.refs_10_), channel_id=1, source_target_pairs={{0,8},{8,0},{16,24},{24,16},{32,40},{40,32},{48,56},{56,48},{64,72... | collective-permute-start | bytes 884744 | tf_op jit(solution)/shard_map/ppermute | solution.py:213
  58.4 3.4 %collective-permute-start.14 = (bf16[4,96,384]{2,1,0:T(8,128)(2,1)S(1)}, bf16[4,96,384]{2,1,0:T(8,128)(2,1)S(1)}, u32[]{:S(2)}, u32[]{:S(2)}) collective-permute-start(bf16[4,96,384]{2,1,0:T(8,128)(2,1)S(1)} %collective-permute-done.13.refs_6_), channel_id=1, source_target_pairs={{0,8},{8,0},{16,24},{24,16},{32,40},{40,32},{48,56},{56,48},{64,72... | collective-permute-start | bytes 884744 | tf_op jit(solution)/shard_map/ppermute | solution.py:213
  61.2 1.6 collective-permute-start.12
  61.2 2.0 %collective-permute-start.10 = (bf16[4,96,384]{2,1,0:T(8,128)(2,1)S(1)}, bf16[4,96,384]{2,1,0:T(8,128)(2,1)S(1)}, u32[]{:S(2)}, u32[]{:S(2)}) collective-permute-start(bf16[4,96,384]{2,1,0:T(8,128)(2,1)S(1)} %collective-permute-done.9.refs_2_), channel_id=1, source_target_pairs={{0,8},{8,0},{16,24},{24,16},{32,40},{40,32},{48,56},{56,48},{64,72... | collective-permute-start | bytes 884744 | tf_op jit(solution)/shard_map/ppermute | solution.py:213
  61.7 1.9 %collective-permute-start.20 = (bf16[4,96,384]{2,1,0:T(8,128)(2,1)S(1)}, bf16[4,96,384]{2,1,0:T(8,128)(2,1)S(1)}, u32[]{:S(2)}, u32[]{:S(2)}) collective-permute-start(bf16[4,96,384]{2,1,0:T(8,128)(2,1)S(1)} %collective-permute-done.7.refs_14_), channel_id=1, source_target_pairs={{0,8},{8,0},{16,24},{24,16},{32,40},{40,32},{48,56},{56,48},{64,72... | collective-permute-start | bytes 884744 | tf_op jit(solution)/shard_map/ppermute | solution.py:213
  70.2 22.2 %slice-start = ((s8[4718592]{0:T(1024)(128)(4,1)}), s8[4194304]{0:T(1024)(128)(4,1)S(1)}, s32[]{:S(2)}) async-start(s8[4718592]{0:T(1024)(128)(4,1)} %bitcast.24), calls=%async_computation.4 | async-start | bytes 8388608
  70.2 22.2 %slice-start.1 = ((s8[4718592]{0:T(1024)(128)(4,1)}), s8[524288]{0:T(1024)(128)(4,1)S(1)}, s32[]{:S(2)}) async-start(s8[4718592]{0:T(1024)(128)(4,1)} %bitcast.24), calls=%async_computation.5 | async-start | bytes 1048576
  70.2 19.4 %collective-permute-start.25 = (bf16[512,3072]{1,0:T(8,128)(2,1)}, bf16[512,3072]{1,0:T(8,128)(2,1)S(1)}, u32[]{:S(2)}, u32[]{:S(2)}) collective-permute-start(bf16[512,3072]{1,0:T(8,128)(2,1)} %all-gather.2.cloned.1.call-done.mixed.own_mixed), channel_id=1, source_target_pairs={{0,8},{8,0},{16,24},{24,16},{32,40},{40,32},{48,56},{56,48},{64,72... | collective-permute-start | bytes 9437192 | tf_op jit(solution)/shard_map/ppermute | solution.py:399
  77.2 4.7 %collective-permute-start.23 = (f32[8,512]{1,0:T(8,128)S(1)}, f32[8,512]{1,0:T(8,128)S(1)}, u32[]{:S(2)}, u32[]{:S(2)}) collective-permute-start(f32[8,512]{1,0:T(8,128)S(1)} %get-tuple-element.53), channel_id=1, source_target_pairs={{0,2},{1,3},{2,0},{3,1},{4,6},{5,7},{6,4},{7,5},{8,10},{9,11},{10,... | collective-permute-start | bytes 49160 | tf_op jit(solution)/shard_map/ppermute | solution.py:395
  79.0 5.5 %collective-permute-start.22 = (f32[8,512]{1,0:T(8,128)S(1)}, f32[8,512]{1,0:T(8,128)S(1)}, u32[]{:S(2)}, u32[]{:S(2)}) collective-permute-start(f32[8,512]{1,0:T(8,128)S(1)} %get-tuple-element.53), channel_id=1, source_target_pairs={{0,3},{1,2},{2,1},{3,0},{4,7},{5,6},{6,5},{7,4},{8,11},{9,10},{10,... | collective-permute-start | bytes 49160 | tf_op jit(solution)/shard_map/ppermute | solution.py:395
  80.5 4.1 %collective-permute-start.21 = (f32[8,512]{1,0:T(8,128)S(1)}, f32[8,512]{1,0:T(8,128)S(1)}, u32[]{:S(2)}, u32[]{:S(2)}) collective-permute-start(f32[8,512]{1,0:T(8,128)S(1)} %get-tuple-element.53), channel_id=1, source_target_pairs={{0,1},{1,0},{2,3},{3,2},{4,5},{5,4},{6,7},{7,6},{8,9},{9,8},{10,11... | collective-permute-start | bytes 49160 | tf_op jit(solution)/shard_map/ppermute | solution.py:395
  84.6 5.0 %collective-permute-start.24 = (f32[8,512]{1,0:T(8,128)S(1)}, f32[8,512]{1,0:T(8,128)S(1)}, u32[]{:S(2)}, u32[]{:S(2)}) collective-permute-start(f32[8,512]{1,0:T(8,128)S(1)} %add_add_fusion.refs_0_), channel_id=1, source_target_pairs={{0,7},{1,6},{2,5},{3,4},{4,3},{5,2},{6,1},{7,0},{8,15},{9,14},{10,... | collective-permute-start | bytes 49160 | tf_op jit(solution)/shard_map/ppermute | solution.py:395
  89.6 2.7 %copy-start.3 = (bf16[512,3072]{1,0:T(8,128)(2,1)}, bf16[512,3072]{1,0:T(8,128)(2,1)S(1)}, u32[]{:S(2)}) copy-start(bf16[512,3072]{1,0:T(8,128)(2,1)S(1)} %collective-permute-done.25.other_mixed) | copy-start | bytes 9437188
  92.4 4.3 %collective-permute-start.26 = (bf16[512,768]{1,0:T(8,128)(2,1)S(1)}, bf16[512,768]{1,0:T(8,128)(2,1)S(1)}, u32[]{:S(2)}, u32[]{:S(2)}) collective-permute-start(bf16[512,768]{1,0:T(8,128)(2,1)S(1)} %get-tuple-element.56.grad_proj.own_grad), channel_id=1, source_target_pairs={{0,8},{8,0},{16,24},{24,16},{32,40},{40,32},{48,56},{56,48},{64,72... | collective-permute-start | bytes 2359304 | tf_op jit(solution)/shard_map/ppermute | solution.py:405
  140.0 18.1 %collective-permute-start.27 = (bf16[192,384]{1,0:T(8,128)(2,1)S(1)}, bf16[192,384]{1,0:T(8,128)(2,1)S(1)}, u32[]{:S(2)}, u32[]{:S(2)}) collective-permute-start(bf16[192,384]{1,0:T(8,128)(2,1)S(1)} %reduce_sum.12), channel_id=1, source_target_pairs={{0,0},{1,32},{2,64},{3,96},{4,128},{5,160},{6,192},{7,224},{8,4},{... | collective-permute-start | bytes 442376 | tf_op jit(solution)/shard_map/ppermute | solution.py:421
Sparse Core Ops, SparseCore 0:
  17.3 52.8 all-gather.1
  96.8 45.8 reduce-scatter.1

commit v6 on v5

--- a/solution.py
+++ b/solution.py
@@ -48,16 +48,16 @@
 
 def rows_by_token(order_ref, live):
     token = to_column(order_ref[:, :KEEP_MAX].astype(F32)).astype(jnp.int32)
-    row_at = lax.broadcasted_iota(jnp.int32, (KEEP_MAX, P_SIZE), 0)
+    token = jnp.where(lax.broadcasted_iota(jnp.int32, (KEEP_MAX, 1), 0) < live, token, -1)
     token_at = lax.broadcasted_iota(jnp.int32, (KEEP_MAX, P_SIZE), 1)
-    return jnp.where((token == token_at) & (row_at < live), 1.0, 0.0).astype(BF)
+    return jnp.where(token == token_at, 1.0, 0.0).astype(BF)
 
 
 def tokens_by_row(order_ref, live):
     token_at = lax.broadcasted_iota(jnp.int32, (P_SIZE, KEEP_MAX), 0)
-    row_at = lax.broadcasted_iota(jnp.int32, (P_SIZE, KEEP_MAX), 1)
-    hit = (order_ref[:, :KEEP_MAX] == token_at) & (row_at < live)
-    return jnp.where(hit, 1.0, 0.0).astype(BF)
+    row_at = lax.broadcasted_iota(jnp.int32, (1, KEEP_MAX), 1)
+    token = jnp.where(row_at < live, order_ref[:, :KEEP_MAX], -1)
+    return jnp.where(token == token_at, 1.0, 0.0).astype(BF)
 
 
 def dot(a, b, contract):
@@ -79,7 +79,7 @@
     column = lax.broadcasted_iota(jnp.int32, (KEEP_MAX, KEEP_MAX), 1)
     scores = jnp.where(column < live, scores, -1000000000.0)
     exponent = jnp.exp(scores - jnp.max(scores, axis=-1, keepdims=True))
-    w = exponent / jnp.sum(exponent, axis=-1, keepdims=True)
+    w = exponent * (1.0 / jnp.sum(exponent, axis=-1, keepdims=True))
     weight[0] = w
     mixed[...] = dot(w.astype(BF), v, (1, 0)).astype(BF)
 
@@ -391,6 +391,8 @@
     columns = assemble(info, pieces, ranks)
     mixed_all, grad_c, columns = lax.optimization_barrier((mixed_all, grad_c, columns))
     projected, sums = project(info, mixed_all, columns, grad_c, gain)
+    columns, sums = lax.optimization_barrier((columns, sums))
+
     def swapped(values, bits):
         return lax.ppermute(values, "mp", [(m, m ^ bits) for m in range(ranks)])
 

time: 166 us -> 166 us (level)
  transfers between devices with their start and end apart: 30 -> 30, of which waited for: 16 -> 16; matrix products, arithmetic and copies ran while one was open for 0% -> 0% of each run, Pallas kernels for 24% -> 23%
where the time goes in v6:
time: 166 us
  Pallas kernels  43.1 us (26%)
  blocking collectives  37.7 us (23%)
  waiting for transfers between devices  35 us (21%)
  starting transfers between devices  34.3 us (21%)
  between operations  14.3 us (9%)
    pallas_call x9, Pallas kernels, call(): pl.pallas_call(kernel, grid_spec=pltpu.PrefetchScalarGridSpec(num_scalar_...  43.1 us
    all_to_all x1, blocking collectives, on_device(): lax.all_to_all(pair, 'dp', split_axis=0, concat_axis=0, tiled=True, axis_...  37.7 us
    ppermute x6, starting transfers between devices, spread_columns(): lax.ppermute(part, 'dp', along[way][s])  17 us
    ppermute x6, waiting for transfers between devices, spread_columns(): piece = four if s == 0 else lax.ppermute(four, 'dp', along[way][s])  12.2 us
    ppermute x6, starting transfers between devices, spread_columns(): piece = four if s == 0 else lax.ppermute(four, 'dp', along[way][s])  7.58 us
    ppermute x4, waiting for transfers between devices, swapped(): return lax.ppermute(values, 'mp', [(m, m ^ bits) for m in range(ranks)])  7.18 us
    ppermute x1, waiting for transfers between devices, on_device(): total = lax.ppermute(total, ('dp', 'mp'), home)  5.93 us
    ppermute x4, starting transfers between devices, swapped(): return lax.ppermute(values, 'mp', [(m, m ^ bits) for m in range(ranks)])  5.21 us
  transfers between devices with their start and end apart: 30, of which 16 were waited for; matrix products, arithmetic and copies ran while one was open for 0% of the time, Pallas kernels for 23%

profile of v6, /device:TPU:2, one launch (start us, length us, event | category | flops | bytes accessed | tf_op | source)
XLA Modules:
  0.0 165.6 jit_solution(17588671026846390813)
XLA Ops:
  7.4 1.5 shard_map.120
  8.9 0.8 collective-permute-start
  9.7 7.4 %shard_map.119 = (bf16[512,384]{1,0:T(8,128)(2,1)}, bf16[512,384]{1,0:T(8,128)(2,1)}, bf16[512,384]{1,0:T(8,128)(2,1)}, bf16[512,384]{1,0:T(8,128)(2,1)}, f32[3,512,512]{2,1,0:T(8,128)}) custom-call(s32[6]{0:T(128)S(1)} %stack.57.info, s32[32]{0:T(128)S(1)} %copy-done.2, s32[1,1024]{1,0:T(1,128)} %order.5, bf16[1,1024,384]{2,1,0:T(8,128)(2,1)} %query.1, ...), custom_call_target="tpu_custom_call" | custom-call | bytes 4726784 | tf_op jit(solution)/shard_map/pallas_call | solution.py:21
  17.2 10.8 %collective-permute-start.3 = (bf16[96,384]{1,0:T(8,128)(2,1)S(1)}, bf16[96,384]{1,0:T(8,128)(2,1)S(1)}, u32[]{:S(2)}, u32[]{:S(2)}) collective-permute-start(bf16[96,384]{1,0:T(8,128)(2,1)S(1)} %get-tuple-element.43), channel_id=1, source_target_pairs={{0,128},{8,136},{16,144},{24,152},{32,160},{40,168},{48,176},{56,1... | collective-permute-start | bytes 221192 | tf_op jit(solution)/shard_map/ppermute | solution.py:201
  28.0 0.6 collective-permute-start.2
  28.6 1.4 collective-permute-start.1
  30.0 2.1 %collective-permute-start.6 = (bf16[96,384]{1,0:T(8,128)(2,1)S(1)}, bf16[96,384]{1,0:T(8,128)(2,1)S(1)}, u32[]{:S(2)}, u32[]{:S(2)}) collective-permute-start(bf16[96,384]{1,0:T(8,128)(2,1)S(1)} %get-tuple-element.44), channel_id=1, source_target_pairs={{0,32},{8,40},{16,48},{24,56},{32,0},{40,8},{48,16},{56,24},{64,96... | collective-permute-start | bytes 221192 | tf_op jit(solution)/shard_map/ppermute | solution.py:201
  32.2 1.4 collective-permute-start.5
  33.6 0.6 collective-permute-start.4
  34.2 1.7 %collective-permute-done.6 = bf16[96,384]{1,0:T(8,128)(2,1)S(1)} collective-permute-done((bf16[96,384]{1,0:T(8,128)(2,1)S(1)}, bf16[96,384]{1,0:T(8,128)(2,1)S(1)}, u32[]{:S(2)}, u32[]{:S(2)}) %collective-permute-start.6) | collective-permute-done | bytes 73760 | tf_op jit(solution)/shard_map/ppermute | solution.py:201
  35.9 0.8 collective-permute-done.5
  36.7 1.3 collective-permute-done.4
  38.0 1.9 %collective-permute-start.18 = (bf16[4,96,384]{2,1,0:T(8,128)(2,1)S(1)}, bf16[4,96,384]{2,1,0:T(8,128)(2,1)S(1)}, u32[]{:S(2)}, u32[]{:S(2)}) collective-permute-start(bf16[4,96,384]{2,1,0:T(8,128)(2,1)S(1)} %pad_maximum_fusion.1.refs_8_), channel_id=1, source_target_pairs={{0,192},{8,200},{16,208},{24,216},{32,224},{40,232},{48,240},{56,2... | collective-permute-start | bytes 884744 | tf_op jit(solution)/shard_map/ppermute | solution.py:210
  40.1 1.3 collective-permute-start.7
  41.5 1.2 collective-permute-start.13
  42.6 2.2 %collective-permute-done.18.refs_12_ = bf16[4,96,384]{2,1,0:T(8,128)(2,1)S(1)} collective-permute-done((bf16[4,96,384]{2,1,0:T(8,128)(2,1)S(1)}, bf16[4,96,384]{2,1,0:T(8,128)(2,1)S(1)}, u32[]{:S(2)}, u32[]{:S(2)}) %collective-permute-start.18) | collective-permute-done | bytes 294944 | tf_op jit(solution)/shard_map/ppermute | solution.py:210
  44.8 2.4 %collective-permute-start.11 = (bf16[4,96,384]{2,1,0:T(8,128)(2,1)S(1)}, bf16[4,96,384]{2,1,0:T(8,128)(2,1)S(1)}, u32[]{:S(2)}, u32[]{:S(2)}) collective-permute-start(bf16[4,96,384]{2,1,0:T(8,128)(2,1)S(1)} %pad_maximum_fusion.refs_0_), channel_id=1, source_target_pairs={{0,48},{8,56},{16,0},{24,8},{32,16},{40,24},{48,32},{56,40},{64,11... | collective-permute-start | bytes 884744 | tf_op jit(solution)/shard_map/ppermute | solution.py:210
  47.2 7.0 %collective-permute-done.16.refs_10_ = bf16[4,96,384]{2,1,0:T(8,128)(2,1)S(1)} collective-permute-done((bf16[4,96,384]{2,1,0:T(8,128)(2,1)S(1)}, bf16[4,96,384]{2,1,0:T(8,128)(2,1)S(1)}, u32[]{:S(2)}, u32[]{:S(2)}) %collective-permute-start.16) | collective-permute-done | bytes 294944 | tf_op jit(solution)/shard_map/ppermute | solution.py:210
  54.2 0.6 collective-permute-start.9
  54.8 0.5 collective-permute-start.19
  55.3 2.4 %shard_map.121.grad = bf16[512,768]{1,0:T(8,128)(2,1)S(1)} custom-call(s32[6]{0:T(128)S(1)} %stack.57.info, s32[32]{0:T(128)S(1)} %copy-done.2, s32[1,1024]{1,0:T(1,128)S(1)} %copy-done.1, bf16[1,1024,768]{2,1,0:T(8,128)(2,1)S(1)} %copy-done), custom_call_target="tpu_custom_call" | custom-call | bytes 3153920 | tf_op jit(solution)/shard_map/pallas_call | solution.py:21
  57.7 0.4 collective-permute-start.17
  58.1 0.4 collective-permute-done.11.refs_4_
  58.5 2.7 %collective-permute-done.9.refs_2_ = bf16[4,96,384]{2,1,0:T(8,128)(2,1)S(1)} collective-permute-done((bf16[4,96,384]{2,1,0:T(8,128)(2,1)S(1)}, bf16[4,96,384]{2,1,0:T(8,128)(2,1)S(1)}, u32[]{:S(2)}, u32[]{:S(2)}) %collective-permute-start.9) | collective-permute-done | bytes 294944 | tf_op jit(solution)/shard_map/ppermute | solution.py:210
  61.2 0.5 collective-permute-start.10
  61.8 1.0 collective-permute-done.12.refs_5_
  62.8 0.4 collective-permute-done.10.refs_3_
  63.2 0.4 collective-permute-done.20.refs_15_
  63.6 3.2 %shard_map.122 = bf16[8,384,768]{2,1,0:T(8,128)(2,1)} custom-call(s32[6]{0:T(128)S(1)} %stack.57.info, bf16[4,96,384]{2,1,0:T(8,128)(2,1)S(1)} %pad_maximum_fusion.refs_0_, bf16[4,96,384]{2,1,0:T(8,128)(2,1)S(1)} %collective-permute-done.8.refs_1_, bf16[4,96,384]{2,1,0:T(8,128)(2,1)S(1)} %collective-permute-done.9.refs_2_, ...), custom_call_target="tpu_custom_call" | custom-call | bytes 9437184 | tf_op jit(solution)/shard_map/pallas_call | solution.py:21
  66.9 3.3 %all-gather.2.cloned.1.call-done.mixed.own_mixed = bf16[512,3072]{1,0:T(8,128)(2,1)} async-done(((bf16[512,384]{1,0:T(8,128)(2,1)}), bf16[512,3072]{1,0:T(8,128)(2,1)}) %all-gather.2.cloned.1.call-update) | async-done | bytes 3145744 | tf_op jit(solution)/shard_map/all_gather | solution.py:386
  70.2 7.0 %shard_map.123 = (f32[512,768]{1,0:T(8,128)S(1)}, f32[8,512]{1,0:T(8,128)S(1)}) custom-call(s32[6]{0:T(128)S(1)} %stack.57.info, bf16[512,3072]{1,0:T(8,128)(2,1)} %all-gather.2.cloned.1.call-done.mixed.own_mixed, bf16[3072,768]{1,0:T(8,128)(2,1)} %bitcast.23, bf16[512,768]{1,0:T(8,128)(2,1)S(1)} %shard_map.121.grad, bf16[1,6144]{1,0:T(2,128)(2,1)S(1)} %reshape.19.gain), custom_call_target="tpu_custom_call" | custom-call | bytes 17326080 | tf_op jit(solution)/shard_map/pallas_call | solution.py:21
  77.2 1.8 %collective-permute-start.23 = (f32[8,512]{1,0:T(8,128)S(1)}, f32[8,512]{1,0:T(8,128)S(1)}, u32[]{:S(2)}, u32[]{:S(2)}) collective-permute-start(f32[8,512]{1,0:T(8,128)S(1)} %get-tuple-element.56), channel_id=1, source_target_pairs={{0,2},{1,3},{2,0},{3,1},{4,6},{5,7},{6,4},{7,5},{8,10},{9,11},{10,... | collective-permute-start | bytes 49160 | tf_op jit(solution)/shard_map/ppermute | solution.py:397
  79.0 1.5 collective-permute-start.22
  80.5 0.3 collective-permute-start.21
  80.8 1.1 collective-permute-done.23
  82.0 2.6 %collective-permute-done.22 = f32[8,512]{1,0:T(8,128)S(1)} collective-permute-done((f32[8,512]{1,0:T(8,128)S(1)}, f32[8,512]{1,0:T(8,128)S(1)}, u32[]{:S(2)}, u32[]{:S(2)}) %collective-permute-start.22) | collective-permute-done | bytes 16416 | tf_op jit(solution)/shard_map/ppermute | solution.py:397
  84.6 1.6 collective-permute-start.24
  86.2 3.4 %collective-permute-done.24.refs_1_ = f32[8,512]{1,0:T(8,128)S(1)} collective-permute-done((f32[8,512]{1,0:T(8,128)S(1)}, f32[8,512]{1,0:T(8,128)S(1)}, u32[]{:S(2)}, u32[]{:S(2)}) %collective-permute-start.24) | collective-permute-done | bytes 16416 | tf_op jit(solution)/shard_map/ppermute | solution.py:397
  89.6 2.7 %shard_map.124 = (bf16[512,768]{1,0:T(8,128)(2,1)S(1)}, bf16[512,768]{1,0:T(8,128)(2,1)}) custom-call(s32[6]{0:T(128)S(1)} %stack.57.info, s32[32]{0:T(128)S(1)} %copy-done.2, f32[512,768]{1,0:T(8,128)S(1)} %get-tuple-element.54.projected, bf16[512,768]{1,0:T(8,128)(2,1)S(1)} %shard_map.121.grad, bf16[1,6144]{1,0:T(2,128)(2,1)S(1)} %reshape.19.gain, ...), custom_call_target="tpu_custom_call" | custom-call | bytes 4808704 | tf_op jit(solution)/shard_map/pallas_call | solution.py:21
  92.4 4.3 %shard_map.125 = bf16[8,512,384]{2,1,0:T(8,128)(2,1)} custom-call(bf16[512,768]{1,0:T(8,128)(2,1)S(1)} %get-tuple-element.59.grad_proj.own_grad, bf16[3072,768]{1,0:T(8,128)(2,1)S(1)} %bitcast.26), custom_call_target="tpu_custom_call" | custom-call | bytes 11010048 | tf_op jit(solution)/shard_map/pallas_call | solution.py:21
  96.7 5.2 %shard_map.127 = bf16[4,768,384]{2,1,0:T(8,128)(2,1)S(1)} custom-call(s32[6]{0:T(128)S(1)} %stack.57.info, bf16[512,768]{1,0:T(8,128)(2,1)S(1)} %get-tuple-element.59.grad_proj.own_grad, bf16[512,768]{1,0:T(8,128)(2,1)S(1)} %collective-permute-done.26.other_grad, bf16[512,3072]{1,0:T(8,128)(2,1)} %all-gather.2.cloned.1.call-done.mixed.own_mixed, ...), custom_call_target="tpu_custom_call" | custom-call | bytes 15728640 | tf_op jit(solution)/shard_map/pallas_call | solution.py:21
  102.0 37.7 %all_to_all.5 = bf16[16,192,384]{2,1,0:T(8,128)(2,1)S(1)} all-to-all(bf16[16,192,384]{2,1,0:T(8,128)(2,1)S(1)} %bitcast.27), channel_id=1, replica_groups={{0,16,32,48,64,80,96,112,128,144,160,176,192,208,224,240},{8,24,40,56,7..., dimensions={0} | all-to-all | bytes 4718592 | tf_op jit(solution)/shard_map/all_to_all | solution.py:415
  139.6 0.3 reduce_sum.12
  140.0 2.0 %collective-permute-start.27 = (bf16[192,384]{1,0:T(8,128)(2,1)S(1)}, bf16[192,384]{1,0:T(8,128)(2,1)S(1)}, u32[]{:S(2)}, u32[]{:S(2)}) collective-permute-start(bf16[192,384]{1,0:T(8,128)(2,1)S(1)} %reduce_sum.12), channel_id=1, source_target_pairs={{0,0},{1,32},{2,64},{3,96},{4,128},{5,160},{6,192},{7,224},{8,4},{... | collective-permute-start | bytes 442376 | tf_op jit(solution)/shard_map/ppermute | solution.py:423
  142.0 0.8 reduce-scatter.2.cloned.1.call-done
  142.8 9.3 %shard_map.126 = (bf16[1,1024,384]{2,1,0:T(8,128)(2,1)}, bf16[1,1024,384]{2,1,0:T(8,128)(2,1)}, bf16[1,1024,384]{2,1,0:T(8,128)(2,1)}, bf16[1,1024,768]{2,1,0:T(8,128)(2,1)}) custom-call(s32[6]{0:T(128)S(1)} %stack.57.info, s32[32]{0:T(128)S(1)} %copy-done.2, s32[1,1024]{1,0:T(1,128)} %order.5, bf16[512,384]{1,0:T(8,128)(2,1)} %bitcast.28, ...), custom_call_target="tpu_custom_call" | custom-call | bytes 11018240 | tf_op jit(solution)/shard_map/pallas_call | solution.py:21
  152.1 5.9 %collective-permute-done.27 = bf16[192,384]{1,0:T(8,128)(2,1)S(1)} collective-permute-done((bf16[192,384]{1,0:T(8,128)(2,1)S(1)}, bf16[192,384]{1,0:T(8,128)(2,1)S(1)}, u32[]{:S(2)}, u32[]{:S(2)}) %collective-permute-start.27) | collective-permute-done | bytes 147488 | tf_op jit(solution)/shard_map/ppermute | solution.py:423
  158.0 0.7 convert_bitcast_fusion
  (47 shorter events, 0.8 us)
Async XLA Ops:
  7.2 2.5 %copy-start.2 = (s32[32]{0:T(128)S(1)}, s32[32]{0:T(128)}, u32[]{:S(2)}) copy-start(s32[32]{0:T(128)} %counts.7) | copy-start | bytes 388
  7.2 63.0 %all-gather.2.cloned.1.call-start = ((), (), s32[]{:S(2)}) async-start(), calls=%async_computation.2 | async-start | bytes 3538944 | tf_op jit(solution)/shard_map/all_gather | solution.py:386
  8.8 46.4 %copy-start.4 = (bf16[6144]{0:T(1024)(128)(2,1)S(1)}, bf16[6144]{0:T(1024)(128)(2,1)}, u32[]{:S(2)}) copy-start(bf16[6144]{0:T(1024)(128)(2,1)} %param.12) | copy-start | bytes 36868
  8.8 46.5 %copy-start = (bf16[1,1024,768]{2,1,0:T(8,128)(2,1)S(1)}, bf16[1,1024,768]{2,1,0:T(8,128)(2,1)}, u32[]{:S(2)}) copy-start(bf16[1,1024,768]{2,1,0:T(8,128)(2,1)} %tokens.1) | copy-start | bytes 4718596
  8.9 46.4 %copy-start.1 = (s32[1,1024]{1,0:T(1,128)S(1)}, s32[1,1024]{1,0:T(1,128)}, u32[]{:S(2)}) copy-start(s32[1,1024]{1,0:T(1,128)} %order.5) | copy-start | bytes 12292
  8.9 8.2 %collective-permute-start = (bf16[2,96,384]{2,1,0:T(8,128)(2,1)S(1)}, bf16[2,96,384]{2,1,0:T(8,128)(2,1)S(1)}, u32[]{:S(2)}, u32[]{:S(2)}) collective-permute-start(bf16[2,96,384]{2,1,0:T(8,128)(2,1)S(1)} %shard_map.120), channel_id=1, source_target_pairs={{0,0},{1,1},{2,2},{3,3},{4,4},{5,5},{6,6},{7,7},{8,12},{9,13},{10,... | collective-permute-start | bytes 442376 | tf_op jit(solution)/shard_map/ppermute | solution.py:189
  17.1 125.6 %reduce-scatter.2.cloned.1.call-start = ((), (), s32[]{:S(2)}) async-start(), calls=%async_computation.3 | async-start | bytes 3538944 | tf_op jit(solution)/shard_map/reduce_scatter | solution.py:409
  17.2 16.4 %collective-permute-start.3 = (bf16[96,384]{1,0:T(8,128)(2,1)S(1)}, bf16[96,384]{1,0:T(8,128)(2,1)S(1)}, u32[]{:S(2)}, u32[]{:S(2)}) collective-permute-start(bf16[96,384]{1,0:T(8,128)(2,1)S(1)} %get-tuple-element.43), channel_id=1, source_target_pairs={{0,128},{8,136},{16,144},{24,152},{32,160},{40,168},{48,176},{56,1... | collective-permute-start | bytes 221192 | tf_op jit(solution)/shard_map/ppermute | solution.py:201
  28.0 6.2 %collective-permute-start.2 = (bf16[96,384]{1,0:T(8,128)(2,1)S(1)}, bf16[96,384]{1,0:T(8,128)(2,1)S(1)}, u32[]{:S(2)}, u32[]{:S(2)}) collective-permute-start(bf16[96,384]{1,0:T(8,128)(2,1)S(1)} %get-tuple-element.43), channel_id=1, source_target_pairs={{0,192},{8,200},{16,208},{24,216},{32,224},{40,232},{48,240},{56,2... | collective-permute-start | bytes 221192 | tf_op jit(solution)/shard_map/ppermute | solution.py:201
  28.6 5.6 %collective-permute-start.1 = (bf16[96,384]{1,0:T(8,128)(2,1)S(1)}, bf16[96,384]{1,0:T(8,128)(2,1)S(1)}, u32[]{:S(2)}, u32[]{:S(2)}) collective-permute-start(bf16[96,384]{1,0:T(8,128)(2,1)S(1)} %get-tuple-element.43), channel_id=1, source_target_pairs={{0,64},{8,72},{16,80},{24,88},{32,96},{40,104},{48,112},{56,120},{... | collective-permute-start | bytes 221192 | tf_op jit(solution)/shard_map/ppermute | solution.py:201
  30.0 5.9 %collective-permute-start.6 = (bf16[96,384]{1,0:T(8,128)(2,1)S(1)}, bf16[96,384]{1,0:T(8,128)(2,1)S(1)}, u32[]{:S(2)}, u32[]{:S(2)}) collective-permute-start(bf16[96,384]{1,0:T(8,128)(2,1)S(1)} %get-tuple-element.44), channel_id=1, source_target_pairs={{0,32},{8,40},{16,48},{24,56},{32,0},{40,8},{48,16},{56,24},{64,96... | collective-permute-start | bytes 221192 | tf_op jit(solution)/shard_map/ppermute | solution.py:201
  32.2 4.5 %collective-permute-start.5 = (bf16[96,384]{1,0:T(8,128)(2,1)S(1)}, bf16[96,384]{1,0:T(8,128)(2,1)S(1)}, u32[]{:S(2)}, u32[]{:S(2)}) collective-permute-start(bf16[96,384]{1,0:T(8,128)(2,1)S(1)} %get-tuple-element.44), channel_id=1, source_target_pairs={{0,48},{8,56},{16,0},{24,8},{32,16},{40,24},{48,32},{56,40},{64,11... | collective-permute-start | bytes 221192 | tf_op jit(solution)/shard_map/ppermute | solution.py:201
  33.6 4.4 %collective-permute-start.4 = (bf16[96,384]{1,0:T(8,128)(2,1)S(1)}, bf16[96,384]{1,0:T(8,128)(2,1)S(1)}, u32[]{:S(2)}, u32[]{:S(2)}) collective-permute-start(bf16[96,384]{1,0:T(8,128)(2,1)S(1)} %get-tuple-element.44), channel_id=1, source_target_pairs={{0,16},{8,24},{16,32},{24,40},{32,48},{40,56},{48,0},{56,8},{64,80... | collective-permute-start | bytes 221192 | tf_op jit(solution)/shard_map/ppermute | solution.py:201
  38.0 6.8 %collective-permute-start.18 = (bf16[4,96,384]{2,1,0:T(8,128)(2,1)S(1)}, bf16[4,96,384]{2,1,0:T(8,128)(2,1)S(1)}, u32[]{:S(2)}, u32[]{:S(2)}) collective-permute-start(bf16[4,96,384]{2,1,0:T(8,128)(2,1)S(1)} %pad_maximum_fusion.1.refs_8_), channel_id=1, source_target_pairs={{0,192},{8,200},{16,208},{24,216},{32,224},{40,232},{48,240},{56,2... | collective-permute-start | bytes 884744 | tf_op jit(solution)/shard_map/ppermute | solution.py:210
  39.9 14.3 %collective-permute-start.16 = (bf16[4,96,384]{2,1,0:T(8,128)(2,1)S(1)}, bf16[4,96,384]{2,1,0:T(8,128)(2,1)S(1)}, u32[]{:S(2)}, u32[]{:S(2)}) collective-permute-start(bf16[4,96,384]{2,1,0:T(8,128)(2,1)S(1)} %pad_maximum_fusion.1.refs_8_), channel_id=1, source_target_pairs={{0,64},{8,72},{16,80},{24,88},{32,96},{40,104},{48,112},{56,120},{... | collective-permute-start | bytes 884744 | tf_op jit(solution)/shard_map/ppermute | solution.py:210
  40.1 14.6 %collective-permute-start.15 = (bf16[4,96,384]{2,1,0:T(8,128)(2,1)S(1)}, bf16[4,96,384]{2,1,0:T(8,128)(2,1)S(1)}, u32[]{:S(2)}, u32[]{:S(2)}) collective-permute-start(bf16[4,96,384]{2,1,0:T(8,128)(2,1)S(1)} %pad_maximum_fusion.1.refs_8_), channel_id=1, source_target_pairs={{0,8},{8,0},{16,24},{24,16},{32,40},{40,32},{48,56},{56,48},{64,72... | collective-permute-start | bytes 884744 | tf_op jit(solution)/shard_map/ppermute | solution.py:213
  40.1 14.6 %collective-permute-start.7 = (bf16[4,96,384]{2,1,0:T(8,128)(2,1)S(1)}, bf16[4,96,384]{2,1,0:T(8,128)(2,1)S(1)}, u32[]{:S(2)}, u32[]{:S(2)}) collective-permute-start(bf16[4,96,384]{2,1,0:T(8,128)(2,1)S(1)} %pad_maximum_fusion.1.refs_8_), channel_id=1, source_target_pairs={{0,128},{8,136},{16,144},{24,152},{32,160},{40,168},{48,176},{56,1... | collective-permute-start | bytes 884744 | tf_op jit(solution)/shard_map/ppermute | solution.py:210
  41.5 16.2 %collective-permute-start.13 = (bf16[4,96,384]{2,1,0:T(8,128)(2,1)S(1)}, bf16[4,96,384]{2,1,0:T(8,128)(2,1)S(1)}, u32[]{:S(2)}, u32[]{:S(2)}) collective-permute-start(bf16[4,96,384]{2,1,0:T(8,128)(2,1)S(1)} %pad_maximum_fusion.refs_0_), channel_id=1, source_target_pairs={{0,32},{8,40},{16,48},{24,56},{32,0},{40,8},{48,16},{56,24},{64,96... | collective-permute-start | bytes 884744 | tf_op jit(solution)/shard_map/ppermute | solution.py:210
  44.8 13.6 %collective-permute-start.11 = (bf16[4,96,384]{2,1,0:T(8,128)(2,1)S(1)}, bf16[4,96,384]{2,1,0:T(8,128)(2,1)S(1)}, u32[]{:S(2)}, u32[]{:S(2)}) collective-permute-start(bf16[4,96,384]{2,1,0:T(8,128)(2,1)S(1)} %pad_maximum_fusion.refs_0_), channel_id=1, source_target_pairs={{0,48},{8,56},{16,0},{24,8},{32,16},{40,24},{48,32},{56,40},{64,11... | collective-permute-start | bytes 884744 | tf_op jit(solution)/shard_map/ppermute | solution.py:210
  54.2 7.1 %collective-permute-start.9 = (bf16[4,96,384]{2,1,0:T(8,128)(2,1)S(1)}, bf16[4,96,384]{2,1,0:T(8,128)(2,1)S(1)}, u32[]{:S(2)}, u32[]{:S(2)}) collective-permute-start(bf16[4,96,384]{2,1,0:T(8,128)(2,1)S(1)} %pad_maximum_fusion.refs_0_), channel_id=1, source_target_pairs={{0,16},{8,24},{16,32},{24,40},{32,48},{40,56},{48,0},{56,8},{64,80... | collective-permute-start | bytes 884744 | tf_op jit(solution)/shard_map/ppermute | solution.py:210
  54.8 6.5 %collective-permute-start.8 = (bf16[4,96,384]{2,1,0:T(8,128)(2,1)S(1)}, bf16[4,96,384]{2,1,0:T(8,128)(2,1)S(1)}, u32[]{:S(2)}, u32[]{:S(2)}) collective-permute-start(bf16[4,96,384]{2,1,0:T(8,128)(2,1)S(1)} %pad_maximum_fusion.refs_0_), channel_id=1, source_target_pairs={{0,8},{8,0},{16,24},{24,16},{32,40},{40,32},{48,56},{56,48},{64,72... | collective-permute-start | bytes 884744 | tf_op jit(solution)/shard_map/ppermute | solution.py:213
  54.8 7.0 %collective-permute-start.19 = (bf16[4,96,384]{2,1,0:T(8,128)(2,1)S(1)}, bf16[4,96,384]{2,1,0:T(8,128)(2,1)S(1)}, u32[]{:S(2)}, u32[]{:S(2)}) collective-permute-start(bf16[4,96,384]{2,1,0:T(8,128)(2,1)S(1)} %collective-permute-done.18.refs_12_), channel_id=1, source_target_pairs={{0,8},{8,0},{16,24},{24,16},{32,40},{40,32},{48,56},{56,48},{64,72... | collective-permute-start | bytes 884744 | tf_op jit(solution)/shard_map/ppermute | solution.py:213
  57.7 4.1 %collective-permute-start.17 = (bf16[4,96,384]{2,1,0:T(8,128)(2,1)S(1)}, bf16[4,96,384]{2,1,0:T(8,128)(2,1)S(1)}, u32[]{:S(2)}, u32[]{:S(2)}) collective-permute-start(bf16[4,96,384]{2,1,0:T(8,128)(2,1)S(1)} %collective-permute-done.16.refs_10_), channel_id=1, source_target_pairs={{0,8},{8,0},{16,24},{24,16},{32,40},{40,32},{48,56},{56,48},{64,72... | collective-permute-start | bytes 884744 | tf_op jit(solution)/shard_map/ppermute | solution.py:213
  58.4 3.4 %collective-permute-start.14 = (bf16[4,96,384]{2,1,0:T(8,128)(2,1)S(1)}, bf16[4,96,384]{2,1,0:T(8,128)(2,1)S(1)}, u32[]{:S(2)}, u32[]{:S(2)}) collective-permute-start(bf16[4,96,384]{2,1,0:T(8,128)(2,1)S(1)} %collective-permute-done.13.refs_6_), channel_id=1, source_target_pairs={{0,8},{8,0},{16,24},{24,16},{32,40},{40,32},{48,56},{56,48},{64,72... | collective-permute-start | bytes 884744 | tf_op jit(solution)/shard_map/ppermute | solution.py:213
  61.2 1.6 collective-permute-start.12
  61.2 2.0 %collective-permute-start.10 = (bf16[4,96,384]{2,1,0:T(8,128)(2,1)S(1)}, bf16[4,96,384]{2,1,0:T(8,128)(2,1)S(1)}, u32[]{:S(2)}, u32[]{:S(2)}) collective-permute-start(bf16[4,96,384]{2,1,0:T(8,128)(2,1)S(1)} %collective-permute-done.9.refs_2_), channel_id=1, source_target_pairs={{0,8},{8,0},{16,24},{24,16},{32,40},{40,32},{48,56},{56,48},{64,72... | collective-permute-start | bytes 884744 | tf_op jit(solution)/shard_map/ppermute | solution.py:213
  61.7 1.9 %collective-permute-start.20 = (bf16[4,96,384]{2,1,0:T(8,128)(2,1)S(1)}, bf16[4,96,384]{2,1,0:T(8,128)(2,1)S(1)}, u32[]{:S(2)}, u32[]{:S(2)}) collective-permute-start(bf16[4,96,384]{2,1,0:T(8,128)(2,1)S(1)} %collective-permute-done.7.refs_14_), channel_id=1, source_target_pairs={{0,8},{8,0},{16,24},{24,16},{32,40},{40,32},{48,56},{56,48},{64,72... | collective-permute-start | bytes 884744 | tf_op jit(solution)/shard_map/ppermute | solution.py:213
  70.2 22.2 %slice-start = ((s8[4718592]{0:T(1024)(128)(4,1)}), s8[4194304]{0:T(1024)(128)(4,1)S(1)}, s32[]{:S(2)}) async-start(s8[4718592]{0:T(1024)(128)(4,1)} %bitcast.24), calls=%async_computation.4 | async-start | bytes 8388608
  70.2 22.2 %slice-start.1 = ((s8[4718592]{0:T(1024)(128)(4,1)}), s8[524288]{0:T(1024)(128)(4,1)S(1)}, s32[]{:S(2)}) async-start(s8[4718592]{0:T(1024)(128)(4,1)} %bitcast.24), calls=%async_computation.5 | async-start | bytes 1048576
  70.2 19.4 %collective-permute-start.25 = (bf16[512,3072]{1,0:T(8,128)(2,1)}, bf16[512,3072]{1,0:T(8,128)(2,1)S(1)}, u32[]{:S(2)}, u32[]{:S(2)}) collective-permute-start(bf16[512,3072]{1,0:T(8,128)(2,1)} %all-gather.2.cloned.1.call-done.mixed.own_mixed), channel_id=1, source_target_pairs={{0,8},{8,0},{16,24},{24,16},{32,40},{40,32},{48,56},{56,48},{64,72... | collective-permute-start | bytes 9437192 | tf_op jit(solution)/shard_map/ppermute | solution.py:401
  77.2 4.7 %collective-permute-start.23 = (f32[8,512]{1,0:T(8,128)S(1)}, f32[8,512]{1,0:T(8,128)S(1)}, u32[]{:S(2)}, u32[]{:S(2)}) collective-permute-start(f32[8,512]{1,0:T(8,128)S(1)} %get-tuple-element.56), channel_id=1, source_target_pairs={{0,2},{1,3},{2,0},{3,1},{4,6},{5,7},{6,4},{7,5},{8,10},{9,11},{10,... | collective-permute-start | bytes 49160 | tf_op jit(solution)/shard_map/ppermute | solution.py:397
  79.0 5.5 %collective-permute-start.22 = (f32[8,512]{1,0:T(8,128)S(1)}, f32[8,512]{1,0:T(8,128)S(1)}, u32[]{:S(2)}, u32[]{:S(2)}) collective-permute-start(f32[8,512]{1,0:T(8,128)S(1)} %get-tuple-element.56), channel_id=1, source_target_pairs={{0,3},{1,2},{2,1},{3,0},{4,7},{5,6},{6,5},{7,4},{8,11},{9,10},{10,... | collective-permute-start | bytes 49160 | tf_op jit(solution)/shard_map/ppermute | solution.py:397
  80.5 4.1 %collective-permute-start.21 = (f32[8,512]{1,0:T(8,128)S(1)}, f32[8,512]{1,0:T(8,128)S(1)}, u32[]{:S(2)}, u32[]{:S(2)}) collective-permute-start(f32[8,512]{1,0:T(8,128)S(1)} %get-tuple-element.56), channel_id=1, source_target_pairs={{0,1},{1,0},{2,3},{3,2},{4,5},{5,4},{6,7},{7,6},{8,9},{9,8},{10,11... | collective-permute-start | bytes 49160 | tf_op jit(solution)/shard_map/ppermute | solution.py:397
  84.6 5.0 %collective-permute-start.24 = (f32[8,512]{1,0:T(8,128)S(1)}, f32[8,512]{1,0:T(8,128)S(1)}, u32[]{:S(2)}, u32[]{:S(2)}) collective-permute-start(f32[8,512]{1,0:T(8,128)S(1)} %add_add_fusion.refs_0_), channel_id=1, source_target_pairs={{0,7},{1,6},{2,5},{3,4},{4,3},{5,2},{6,1},{7,0},{8,15},{9,14},{10,... | collective-permute-start | bytes 49160 | tf_op jit(solution)/shard_map/ppermute | solution.py:397
  89.6 2.7 %copy-start.3 = (bf16[512,3072]{1,0:T(8,128)(2,1)}, bf16[512,3072]{1,0:T(8,128)(2,1)S(1)}, u32[]{:S(2)}) copy-start(bf16[512,3072]{1,0:T(8,128)(2,1)S(1)} %collective-permute-done.25.other_mixed) | copy-start | bytes 9437188
  92.4 4.3 %collective-permute-start.26 = (bf16[512,768]{1,0:T(8,128)(2,1)S(1)}, bf16[512,768]{1,0:T(8,128)(2,1)S(1)}, u32[]{:S(2)}, u32[]{:S(2)}) collective-permute-start(bf16[512,768]{1,0:T(8,128)(2,1)S(1)} %get-tuple-element.59.grad_proj.own_grad), channel_id=1, source_target_pairs={{0,8},{8,0},{16,24},{24,16},{32,40},{40,32},{48,56},{56,48},{64,72... | collective-permute-start | bytes 2359304 | tf_op jit(solution)/shard_map/ppermute | solution.py:407
  140.0 18.1 %collective-permute-start.27 = (bf16[192,384]{1,0:T(8,128)(2,1)S(1)}, bf16[192,384]{1,0:T(8,128)(2,1)S(1)}, u32[]{:S(2)}, u32[]{:S(2)}) collective-permute-start(bf16[192,384]{1,0:T(8,128)(2,1)S(1)} %reduce_sum.12), channel_id=1, source_target_pairs={{0,0},{1,32},{2,64},{3,96},{4,128},{5,160},{6,192},{7,224},{8,4},{... | collective-permute-start | bytes 442376 | tf_op jit(solution)/shard_map/ppermute | solution.py:423
Sparse Core Ops, SparseCore 0:
  17.3 52.8 all-gather.1
  96.8 45.8 reduce-scatter.1

commit v7 on v5

--- a/solution.py
+++ b/solution.py
@@ -330,7 +330,7 @@
         [pl.BlockSpec((KEEP_MAX, width), lambda k: (0, 0)), pl.BlockSpec((block, width), lambda k: (k, 0))],
         pl.BlockSpec((2, KEEP_MAX, block // 2), lambda k: (k, 0, 0)),
         pltpu.HBM((depth * 2 // block, KEEP_MAX, block // 2), BF),
-        [], grad_proj, in_vmem(weight), vmem=12,
+        [], grad_proj, in_hbm(weight), vmem=12,
     )
 
 

time: 166 us -> 167 us (level)
  no operation moved by 1% of the time
where the time goes in v7:
time: 167 us
  Pallas kernels  44.5 us (27%)
  blocking collectives  37.7 us (23%)
  waiting for transfers between devices  34.9 us (21%)
  starting transfers between devices  34.4 us (21%)
  between operations  14.2 us (9%)
    pallas_call x9, Pallas kernels, call(): pl.pallas_call(kernel, grid_spec=pltpu.PrefetchScalarGridSpec(num_scalar_...  44.5 us
    all_to_all x1, blocking collectives, on_device(): lax.all_to_all(pair, 'dp', split_axis=0, concat_axis=0, tiled=True, axis_...  37.7 us
    ppermute x6, starting transfers between devices, spread_columns(): lax.ppermute(part, 'dp', along[way][s])  17 us
    ppermute x6, waiting for transfers between devices, spread_columns(): piece = four if s == 0 else lax.ppermute(four, 'dp', along[way][s])  12.2 us
    ppermute x6, starting transfers between devices, spread_columns(): piece = four if s == 0 else lax.ppermute(four, 'dp', along[way][s])  7.59 us
    ppermute x4, waiting for transfers between devices, swapped(): return lax.ppermute(values, 'mp', [(m, m ^ bits) for m in range(ranks)])  7.18 us
    ppermute x1, waiting for transfers between devices, on_device(): total = lax.ppermute(total, ('dp', 'mp'), home)  6.14 us
    ppermute x4, starting transfers between devices, swapped(): return lax.ppermute(values, 'mp', [(m, m ^ bits) for m in range(ranks)])  5.21 us
  transfers between devices with their start and end apart: 30, of which 16 were waited for; matrix products, arithmetic and copies ran while one was open for 0% of the time, Pallas kernels for 24%

profile of v7, /device:TPU:2, one launch (start us, length us, event | category | flops | bytes accessed | tf_op | source)
XLA Modules:
  0.0 167.0 jit_solution(7204838755766997497)
XLA Ops:
  7.4 1.5 shard_map.120
  8.9 0.8 collective-permute-start
  9.7 7.4 %shard_map.119 = (bf16[512,384]{1,0:T(8,128)(2,1)}, bf16[512,384]{1,0:T(8,128)(2,1)}, bf16[512,384]{1,0:T(8,128)(2,1)}, bf16[512,384]{1,0:T(8,128)(2,1)}, f32[3,512,512]{2,1,0:T(8,128)}) custom-call(s32[6]{0:T(128)S(1)} %stack.57.info, s32[32]{0:T(128)S(1)} %copy-done.2, s32[1,1024]{1,0:T(1,128)} %order.5, bf16[1,1024,384]{2,1,0:T(8,128)(2,1)} %query.1, ...), custom_call_target="tpu_custom_call" | custom-call | bytes 4726784 | tf_op jit(solution)/shard_map/pallas_call | solution.py:21
  17.2 10.8 %collective-permute-start.3 = (bf16[96,384]{1,0:T(8,128)(2,1)S(1)}, bf16[96,384]{1,0:T(8,128)(2,1)S(1)}, u32[]{:S(2)}, u32[]{:S(2)}) collective-permute-start(bf16[96,384]{1,0:T(8,128)(2,1)S(1)} %get-tuple-element.41), channel_id=1, source_target_pairs={{0,128},{8,136},{16,144},{24,152},{32,160},{40,168},{48,176},{56,1... | collective-permute-start | bytes 221192 | tf_op jit(solution)/shard_map/ppermute | solution.py:201
  28.0 0.6 collective-permute-start.2
  28.6 1.4 collective-permute-start.1
  30.0 2.1 %collective-permute-start.6 = (bf16[96,384]{1,0:T(8,128)(2,1)S(1)}, bf16[96,384]{1,0:T(8,128)(2,1)S(1)}, u32[]{:S(2)}, u32[]{:S(2)}) collective-permute-start(bf16[96,384]{1,0:T(8,128)(2,1)S(1)} %get-tuple-element.42), channel_id=1, source_target_pairs={{0,32},{8,40},{16,48},{24,56},{32,0},{40,8},{48,16},{56,24},{64,96... | collective-permute-start | bytes 221192 | tf_op jit(solution)/shard_map/ppermute | solution.py:201
  32.2 1.4 collective-permute-start.5
  33.6 0.6 collective-permute-start.4
  34.3 1.7 collective-permute-done.6
  35.9 0.8 collective-permute-done.5
  36.7 1.3 collective-permute-done.4
  38.0 1.9 %collective-permute-start.18 = (bf16[4,96,384]{2,1,0:T(8,128)(2,1)S(1)}, bf16[4,96,384]{2,1,0:T(8,128)(2,1)S(1)}, u32[]{:S(2)}, u32[]{:S(2)}) collective-permute-start(bf16[4,96,384]{2,1,0:T(8,128)(2,1)S(1)} %pad_maximum_fusion.1.refs_8_), channel_id=1, source_target_pairs={{0,192},{8,200},{16,208},{24,216},{32,224},{40,232},{48,240},{56,2... | collective-permute-start | bytes 884744 | tf_op jit(solution)/shard_map/ppermute | solution.py:210
  40.1 1.3 collective-permute-start.7
  41.5 1.2 collective-permute-start.13
  42.7 2.2 %collective-permute-done.18.refs_12_ = bf16[4,96,384]{2,1,0:T(8,128)(2,1)S(1)} collective-permute-done((bf16[4,96,384]{2,1,0:T(8,128)(2,1)S(1)}, bf16[4,96,384]{2,1,0:T(8,128)(2,1)S(1)}, u32[]{:S(2)}, u32[]{:S(2)}) %collective-permute-start.18) | collective-permute-done | bytes 294944 | tf_op jit(solution)/shard_map/ppermute | solution.py:210
  44.8 2.4 %collective-permute-start.11 = (bf16[4,96,384]{2,1,0:T(8,128)(2,1)S(1)}, bf16[4,96,384]{2,1,0:T(8,128)(2,1)S(1)}, u32[]{:S(2)}, u32[]{:S(2)}) collective-permute-start(bf16[4,96,384]{2,1,0:T(8,128)(2,1)S(1)} %pad_maximum_fusion.refs_0_), channel_id=1, source_target_pairs={{0,48},{8,56},{16,0},{24,8},{32,16},{40,24},{48,32},{56,40},{64,11... | collective-permute-start | bytes 884744 | tf_op jit(solution)/shard_map/ppermute | solution.py:210
  47.2 7.0 %collective-permute-done.16.refs_10_ = bf16[4,96,384]{2,1,0:T(8,128)(2,1)S(1)} collective-permute-done((bf16[4,96,384]{2,1,0:T(8,128)(2,1)S(1)}, bf16[4,96,384]{2,1,0:T(8,128)(2,1)S(1)}, u32[]{:S(2)}, u32[]{:S(2)}) %collective-permute-start.16) | collective-permute-done | bytes 294944 | tf_op jit(solution)/shard_map/ppermute | solution.py:210
  54.2 0.6 collective-permute-start.9
  54.8 0.5 collective-permute-start.19
  55.3 2.4 %shard_map.121.grad = bf16[512,768]{1,0:T(8,128)(2,1)S(1)} custom-call(s32[6]{0:T(128)S(1)} %stack.57.info, s32[32]{0:T(128)S(1)} %copy-done.2, s32[1,1024]{1,0:T(1,128)S(1)} %copy-done.1, bf16[1,1024,768]{2,1,0:T(8,128)(2,1)S(1)} %copy-done), custom_call_target="tpu_custom_call" | custom-call | bytes 3153920 | tf_op jit(solution)/shard_map/pallas_call | solution.py:21
  57.7 0.4 collective-permute-start.17
  58.1 0.3 collective-permute-done.11.refs_4_
  58.6 2.7 %collective-permute-done.9.refs_2_ = bf16[4,96,384]{2,1,0:T(8,128)(2,1)S(1)} collective-permute-done((bf16[4,96,384]{2,1,0:T(8,128)(2,1)S(1)}, bf16[4,96,384]{2,1,0:T(8,128)(2,1)S(1)}, u32[]{:S(2)}, u32[]{:S(2)}) %collective-permute-start.9) | collective-permute-done | bytes 294944 | tf_op jit(solution)/shard_map/ppermute | solution.py:210
  61.2 0.5 collective-permute-start.10
  61.8 1.0 collective-permute-done.12.refs_5_
  62.8 0.4 collective-permute-done.10.refs_3_
  63.2 0.4 collective-permute-done.20.refs_15_
  63.6 3.2 %shard_map.122 = bf16[8,384,768]{2,1,0:T(8,128)(2,1)} custom-call(s32[6]{0:T(128)S(1)} %stack.57.info, bf16[4,96,384]{2,1,0:T(8,128)(2,1)S(1)} %pad_maximum_fusion.refs_0_, bf16[4,96,384]{2,1,0:T(8,128)(2,1)S(1)} %collective-permute-done.8.refs_1_, bf16[4,96,384]{2,1,0:T(8,128)(2,1)S(1)} %collective-permute-done.9.refs_2_, ...), custom_call_target="tpu_custom_call" | custom-call | bytes 9437184 | tf_op jit(solution)/shard_map/pallas_call | solution.py:21
  66.9 3.3 %all-gather.2.cloned.1.call-done.mixed.own_mixed = bf16[512,3072]{1,0:T(8,128)(2,1)} async-done(((bf16[512,384]{1,0:T(8,128)(2,1)}), bf16[512,3072]{1,0:T(8,128)(2,1)}) %all-gather.2.cloned.1.call-update) | async-done | bytes 3145744 | tf_op jit(solution)/shard_map/all_gather | solution.py:386
  70.2 6.3 %shard_map.123 = (f32[512,768]{1,0:T(8,128)S(1)}, f32[8,512]{1,0:T(8,128)S(1)}) custom-call(s32[6]{0:T(128)S(1)} %stack.57.info, bf16[512,3072]{1,0:T(8,128)(2,1)} %all-gather.2.cloned.1.call-done.mixed.own_mixed, bf16[3072,768]{1,0:T(8,128)(2,1)} %bitcast.24, bf16[512,768]{1,0:T(8,128)(2,1)S(1)} %shard_map.121.grad, bf16[1,6144]{1,0:T(2,128)(2,1)S(1)} %reshape.19.gain), custom_call_target="tpu_custom_call" | custom-call | bytes 17326080 | tf_op jit(solution)/shard_map/pallas_call | solution.py:21
  76.5 1.8 %collective-permute-start.23 = (f32[8,512]{1,0:T(8,128)S(1)}, f32[8,512]{1,0:T(8,128)S(1)}, u32[]{:S(2)}, u32[]{:S(2)}) collective-permute-start(f32[8,512]{1,0:T(8,128)S(1)} %get-tuple-element.53), channel_id=1, source_target_pairs={{0,2},{1,3},{2,0},{3,1},{4,6},{5,7},{6,4},{7,5},{8,10},{9,11},{10,... | collective-permute-start | bytes 49160 | tf_op jit(solution)/shard_map/ppermute | solution.py:395
  78.3 1.5 collective-permute-start.22
  79.8 0.3 collective-permute-start.21
  80.1 1.1 collective-permute-done.23
  81.2 2.6 %collective-permute-done.22 = f32[8,512]{1,0:T(8,128)S(1)} collective-permute-done((f32[8,512]{1,0:T(8,128)S(1)}, f32[8,512]{1,0:T(8,128)S(1)}, u32[]{:S(2)}, u32[]{:S(2)}) %collective-permute-start.22) | collective-permute-done | bytes 16416 | tf_op jit(solution)/shard_map/ppermute | solution.py:395
  83.9 1.6 collective-permute-start.24
  85.5 3.4 %collective-permute-done.24.refs_1_ = f32[8,512]{1,0:T(8,128)S(1)} collective-permute-done((f32[8,512]{1,0:T(8,128)S(1)}, f32[8,512]{1,0:T(8,128)S(1)}, u32[]{:S(2)}, u32[]{:S(2)}) %collective-permute-start.24) | collective-permute-done | bytes 16416 | tf_op jit(solution)/shard_map/ppermute | solution.py:395
  88.9 2.8 %shard_map.124 = (bf16[512,768]{1,0:T(8,128)(2,1)S(1)}, bf16[512,768]{1,0:T(8,128)(2,1)}) custom-call(s32[6]{0:T(128)S(1)} %stack.57.info, s32[32]{0:T(128)S(1)} %copy-done.2, f32[512,768]{1,0:T(8,128)S(1)} %get-tuple-element.52.projected, bf16[512,768]{1,0:T(8,128)(2,1)S(1)} %shard_map.121.grad, bf16[1,6144]{1,0:T(2,128)(2,1)S(1)} %reshape.19.gain, ...), custom_call_target="tpu_custom_call" | custom-call | bytes 4808704 | tf_op jit(solution)/shard_map/pallas_call | solution.py:21
  91.7 6.3 %shard_map.125 = bf16[8,512,384]{2,1,0:T(8,128)(2,1)} custom-call(bf16[512,768]{1,0:T(8,128)(2,1)S(1)} %get-tuple-element.56.grad_proj.own_grad, bf16[3072,768]{1,0:T(8,128)(2,1)} %bitcast.25), custom_call_target="tpu_custom_call" | custom-call | bytes 11010048 | tf_op jit(solution)/shard_map/pallas_call | solution.py:21
  98.0 5.2 %shard_map.127 = bf16[4,768,384]{2,1,0:T(8,128)(2,1)S(1)} custom-call(s32[6]{0:T(128)S(1)} %stack.57.info, bf16[512,768]{1,0:T(8,128)(2,1)S(1)} %get-tuple-element.56.grad_proj.own_grad, bf16[512,768]{1,0:T(8,128)(2,1)S(1)} %collective-permute-done.26.other_grad, bf16[512,3072]{1,0:T(8,128)(2,1)} %all-gather.2.cloned.1.call-done.mixed.own_mixed, ...), custom_call_target="tpu_custom_call" | custom-call | bytes 15728640 | tf_op jit(solution)/shard_map/pallas_call | solution.py:21
  103.3 37.7 %all_to_all.5 = bf16[16,192,384]{2,1,0:T(8,128)(2,1)S(1)} all-to-all(bf16[16,192,384]{2,1,0:T(8,128)(2,1)S(1)} %bitcast.23), channel_id=1, replica_groups={{0,16,32,48,64,80,96,112,128,144,160,176,192,208,224,240},{8,24,40,56,7..., dimensions={0} | all-to-all | bytes 4718592 | tf_op jit(solution)/shard_map/all_to_all | solution.py:413
  141.0 0.3 reduce_sum.12
  141.3 2.1 %collective-permute-start.27 = (bf16[192,384]{1,0:T(8,128)(2,1)S(1)}, bf16[192,384]{1,0:T(8,128)(2,1)S(1)}, u32[]{:S(2)}, u32[]{:S(2)}) collective-permute-start(bf16[192,384]{1,0:T(8,128)(2,1)S(1)} %reduce_sum.12), channel_id=1, source_target_pairs={{0,0},{1,32},{2,64},{3,96},{4,128},{5,160},{6,192},{7,224},{8,4},{... | collective-permute-start | bytes 442376 | tf_op jit(solution)/shard_map/ppermute | solution.py:421
  143.4 0.5 reduce-scatter.2.cloned.1.call-done
  143.9 9.3 %shard_map.126 = (bf16[1,1024,384]{2,1,0:T(8,128)(2,1)}, bf16[1,1024,384]{2,1,0:T(8,128)(2,1)}, bf16[1,1024,384]{2,1,0:T(8,128)(2,1)}, bf16[1,1024,768]{2,1,0:T(8,128)(2,1)}) custom-call(s32[6]{0:T(128)S(1)} %stack.57.info, s32[32]{0:T(128)S(1)} %copy-done.2, s32[1,1024]{1,0:T(1,128)} %order.5, bf16[512,384]{1,0:T(8,128)(2,1)} %bitcast.26, ...), custom_call_target="tpu_custom_call" | custom-call | bytes 11018240 | tf_op jit(solution)/shard_map/pallas_call | solution.py:21
  153.2 6.1 %collective-permute-done.27 = bf16[192,384]{1,0:T(8,128)(2,1)S(1)} collective-permute-done((bf16[192,384]{1,0:T(8,128)(2,1)S(1)}, bf16[192,384]{1,0:T(8,128)(2,1)S(1)}, u32[]{:S(2)}, u32[]{:S(2)}) %collective-permute-start.27) | collective-permute-done | bytes 147488 | tf_op jit(solution)/shard_map/ppermute | solution.py:421
  159.4 0.7 convert_bitcast_fusion
  (42 shorter events, 0.8 us)
Async XLA Ops:
  7.2 2.5 %copy-start.2 = (s32[32]{0:T(128)S(1)}, s32[32]{0:T(128)}, u32[]{:S(2)}) copy-start(s32[32]{0:T(128)} %counts.7) | copy-start | bytes 388
  7.2 63.0 %all-gather.2.cloned.1.call-start = ((), (), s32[]{:S(2)}) async-start(), calls=%async_computation.2 | async-start | bytes 3538944 | tf_op jit(solution)/shard_map/all_gather | solution.py:386
  8.8 46.5 %copy-start.4 = (bf16[6144]{0:T(1024)(128)(2,1)S(1)}, bf16[6144]{0:T(1024)(128)(2,1)}, u32[]{:S(2)}) copy-start(bf16[6144]{0:T(1024)(128)(2,1)} %param.12) | copy-start | bytes 36868
  8.8 46.5 %copy-start = (bf16[1,1024,768]{2,1,0:T(8,128)(2,1)S(1)}, bf16[1,1024,768]{2,1,0:T(8,128)(2,1)}, u32[]{:S(2)}) copy-start(bf16[1,1024,768]{2,1,0:T(8,128)(2,1)} %tokens.1) | copy-start | bytes 4718596
  8.9 46.5 %copy-start.1 = (s32[1,1024]{1,0:T(1,128)S(1)}, s32[1,1024]{1,0:T(1,128)}, u32[]{:S(2)}) copy-start(s32[1,1024]{1,0:T(1,128)} %order.5) | copy-start | bytes 12292
  8.9 8.2 %collective-permute-start = (bf16[2,96,384]{2,1,0:T(8,128)(2,1)S(1)}, bf16[2,96,384]{2,1,0:T(8,128)(2,1)S(1)}, u32[]{:S(2)}, u32[]{:S(2)}) collective-permute-start(bf16[2,96,384]{2,1,0:T(8,128)(2,1)S(1)} %shard_map.120), channel_id=1, source_target_pairs={{0,0},{1,1},{2,2},{3,3},{4,4},{5,5},{6,6},{7,7},{8,12},{9,13},{10,... | collective-permute-start | bytes 442376 | tf_op jit(solution)/shard_map/ppermute | solution.py:189
  17.2 126.7 %reduce-scatter.2.cloned.1.call-start = ((), (), s32[]{:S(2)}) async-start(), calls=%async_computation.3 | async-start | bytes 3538944 | tf_op jit(solution)/shard_map/reduce_scatter | solution.py:407
  17.2 16.4 %collective-permute-start.3 = (bf16[96,384]{1,0:T(8,128)(2,1)S(1)}, bf16[96,384]{1,0:T(8,128)(2,1)S(1)}, u32[]{:S(2)}, u32[]{:S(2)}) collective-permute-start(bf16[96,384]{1,0:T(8,128)(2,1)S(1)} %get-tuple-element.41), channel_id=1, source_target_pairs={{0,128},{8,136},{16,144},{24,152},{32,160},{40,168},{48,176},{56,1... | collective-permute-start | bytes 221192 | tf_op jit(solution)/shard_map/ppermute | solution.py:201
  28.0 6.2 %collective-permute-start.2 = (bf16[96,384]{1,0:T(8,128)(2,1)S(1)}, bf16[96,384]{1,0:T(8,128)(2,1)S(1)}, u32[]{:S(2)}, u32[]{:S(2)}) collective-permute-start(bf16[96,384]{1,0:T(8,128)(2,1)S(1)} %get-tuple-element.41), channel_id=1, source_target_pairs={{0,192},{8,200},{16,208},{24,216},{32,224},{40,232},{48,240},{56,2... | collective-permute-start | bytes 221192 | tf_op jit(solution)/shard_map/ppermute | solution.py:201
  28.6 5.6 %collective-permute-start.1 = (bf16[96,384]{1,0:T(8,128)(2,1)S(1)}, bf16[96,384]{1,0:T(8,128)(2,1)S(1)}, u32[]{:S(2)}, u32[]{:S(2)}) collective-permute-start(bf16[96,384]{1,0:T(8,128)(2,1)S(1)} %get-tuple-element.41), channel_id=1, source_target_pairs={{0,64},{8,72},{16,80},{24,88},{32,96},{40,104},{48,112},{56,120},{... | collective-permute-start | bytes 221192 | tf_op jit(solution)/shard_map/ppermute | solution.py:201
  30.0 5.9 %collective-permute-start.6 = (bf16[96,384]{1,0:T(8,128)(2,1)S(1)}, bf16[96,384]{1,0:T(8,128)(2,1)S(1)}, u32[]{:S(2)}, u32[]{:S(2)}) collective-permute-start(bf16[96,384]{1,0:T(8,128)(2,1)S(1)} %get-tuple-element.42), channel_id=1, source_target_pairs={{0,32},{8,40},{16,48},{24,56},{32,0},{40,8},{48,16},{56,24},{64,96... | collective-permute-start | bytes 221192 | tf_op jit(solution)/shard_map/ppermute | solution.py:201
  32.2 4.5 %collective-permute-start.5 = (bf16[96,384]{1,0:T(8,128)(2,1)S(1)}, bf16[96,384]{1,0:T(8,128)(2,1)S(1)}, u32[]{:S(2)}, u32[]{:S(2)}) collective-permute-start(bf16[96,384]{1,0:T(8,128)(2,1)S(1)} %get-tuple-element.42), channel_id=1, source_target_pairs={{0,48},{8,56},{16,0},{24,8},{32,16},{40,24},{48,32},{56,40},{64,11... | collective-permute-start | bytes 221192 | tf_op jit(solution)/shard_map/ppermute | solution.py:201
  33.6 4.4 %collective-permute-start.4 = (bf16[96,384]{1,0:T(8,128)(2,1)S(1)}, bf16[96,384]{1,0:T(8,128)(2,1)S(1)}, u32[]{:S(2)}, u32[]{:S(2)}) collective-permute-start(bf16[96,384]{1,0:T(8,128)(2,1)S(1)} %get-tuple-element.42), channel_id=1, source_target_pairs={{0,16},{8,24},{16,32},{24,40},{32,48},{40,56},{48,0},{56,8},{64,80... | collective-permute-start | bytes 221192 | tf_op jit(solution)/shard_map/ppermute | solution.py:201
  38.0 6.8 %collective-permute-start.18 = (bf16[4,96,384]{2,1,0:T(8,128)(2,1)S(1)}, bf16[4,96,384]{2,1,0:T(8,128)(2,1)S(1)}, u32[]{:S(2)}, u32[]{:S(2)}) collective-permute-start(bf16[4,96,384]{2,1,0:T(8,128)(2,1)S(1)} %pad_maximum_fusion.1.refs_8_), channel_id=1, source_target_pairs={{0,192},{8,200},{16,208},{24,216},{32,224},{40,232},{48,240},{56,2... | collective-permute-start | bytes 884744 | tf_op jit(solution)/shard_map/ppermute | solution.py:210
  39.9 14.3 %collective-permute-start.16 = (bf16[4,96,384]{2,1,0:T(8,128)(2,1)S(1)}, bf16[4,96,384]{2,1,0:T(8,128)(2,1)S(1)}, u32[]{:S(2)}, u32[]{:S(2)}) collective-permute-start(bf16[4,96,384]{2,1,0:T(8,128)(2,1)S(1)} %pad_maximum_fusion.1.refs_8_), channel_id=1, source_target_pairs={{0,64},{8,72},{16,80},{24,88},{32,96},{40,104},{48,112},{56,120},{... | collective-permute-start | bytes 884744 | tf_op jit(solution)/shard_map/ppermute | solution.py:210
  40.1 14.6 %collective-permute-start.15 = (bf16[4,96,384]{2,1,0:T(8,128)(2,1)S(1)}, bf16[4,96,384]{2,1,0:T(8,128)(2,1)S(1)}, u32[]{:S(2)}, u32[]{:S(2)}) collective-permute-start(bf16[4,96,384]{2,1,0:T(8,128)(2,1)S(1)} %pad_maximum_fusion.1.refs_8_), channel_id=1, source_target_pairs={{0,8},{8,0},{16,24},{24,16},{32,40},{40,32},{48,56},{56,48},{64,72... | collective-permute-start | bytes 884744 | tf_op jit(solution)/shard_map/ppermute | solution.py:213
  40.1 14.7 %collective-permute-start.7 = (bf16[4,96,384]{2,1,0:T(8,128)(2,1)S(1)}, bf16[4,96,384]{2,1,0:T(8,128)(2,1)S(1)}, u32[]{:S(2)}, u32[]{:S(2)}) collective-permute-start(bf16[4,96,384]{2,1,0:T(8,128)(2,1)S(1)} %pad_maximum_fusion.1.refs_8_), channel_id=1, source_target_pairs={{0,128},{8,136},{16,144},{24,152},{32,160},{40,168},{48,176},{56,1... | collective-permute-start | bytes 884744 | tf_op jit(solution)/shard_map/ppermute | solution.py:210
  41.5 16.3 %collective-permute-start.13 = (bf16[4,96,384]{2,1,0:T(8,128)(2,1)S(1)}, bf16[4,96,384]{2,1,0:T(8,128)(2,1)S(1)}, u32[]{:S(2)}, u32[]{:S(2)}) collective-permute-start(bf16[4,96,384]{2,1,0:T(8,128)(2,1)S(1)} %pad_maximum_fusion.refs_0_), channel_id=1, source_target_pairs={{0,32},{8,40},{16,48},{24,56},{32,0},{40,8},{48,16},{56,24},{64,96... | collective-permute-start | bytes 884744 | tf_op jit(solution)/shard_map/ppermute | solution.py:210
  44.8 13.6 %collective-permute-start.11 = (bf16[4,96,384]{2,1,0:T(8,128)(2,1)S(1)}, bf16[4,96,384]{2,1,0:T(8,128)(2,1)S(1)}, u32[]{:S(2)}, u32[]{:S(2)}) collective-permute-start(bf16[4,96,384]{2,1,0:T(8,128)(2,1)S(1)} %pad_maximum_fusion.refs_0_), channel_id=1, source_target_pairs={{0,48},{8,56},{16,0},{24,8},{32,16},{40,24},{48,32},{56,40},{64,11... | collective-permute-start | bytes 884744 | tf_op jit(solution)/shard_map/ppermute | solution.py:210
  54.2 7.1 %collective-permute-start.9 = (bf16[4,96,384]{2,1,0:T(8,128)(2,1)S(1)}, bf16[4,96,384]{2,1,0:T(8,128)(2,1)S(1)}, u32[]{:S(2)}, u32[]{:S(2)}) collective-permute-start(bf16[4,96,384]{2,1,0:T(8,128)(2,1)S(1)} %pad_maximum_fusion.refs_0_), channel_id=1, source_target_pairs={{0,16},{8,24},{16,32},{24,40},{32,48},{40,56},{48,0},{56,8},{64,80... | collective-permute-start | bytes 884744 | tf_op jit(solution)/shard_map/ppermute | solution.py:210
  54.8 6.5 %collective-permute-start.8 = (bf16[4,96,384]{2,1,0:T(8,128)(2,1)S(1)}, bf16[4,96,384]{2,1,0:T(8,128)(2,1)S(1)}, u32[]{:S(2)}, u32[]{:S(2)}) collective-permute-start(bf16[4,96,384]{2,1,0:T(8,128)(2,1)S(1)} %pad_maximum_fusion.refs_0_), channel_id=1, source_target_pairs={{0,8},{8,0},{16,24},{24,16},{32,40},{40,32},{48,56},{56,48},{64,72... | collective-permute-start | bytes 884744 | tf_op jit(solution)/shard_map/ppermute | solution.py:213
  54.8 7.0 %collective-permute-start.19 = (bf16[4,96,384]{2,1,0:T(8,128)(2,1)S(1)}, bf16[4,96,384]{2,1,0:T(8,128)(2,1)S(1)}, u32[]{:S(2)}, u32[]{:S(2)}) collective-permute-start(bf16[4,96,384]{2,1,0:T(8,128)(2,1)S(1)} %collective-permute-done.18.refs_12_), channel_id=1, source_target_pairs={{0,8},{8,0},{16,24},{24,16},{32,40},{40,32},{48,56},{56,48},{64,72... | collective-permute-start | bytes 884744 | tf_op jit(solution)/shard_map/ppermute | solution.py:213
  57.7 4.1 %collective-permute-start.17 = (bf16[4,96,384]{2,1,0:T(8,128)(2,1)S(1)}, bf16[4,96,384]{2,1,0:T(8,128)(2,1)S(1)}, u32[]{:S(2)}, u32[]{:S(2)}) collective-permute-start(bf16[4,96,384]{2,1,0:T(8,128)(2,1)S(1)} %collective-permute-done.16.refs_10_), channel_id=1, source_target_pairs={{0,8},{8,0},{16,24},{24,16},{32,40},{40,32},{48,56},{56,48},{64,72... | collective-permute-start | bytes 884744 | tf_op jit(solution)/shard_map/ppermute | solution.py:213
  58.4 3.4 %collective-permute-start.14 = (bf16[4,96,384]{2,1,0:T(8,128)(2,1)S(1)}, bf16[4,96,384]{2,1,0:T(8,128)(2,1)S(1)}, u32[]{:S(2)}, u32[]{:S(2)}) collective-permute-start(bf16[4,96,384]{2,1,0:T(8,128)(2,1)S(1)} %collective-permute-done.13.refs_6_), channel_id=1, source_target_pairs={{0,8},{8,0},{16,24},{24,16},{32,40},{40,32},{48,56},{56,48},{64,72... | collective-permute-start | bytes 884744 | tf_op jit(solution)/shard_map/ppermute | solution.py:213
  61.2 1.6 collective-permute-start.12
  61.2 2.0 %collective-permute-start.10 = (bf16[4,96,384]{2,1,0:T(8,128)(2,1)S(1)}, bf16[4,96,384]{2,1,0:T(8,128)(2,1)S(1)}, u32[]{:S(2)}, u32[]{:S(2)}) collective-permute-start(bf16[4,96,384]{2,1,0:T(8,128)(2,1)S(1)} %collective-permute-done.9.refs_2_), channel_id=1, source_target_pairs={{0,8},{8,0},{16,24},{24,16},{32,40},{40,32},{48,56},{56,48},{64,72... | collective-permute-start | bytes 884744 | tf_op jit(solution)/shard_map/ppermute | solution.py:213
  61.7 1.9 %collective-permute-start.20 = (bf16[4,96,384]{2,1,0:T(8,128)(2,1)S(1)}, bf16[4,96,384]{2,1,0:T(8,128)(2,1)S(1)}, u32[]{:S(2)}, u32[]{:S(2)}) collective-permute-start(bf16[4,96,384]{2,1,0:T(8,128)(2,1)S(1)} %collective-permute-done.7.refs_14_), channel_id=1, source_target_pairs={{0,8},{8,0},{16,24},{24,16},{32,40},{40,32},{48,56},{56,48},{64,72... | collective-permute-start | bytes 884744 | tf_op jit(solution)/shard_map/ppermute | solution.py:213
  70.2 18.7 %collective-permute-start.25 = (bf16[512,3072]{1,0:T(8,128)(2,1)}, bf16[512,3072]{1,0:T(8,128)(2,1)S(1)}, u32[]{:S(2)}, u32[]{:S(2)}) collective-permute-start(bf16[512,3072]{1,0:T(8,128)(2,1)} %all-gather.2.cloned.1.call-done.mixed.own_mixed), channel_id=1, source_target_pairs={{0,8},{8,0},{16,24},{24,16},{32,40},{40,32},{48,56},{56,48},{64,72... | collective-permute-start | bytes 9437192 | tf_op jit(solution)/shard_map/ppermute | solution.py:399
  76.5 4.7 %collective-permute-start.23 = (f32[8,512]{1,0:T(8,128)S(1)}, f32[8,512]{1,0:T(8,128)S(1)}, u32[]{:S(2)}, u32[]{:S(2)}) collective-permute-start(f32[8,512]{1,0:T(8,128)S(1)} %get-tuple-element.53), channel_id=1, source_target_pairs={{0,2},{1,3},{2,0},{3,1},{4,6},{5,7},{6,4},{7,5},{8,10},{9,11},{10,... | collective-permute-start | bytes 49160 | tf_op jit(solution)/shard_map/ppermute | solution.py:395
  78.3 5.5 %collective-permute-start.22 = (f32[8,512]{1,0:T(8,128)S(1)}, f32[8,512]{1,0:T(8,128)S(1)}, u32[]{:S(2)}, u32[]{:S(2)}) collective-permute-start(f32[8,512]{1,0:T(8,128)S(1)} %get-tuple-element.53), channel_id=1, source_target_pairs={{0,3},{1,2},{2,1},{3,0},{4,7},{5,6},{6,5},{7,4},{8,11},{9,10},{10,... | collective-permute-start | bytes 49160 | tf_op jit(solution)/shard_map/ppermute | solution.py:395
  79.8 4.1 %collective-permute-start.21 = (f32[8,512]{1,0:T(8,128)S(1)}, f32[8,512]{1,0:T(8,128)S(1)}, u32[]{:S(2)}, u32[]{:S(2)}) collective-permute-start(f32[8,512]{1,0:T(8,128)S(1)} %get-tuple-element.53), channel_id=1, source_target_pairs={{0,1},{1,0},{2,3},{3,2},{4,5},{5,4},{6,7},{7,6},{8,9},{9,8},{10,11... | collective-permute-start | bytes 49160 | tf_op jit(solution)/shard_map/ppermute | solution.py:395
  83.9 5.0 %collective-permute-start.24 = (f32[8,512]{1,0:T(8,128)S(1)}, f32[8,512]{1,0:T(8,128)S(1)}, u32[]{:S(2)}, u32[]{:S(2)}) collective-permute-start(f32[8,512]{1,0:T(8,128)S(1)} %add_add_fusion.refs_0_), channel_id=1, source_target_pairs={{0,7},{1,6},{2,5},{3,4},{4,3},{5,2},{6,1},{7,0},{8,15},{9,14},{10,... | collective-permute-start | bytes 49160 | tf_op jit(solution)/shard_map/ppermute | solution.py:395
  88.9 2.8 %copy-start.3 = (bf16[512,3072]{1,0:T(8,128)(2,1)}, bf16[512,3072]{1,0:T(8,128)(2,1)S(1)}, u32[]{:S(2)}) copy-start(bf16[512,3072]{1,0:T(8,128)(2,1)S(1)} %collective-permute-done.25.other_mixed) | copy-start | bytes 9437188
  91.7 6.3 %collective-permute-start.26 = (bf16[512,768]{1,0:T(8,128)(2,1)S(1)}, bf16[512,768]{1,0:T(8,128)(2,1)S(1)}, u32[]{:S(2)}, u32[]{:S(2)}) collective-permute-start(bf16[512,768]{1,0:T(8,128)(2,1)S(1)} %get-tuple-element.56.grad_proj.own_grad), channel_id=1, source_target_pairs={{0,8},{8,0},{16,24},{24,16},{32,40},{40,32},{48,56},{56,48},{64,72... | collective-permute-start | bytes 2359304 | tf_op jit(solution)/shard_map/ppermute | solution.py:405
  141.3 18.1 %collective-permute-start.27 = (bf16[192,384]{1,0:T(8,128)(2,1)S(1)}, bf16[192,384]{1,0:T(8,128)(2,1)S(1)}, u32[]{:S(2)}, u32[]{:S(2)}) collective-permute-start(bf16[192,384]{1,0:T(8,128)(2,1)S(1)} %reduce_sum.12), channel_id=1, source_target_pairs={{0,0},{1,32},{2,64},{3,96},{4,128},{5,160},{6,192},{7,224},{8,4},{... | collective-permute-start | bytes 442376 | tf_op jit(solution)/shard_map/ppermute | solution.py:421
Sparse Core Ops, SparseCore 0:
  17.3 52.8 all-gather.1
  98.1 45.7 reduce-scatter.1
